TPU v7x, 256 devices: a whole 4x4x8 slice. The times are simulated.
256 devices in a mesh: row: 8 (over y, core), col: 4 (over x), depth: 8 (over z).
Axes of the slice: x: 4, y: 4, z: 8, core: 2. Of those that a mesh axis runs over, the one named last changes fastest.
Arguments:
- tokens: bfloat16 [2048, 6144], P(('depth', 'row'), 'col'), may hold values from -6 to 6
- weight: bfloat16 [6144, 24576], P('col', 'row'), may hold values from -0.078125 to 0.078125
- bias_term: float32 [24576], P('row'), may hold values from -1 to 1
- cotangent: bfloat16 [2048, 24576], P(('depth', 'col'), 'row'), may hold values from -100 to 100
Outputs:
- input_grad: bfloat16 [2048, 6144], P(('depth', 'row'), 'col')
- activation: bfloat16 [2048, 24576], P(('depth', 'col'), 'row')
- weight_grad: float32 [6144, 24576], P('col', ('row', 'depth'))
- bias_grad: float32 [24576], P(('row', 'depth'))
- grad_norm: float32 [], replicated
All inputs are finite; a program needn't handle non-finite values.
Results may differ from a plain program's by a relative error of at most 0.01.
Values may be sent and summed in bfloat16 or wider, within the bound.
No kernel may reach another device: no remote copies, remote signals or barrier semaphores. Data moves between devices by JAX's collectives and lax.ppermute only.
A program may use at most 128 MiB of HBM per device.

v0:
```python
import math

import jax
import jax.numpy as jnp
from jax import lax
from jax.sharding import PartitionSpec as P

D = 6144
FF = 24576


gelu_scale = 0.7978845608
cubic_coef = 0.044715
norm_eps = 1e-06


def gelu_parts(preact):
    inside_term = gelu_scale * (preact + cubic_coef * preact * preact * preact)
    tanh_term = jnp.tanh(inside_term)
    activation = 0.5 * preact * (1.0 + tanh_term)
    slope_term = 0.5 * (1.0 + tanh_term) + 0.5 * preact * (
        1.0 - tanh_term * tanh_term
    ) * gelu_scale * (1.0 + 3.0 * cubic_coef * preact * preact)
    return (activation, slope_term)


def local(tokens, weight, bias_term, cotangent):
    tok_rows = tokens.shape[0]
    feat_cols = tokens.shape[1]
    n_row = lax.axis_size("row")
    n_depth = lax.axis_size("depth")
    depth_index = lax.axis_index("depth")
    col_index = lax.axis_index("col")
    everyone = lax.all_gather(tokens, ("row", "depth"), axis=0, tiled=True)
    blocked = everyone.reshape(n_row, n_depth, tok_rows, feat_cols)
    picked = lax.dynamic_index_in_dim(blocked, depth_index, axis=1, keepdims=False)
    slice_x = picked.reshape(n_row * tok_rows, feat_cols)
    row_block = slice_x
    preact = (
        lax.psum_scatter(
            jnp.dot(row_block, weight, preferred_element_type=jnp.float32),
            "col",
            scatter_dimension=0,
            tiled=True,
        )
        + bias_term
    )
    activation, slope_term = gelu_parts(preact)
    grad_share = (cotangent.astype(jnp.float32) * slope_term).astype(jnp.bfloat16)
    grad_slice = lax.all_gather(grad_share, "col", axis=0, tiled=True)
    hidden_out = activation.astype(jnp.bfloat16)
    row_block = grad_slice
    input_grad = lax.psum_scatter(
        lax.dot_general(
            row_block, weight, (((1,), (1,)), ((), ())), preferred_element_type=jnp.float32
        ),
        "row",
        scatter_dimension=0,
        tiled=True,
    ).astype(jnp.bfloat16)
    columns = lax.all_to_all(grad_slice, "depth", split_axis=1, concat_axis=0, tiled=True)
    col_width = columns.shape[1]
    ordered = (
        columns.reshape(n_depth, n_row, tok_rows, col_width)
        .transpose(1, 0, 2, 3)
        .reshape(n_row * n_depth * tok_rows, col_width)
    )
    weight_grad = lax.dot_general(
        everyone, ordered, (((0,), (0,)), ((), ())), preferred_element_type=jnp.float32
    )
    bias_grad = jnp.sum(ordered.astype(jnp.float32), axis=0)
    first_col = (col_index == 0).astype(jnp.float32)
    local_sq = jnp.sum(weight_grad * weight_grad) + first_col * jnp.sum(bias_grad * bias_grad)
    total_sq = lax.psum(local_sq, ("row", "col", "depth"))
    grad_norm = jnp.sqrt(total_sq + norm_eps)
    factor = jnp.minimum(1.0, math.sqrt(D * FF) / grad_norm)
    return (input_grad, hidden_out, weight_grad * factor, bias_grad * factor, grad_norm)


def solution(mesh):
    in_specs = (P(("depth", "row"), "col"), P("col", "row"), P("row"), P(("depth", "col"), "row"))
    out_specs = (
        P(("depth", "row"), "col"),
        P(("depth", "col"), "row"),
        P("col", ("row", "depth")),
        P(("row", "depth")),
        P(),
    )
    return jax.shard_map(local, mesh=mesh, in_specs=in_specs, out_specs=out_specs, check_vma=False)
```

profile of v0, /device:TPU:1, one launch (start us, length us, event | category | flops | bytes accessed | tf_op | source)
XLA Modules:
  0.0 322.6 jit_solution(9582385434959073002)
XLA Ops:
  7.2 0.0 all-gather.3.cloned.1.call-start
  7.2 0.7 all-gather.3.cloned.1.call-update
  7.9 0.0 reduce-scatter.3.cloned.1.call-start
  7.9 88.1 %all-gather.3.cloned.1.call-done = bf16[2048,1536]{1,0:T(8,128)(2,1)} async-done(((bf16[32,1536]{1,0:T(8,128)(2,1)}), bf16[2048,1536]{1,0:T(8,128)(2,1)}) %all-gather.3.cloned.1.call-update) | async-done | bytes 6291472 | tf_op jit(solution)/shard_map/all_gather | solution.py:34
  96.1 1.2 constant_dynamic-slice_fusion
  97.3 8.0 %fusion.7 = f32[256,3072]{1,0:T(8,128)} fusion(bf16[256,1536]{1,0:T(8,128)(2,1)S(1)} %bitcast.25, bf16[1536,3072]{1,0:T(8,128)(2,1)} %param.5), kind=kOutput, calls=%fused_computation.17 | convolution fusion | flops 2415919104 | bytes 13369344 | tf_op jit(solution)/shard_map/dot_general | solution.py:41
  105.3 0.0 all-gather.5.cloned.1.call-start
  105.3 37.1 %reduce-scatter.3.cloned.1.call-done = f32[64,3072]{1,0:T(8,128)} async-done(((f32[256,3072]{1,0:T(8,128)}), f32[64,3072]{1,0:T(8,128)}) %reduce-scatter.3.cloned.1.call-update) | async-done | bytes 786448 | tf_op jit(solution)/shard_map/reduce_scatter | solution.py:40
  142.4 2.6 multiply_convert_fusion
  145.0 28.9 %all-gather.5.cloned.1.call-done = bf16[256,3072]{1,0:T(8,128)(2,1)} async-done(((bf16[64,3072]{1,0:T(8,128)(2,1)}), bf16[256,3072]{1,0:T(8,128)(2,1)}) %all-gather.5.cloned.1.call-update) | async-done | bytes 1572880 | tf_op jit(solution)/shard_map/all_gather | solution.py:50
  174.0 2.7 copy.16
  176.7 6.9 %all-to-all-start = ((bf16[256,8,384]{2,0,1:T(8,128)(2,1)}), bf16[256,8,384]{2,0,1:T(8,128)(2,1)S(1)}, u32[]{:S(2)}, u32[]{:S(2)}) async-start(bf16[256,8,384]{2,0,1:T(8,128)(2,1)} %bitcast.19), calls=%async_computation.2 | async-start | bytes 3145728 | tf_op jit(solution)/shard_map/all_to_all | solution.py:61
  183.6 0.0 reduce-scatter.5.cloned.1.call-start
  183.6 7.5 %fusion.8 = f32[256,1536]{1,0:T(8,128)} fusion(bf16[256,3072]{1,0:T(8,128)(2,1)S(1)} %copy-done, bf16[1536,3072]{1,0:T(8,128)(2,1)} %param.5), kind=kOutput, calls=%fused_computation.18 | convolution fusion | flops 2415919104 | bytes 12582912 | tf_op jit(solution)/shard_map/dot_general | solution.py:54
  191.1 30.7 %all-to-all-done = bf16[256,8,384]{2,0,1:T(8,128)(2,1)S(1)} async-done(((bf16[256,8,384]{2,0,1:T(8,128)(2,1)}), bf16[256,8,384]{2,0,1:T(8,128)(2,1)S(1)}, u32[]{:S(2)}, u32[]{:S(2)}) %all-to-all-start) | async-done | bytes 1572896 | tf_op jit(solution)/shard_map/all_to_all | solution.py:61
  221.8 0.2 copy.12
  222.0 0.3 convert_reduce_fusion
  222.4 0.6 multiply_reduce_fusion.1
  223.6 7.7 %multiply_reduce_fusion = (f32[]{:T(128)}, f32[384,1536]{1,0:T(8,128)}) fusion(bf16[2048,384]{1,0:T(8,128)(2,1)S(1)} %bitcast.23, bf16[2048,1536]{1,0:T(8,128)(2,1)} %all-gather.3.cloned.1.call-done), kind=kOutput, calls=%fused_computation.2 | convolution fusion | flops 2417098752 | bytes 10223620 | tf_op jit(solution)/shard_map/dot_general | solution.py:68
  232.0 76.3 %psum.7 = f32[]{:T(128)} all-reduce(f32[]{:T(128)S(6)} %add.44), channel_id=1, replica_groups=mesh['row'=8,'col'=4,'depth'=8] {'row','col','depth'}, use_global_device_ids=true, to_apply=%region_5.6 | all-reduce | flops 1 | bytes 8 | tf_op jit(solution)/shard_map/psum | solution.py:74
  309.0 1.8 multiply_bitcast_fusion
  310.9 2.0 copy.13
  312.8 0.6 broadcast_multiply_fusion
  313.4 1.6 convert_element_type.19
  (10 shorter events, 0.1 us)
Async XLA Ops:
  7.2 88.9 %all-gather.3.cloned.1.call-start = ((), (), s32[]{:S(2)}) async-start(), calls=%async_computation.3 | async-start | bytes 6389760 | tf_op jit(solution)/shard_map/all_gather | solution.py:34
  7.9 134.5 %reduce-scatter.3.cloned.1.call-start = ((), (), s32[]{:S(2)}) async-start(), calls=%async_computation.4 | async-start | bytes 3932160 | tf_op jit(solution)/shard_map/reduce_scatter | solution.py:40
  105.3 37.1 %copy-start.1 = (bf16[64,3072]{1,0:T(8,128)(2,1)S(1)}, bf16[64,3072]{1,0:T(8,128)(2,1)}, u32[]{:S(2)}) copy-start(bf16[64,3072]{1,0:T(8,128)(2,1)} %param.7) | copy-start | bytes 1179652
  105.3 37.1 %copy-start.2 = (f32[3072]{0:T(1024)S(1)}, f32[3072]{0:T(1024)}, u32[]{:S(2)}) copy-start(f32[3072]{0:T(1024)} %param.6) | copy-start | bytes 36868
  105.3 68.7 %all-gather.5.cloned.1.call-start = ((), (), s32[]{:S(2)}) async-start(), calls=%async_computation.5 | async-start | bytes 1966080 | tf_op jit(solution)/shard_map/all_gather | solution.py:50
  176.7 6.9 %copy-start = (bf16[256,3072]{1,0:T(8,128)(2,1)S(1)}, bf16[256,3072]{1,0:T(8,128)(2,1)}, u32[]{:S(2)}) copy-start(bf16[256,3072]{1,0:T(8,128)(2,1)} %all-gather.5.cloned.1.call-done) | copy-start | bytes 4718596
  176.7 45.1 %all-to-all-start = ((bf16[256,8,384]{2,0,1:T(8,128)(2,1)}), bf16[256,8,384]{2,0,1:T(8,128)(2,1)S(1)}, u32[]{:S(2)}, u32[]{:S(2)}) async-start(bf16[256,8,384]{2,0,1:T(8,128)(2,1)} %bitcast.19), calls=%async_computation.2 | async-start | bytes 3145728 | tf_op jit(solution)/shard_map/all_to_all | solution.py:61
  183.6 129.8 %reduce-scatter.5.cloned.1.call-start = ((), (), s32[]{:S(2)}) async-start(), calls=%async_computation.6 | async-start | bytes 1769472 | tf_op jit(solution)/shard_map/reduce_scatter | solution.py:53
Sparse Core Ops, SparseCore 0:
  10.7 85.2 all-gather.2
  105.4 36.9 reduce-scatter.2
  145.2 28.7 all-gather.4
  191.2 33.8 reduce-scatter.4
where the time goes:
time: 323 us
  waiting for transfers between devices  186 us (58%)
  blocking collectives  76.3 us (24%)
  matrix products  23.1 us (7%)
  between operations  17 us (5%)
  other arithmetic  7.49 us (2%)
  starting transfers between devices  7.02 us (2%)
  local copies, waits for them, and re-layouts  6.09 us (2%)
    all_gather x1, waiting for transfers between devices, local(): everyone = lax.all_gather(tokens, ('row', 'depth'), axis=0, tiled=True)  88.1 us
    psum x1, blocking collectives, local(): total_sq = lax.psum(local_sq, ('row', 'col', 'depth'))  76.3 us
    reduce_scatter x1, waiting for transfers between devices, local(): lax.psum_scatter(jnp.dot(row_block, weight, preferred_element_type=jnp.fl...  37.1 us
    all_to_all x1, waiting for transfers between devices, local(): lax.all_to_all(grad_slice, 'depth', split_axis=1, concat_axis=0, tiled=True)  30.7 us
    all_gather x1, waiting for transfers between devices, local(): grad_slice = lax.all_gather(grad_share, 'col', axis=0, tiled=True)  28.9 us
    dot_general x1, matrix products, local(): jnp.dot(row_block, weight, preferred_element_type=jnp.float32)  7.97 us
    dot_general x1, matrix products, local(): lax.dot_general(everyone, ordered, (((0,), (0,)), ((), ())), preferred_el...  7.7 us
    dot_general x1, matrix products, local(): lax.dot_general(row_block, weight, (((1,), (1,)), ((), ())), preferred_el...  7.47 us
  transfers between devices with their start and end apart: 5, of which 4 were waited for; matrix products, arithmetic and copies ran while one was open for 6% of the time, Pallas kernels for 0%

commit v1 on v0

v1 whole, which is shorter than its diff:
```python
import math

import jax
import jax.numpy as jnp
from jax import lax
from jax.sharding import PartitionSpec as P

D = 6144
FF = 24576


gelu_scale = 0.7978845608
cubic_coef = 0.044715
norm_eps = 1e-06


def gelu_parts(preact):
    inside_term = gelu_scale * (preact + cubic_coef * preact * preact * preact)
    tanh_term = jnp.tanh(inside_term)
    activation = 0.5 * preact * (1.0 + tanh_term)
    slope_term = 0.5 * (1.0 + tanh_term) + 0.5 * preact * (
        1.0 - tanh_term * tanh_term
    ) * gelu_scale * (1.0 + 3.0 * cubic_coef * preact * preact)
    return (activation, slope_term)


def sum_axis(value, axis):
    n = lax.axis_size(axis)
    tiles = jnp.broadcast_to(value, (n, 8, 128))
    got = lax.all_to_all(tiles, axis, split_axis=0, concat_axis=0, tiled=True)
    return jnp.sum(got[:, 0, 0])


def local(tokens, weight, bias_term, cotangent):
    n_row = lax.axis_size("row")
    n_col = lax.axis_size("col")
    n_depth = lax.axis_size("depth")
    row_index = lax.axis_index("row")
    col_index = lax.axis_index("col")
    core = row_index % 2
    ff = weight.shape[1]
    feat = weight.shape[0]
    share = cotangent.shape[0]
    block_ff = ff // n_depth

    slice_x = lax.all_gather(tokens, "row", axis=0, tiled=True)
    half_rows = slice_x.shape[0] // 2
    half = lax.dynamic_slice_in_dim(slice_x, core * half_rows, half_rows, axis=0)
    mine = lax.all_gather(half, "depth", axis=0, tiled=True)
    swap = [(i, i ^ 1) for i in range(n_row)]
    other = lax.ppermute(mine, "row", swap)

    partial = jnp.dot(slice_x, weight, preferred_element_type=jnp.float32).astype(jnp.bfloat16)
    parts = lax.all_to_all(
        partial.reshape(n_col, share, ff), "col", split_axis=0, concat_axis=0, tiled=True
    )
    preact = jnp.sum(parts.astype(jnp.float32), axis=0) + bias_term
    activation, slope_term = gelu_parts(preact)
    grad_share = (cotangent.astype(jnp.float32) * slope_term).astype(jnp.bfloat16)
    hidden_out = activation.astype(jnp.bfloat16)

    columns = lax.all_to_all(
        grad_share.reshape(share, n_depth, block_ff).transpose(1, 0, 2),
        "depth",
        split_axis=0,
        concat_axis=0,
        tiled=True,
    )
    ordered = lax.all_gather(columns, "col", axis=0, tiled=False)
    grad_slice = lax.all_gather(grad_share, "col", axis=0, tiled=True)

    input_part = lax.dot_general(
        grad_slice, weight, (((1,), (1,)), ((), ())), preferred_element_type=jnp.float32
    )
    input_grad = lax.psum_scatter(input_part, "row", scatter_dimension=0, tiled=True).astype(
        jnp.bfloat16
    )

    pair = n_col // 2
    g_mine = lax.dynamic_slice_in_dim(ordered, core * pair, pair, axis=0)
    g_other = lax.dynamic_slice_in_dim(ordered, (1 - core) * pair, pair, axis=0)

    def meet(t, g):
        t = t.reshape(n_depth, pair, share, feat)
        t = t.transpose(1, 0, 2, 3).reshape(-1, feat)
        g = g.reshape(-1, block_ff)
        return lax.dot_general(t, g, (((0,), (0,)), ((), ())), preferred_element_type=jnp.float32)

    weight_grad = meet(mine, g_mine) + meet(other, g_other)
    bias_grad = jnp.sum(ordered.astype(jnp.float32), axis=(0, 1, 2))
    first_col = (col_index == 0).astype(jnp.float32)
    local_sq = jnp.sum(weight_grad * weight_grad) + first_col * jnp.sum(bias_grad * bias_grad)
    total_sq = sum_axis(sum_axis(sum_axis(local_sq, "row"), "col"), "depth")
    grad_norm = jnp.sqrt(total_sq + norm_eps)
    factor = jnp.minimum(1.0, math.sqrt(D * FF) / grad_norm)
    return (input_grad, hidden_out, weight_grad * factor, bias_grad * factor, grad_norm)


def solution(mesh):
    in_specs = (P(("depth", "row"), "col"), P("col", "row"), P("row"), P(("depth", "col"), "row"))
    out_specs = (
        P(("depth", "row"), "col"),
        P(("depth", "col"), "row"),
        P("col", ("row", "depth")),
        P(("row", "depth")),
        P(),
    )
    return jax.shard_map(local, mesh=mesh, in_specs=in_specs, out_specs=out_specs, check_vma=False)
```

time: 323 us -> 197 us (0.61)
  waiting for transfers between devices: 186 us -> 55.7 us
    psum x1 -> x0, blocking collectives: 76.3 us -> none  [local(): total_sq = lax.psum(local_sq, ('row', 'col', 'depth'))]
    all_gather x1 -> x2, waiting for transfers between devices: 88.1 us -> 23 us  [the longest x1 23 us: local(): ordered = lax.all_gather(columns, 'col', axis=0, tiled=False)]
    all_to_all x0 -> x4, blocking collectives: none -> 62.1 us  [the longest x1 23 us: local(): lax.all_to_all(partial.reshape(n_col, share, ff), 'col', split_axis=0, co...]
    reduce_scatter x2 -> x1, waiting for transfers between devices: 37.1 us -> 0.01 us  [local(): lax.psum_scatter(input_part, 'row', scatter_dimension=0, tiled=True)]
    all_to_all x1, waiting for transfers between devices: 30.7 us -> 5.3 us  [sum_axis(): got = lax.all_to_all(tiles, axis, split_axis=0, concat_axis=0, tiled=True)]
    all_gather x0 -> x1, blocking collectives: none -> 16.8 us  [local(): slice_x = lax.all_gather(tokens, 'row', axis=0, tiled=True)]
    reduce_sum x1 -> x5, other arithmetic: 0.31 us -> 3.79 us  [the longest x3 1.82 us: sum_axis(): return jnp.sum(got[:, 0, 0])]
    dot_general x3 -> x4, matrix products: 23.1 us -> 21.9 us  [the longest x1 7.94 us: local(): lax.dot_general(grad_slice, weight, (((1,), (1,)), ((), ())), preferred_e...]
  transfers between devices with their start and end apart: 5 -> 6, of which waited for: 4 -> 3; matrix products, arithmetic and copies ran while one was open for 6% -> 16% of each run, Pallas kernels for 0% -> 0%
where the time goes in v1:
time: 197 us; the launch traced here: 196 us
  blocking collectives  78.9 us (40%)
  waiting for transfers between devices  55.7 us (28%)
  matrix products  21.9 us (11%)
  between operations  17.1 us (9%)
  other arithmetic  9.57 us (5%)
  starting transfers between devices  8.64 us (4%)
  local copies, waits for them, and re-layouts  3.78 us (2%)
    all_gather x1, waiting for transfers between devices, local(): grad_slice = lax.all_gather(grad_share, 'col', axis=0, tiled=True)  27.3 us
    all_to_all x1, blocking collectives, local(): lax.all_to_all(partial.reshape(n_col, share, ff), 'col', split_axis=0, co...  23 us
    all_gather x1, waiting for transfers between devices, local(): ordered = lax.all_gather(columns, 'col', axis=0, tiled=False)  23 us
    all_to_all x1, blocking collectives, local(): lax.all_to_all(grad_share.reshape(share, n_depth, block_ff).transpose(1,...  22.7 us
    all_gather x1, blocking collectives, local(): slice_x = lax.all_gather(tokens, 'row', axis=0, tiled=True)  16.8 us
    all_to_all x2, blocking collectives, sum_axis(): got = lax.all_to_all(tiles, axis, split_axis=0, concat_axis=0, tiled=True)  16.4 us
    dot_general x1, matrix products, local(): lax.dot_general(grad_slice, weight, (((1,), (1,)), ((), ())), preferred_e...  7.94 us
    dot_general x2, matrix products, meet(): lax.dot_general(t, g, (((0,), (0,)), ((), ())), preferred_element_type=jn...  7.69 us
  transfers between devices with their start and end apart: 6, of which 3 were waited for; matrix products, arithmetic and copies ran while one was open for 16% of the time, Pallas kernels for 0%

profile of v1, /device:TPU:1, one launch (start us, length us, event | category | flops | bytes accessed | tf_op | source)
XLA Modules:
  0.0 195.7 jit_solution(15709594377288917892)
XLA Ops:
  7.2 16.8 %all_gather.15 = bf16[256,1536]{1,0:T(8,128)(2,1)S(1)} all-gather(bf16[32,1536]{1,0:T(8,128)(2,1)} %param.4), channel_id=1, replica_groups=mesh['row'=8,'col'=4,'depth'=8] {'row'}, dimensions={0}, use_global_device_ids=true | all-gather | bytes 884736 | tf_op jit(solution)/shard_map/all_gather | solution.py:46
  24.0 0.8 constant_dynamic-slice_fusion
  24.8 6.3 %convolution_convert_fusion = bf16[256,3072]{1,0:T(8,128)(2,1)S(1)} fusion(bf16[256,1536]{1,0:T(8,128)(2,1)S(1)} %all_gather.15, bf16[1536,3072]{1,0:T(8,128)(2,1)} %param.5), kind=kOutput, calls=%fused_computation | convolution fusion | flops 2416705536 | bytes 11796480 | tf_op jit(solution)/shard_map/dot_general | solution.py:53
  31.1 23.0 %all_to_all.25 = bf16[4,64,3072]{2,1,0:T(8,128)(2,1)S(1)} all-to-all(bf16[4,64,3072]{2,1,0:T(8,128)(2,1)S(1)} %bitcast.40), channel_id=1, replica_groups=mesh['row'=8,'col'=4,'depth'=8] {'col'}, dimensions={0} | all-to-all | bytes 3145728 | tf_op jit(solution)/shard_map/all_to_all | solution.py:54
  54.4 1.5 multiply_convert_fusion
  56.0 1.0 copy.35
  57.1 22.7 %all_to_all.26 = bf16[8,64,384]{2,1,0:T(8,128)(2,1)} all-to-all(bf16[8,64,384]{2,1,0:T(8,128)(2,1)S(1)} %copy.25), channel_id=1, replica_groups=mesh['row'=8,'col'=4,'depth'=8] {'depth'}, dimensions={0} | all-to-all | bytes 786432 | tf_op jit(solution)/shard_map/all_to_all | solution.py:62
  79.9 1.7 collective-permute-start
  81.7 27.3 %all-gather.5.cloned.1.call-done = bf16[256,3072]{1,0:T(8,128)(2,1)} async-done(((bf16[64,3072]{1,0:T(8,128)(2,1)}), bf16[256,3072]{1,0:T(8,128)(2,1)}) %all-gather.5.cloned.1.call-update) | async-done | bytes 1572880 | tf_op jit(solution)/shard_map/all_gather | solution.py:70
  109.0 7.9 %fusion.26 = f32[256,1536]{1,0:T(8,128)} fusion(bf16[256,3072]{1,0:T(8,128)(2,1)} %all-gather.5.cloned.1.call-done, bf16[1536,3072]{1,0:T(8,128)(2,1)} %param.5), kind=kOutput, calls=%fused_computation.34 | convolution fusion | flops 2415919104 | bytes 12582912 | tf_op jit(solution)/shard_map/dot_general | solution.py:72
  117.0 23.0 %all-gather.9.cloned.1.call-done = bf16[32,64,384]{2,1,0:T(8,128)(2,1)} async-done(((bf16[8,64,384]{2,1,0:T(8,128)(2,1)}), bf16[32,64,384]{2,1,0:T(8,128)(2,1)}) %all-gather.9.cloned.1.call-update) | async-done | bytes 1572880 | tf_op jit(solution)/shard_map/all_gather | solution.py:69
  140.0 1.7 convert_reduce_fusion
  143.0 3.1 %fusion.6 = f32[1536,384]{1,0:T(8,128)S(1)} fusion(bf16[8,2,64,1536]{3,2,1,0:T(8,128)(2,1)S(1)} %bitcast.42, bf16[4,8,64,384]{3,2,1,0:T(8,128)(2,1)} %bitcast.38, s32[]{:T(128)S(6)} %select_n.18), kind=kOutput, calls=%fused_computation.9 | convolution fusion | flops 1207959552 | bytes 6291460 | tf_op jit(solution)/shard_map/dot_general | solution.py:87
  146.1 4.6 %multiply_reduce_fusion = (f32[]{:T(128)}, f32[1536,384]{1,0:T(8,128)S(1)}) fusion(f32[1536,384]{1,0:T(8,128)S(1)} %fusion.6, bf16[4,8,64,384]{3,2,1,0:T(8,128)(2,1)S(1)} %bitcast.39, s32[]{:T(128)S(6)} %select_n.19, bf16[8,2,64,1536]{3,2,1,0:T(8,128)(2,1)} %bitcast.7), kind=kOutput, calls=%fused_computation.12 | convolution fusion | flops 1209729024 | bytes 8650760 | tf_op jit(solution)/shard_map/dot_general | solution.py:87
  151.4 9.6 %all_to_all.27 = f32[8,8,128]{2,1,0:T(8,128)S(1)} all-to-all(f32[8,8,128]{2,1,0:T(8,128)S(1)} %broadcast_in_dim.10), channel_id=1, replica_groups=mesh['row'=8,'col'=4,'depth'=8] {'row'}, dimensions={0} | all-to-all | bytes 65536 | tf_op jit(solution)/shard_map/all_to_all | solution.py:30
  161.0 0.6 slice_reduce_fusion.1
  161.6 0.6 broadcast_in_dim.11
  162.3 6.8 %all_to_all.28 = f32[4,8,128]{2,1,0:T(8,128)S(1)} all-to-all(f32[4,8,128]{2,1,0:T(8,128)S(1)} %broadcast_in_dim.11), channel_id=1, replica_groups=mesh['row'=8,'col'=4,'depth'=8] {'col'}, dimensions={0} | all-to-all | bytes 32768 | tf_op jit(solution)/shard_map/all_to_all | solution.py:30
  169.6 1.2 broadcast_in_dim.12
  170.9 6.7 %all-to-all-start.4 = ((f32[8,8,128]{2,1,0:T(8,128)}), f32[8,8,128]{2,1,0:T(8,128)S(1)}, u32[]{:S(2)}, u32[]{:S(2)}) async-start(f32[8,8,128]{2,1,0:T(8,128)} %broadcast_in_dim.12), calls=%async_computation.5 | async-start | bytes 65536 | tf_op jit(solution)/shard_map/all_to_all | solution.py:30
  177.6 1.6 convert_element_type.26
  179.2 5.3 %all-to-all-done.4 = f32[8,8,128]{2,1,0:T(8,128)S(1)} async-done(((f32[8,8,128]{2,1,0:T(8,128)}), f32[8,8,128]{2,1,0:T(8,128)S(1)}, u32[]{:S(2)}, u32[]{:S(2)}) %all-to-all-start.4) | async-done | bytes 32800 | tf_op jit(solution)/shard_map/all_to_all | solution.py:30
  184.5 0.6 slice_reduce_fusion
  186.4 1.6 broadcast_multiply_fusion
  (25 shorter events, 2.4 us)
Async XLA Ops:
  7.2 72.8 %all-gather.7.cloned.1.call-start = ((), (), s32[]{:S(2)}) async-start(), calls=%async_computation.8 | async-start | bytes 3538944 | tf_op jit(solution)/shard_map/all_gather | solution.py:49
  24.8 84.2 %all-gather.5.cloned.1.call-start = ((), (), s32[]{:S(2)}) async-start(), calls=%async_computation.6 | async-start | bytes 1966080 | tf_op jit(solution)/shard_map/all_gather | solution.py:70
  31.1 23.3 %copy-start.1 = (bf16[64,3072]{1,0:T(8,128)(2,1)S(1)}, bf16[64,3072]{1,0:T(8,128)(2,1)}, u32[]{:S(2)}) copy-start(bf16[64,3072]{1,0:T(8,128)(2,1)} %param.7) | copy-start | bytes 1179652
  31.1 23.3 %copy-start.2 = (f32[3072]{0:T(1024)S(1)}, f32[3072]{0:T(1024)}, u32[]{:S(2)}) copy-start(f32[3072]{0:T(1024)} %param.6) | copy-start | bytes 36868
  55.9 84.1 %all-gather.9.cloned.1.call-start = ((), (), s32[]{:S(2)}) async-start(), calls=%async_computation.9 | async-start | bytes 1966080 | tf_op jit(solution)/shard_map/all_gather | solution.py:69
  79.9 97.8 %reduce-scatter.2.cloned.1.call-start = ((), (), s32[]{:S(2)}) async-start(), calls=%async_computation.7 | async-start | bytes 1769472 | tf_op jit(solution)/shard_map/reduce_scatter | solution.py:75
  79.9 66.2 %collective-permute-start = (bf16[1024,1536]{1,0:T(8,128)(2,1)}, bf16[1024,1536]{1,0:T(8,128)(2,1)}, u32[]{:S(2)}, u32[]{:S(2)}) collective-permute-start(bf16[1024,1536]{1,0:T(8,128)(2,1)} %all-gather.7.cloned.1.call-done), channel_id=1, source_target_pairs={{0,32},{32,0},{64,96},{96,64},{128,160},{160,128},{192,224},{224,1... | collective-permute-start | bytes 9437192 | tf_op jit(solution)/shard_map/ppermute | solution.py:51
  116.9 26.0 %copy-start.3 = (bf16[1024,1536]{1,0:T(8,128)(2,1)S(1)}, bf16[1024,1536]{1,0:T(8,128)(2,1)}, u32[]{:S(2)}) copy-start(bf16[1024,1536]{1,0:T(8,128)(2,1)} %all-gather.7.cloned.1.call-done) | copy-start | bytes 9437188
  143.0 3.1 %copy-start = (bf16[32,64,384]{2,1,0:T(8,128)(2,1)S(1)}, bf16[32,64,384]{2,1,0:T(8,128)(2,1)}, u32[]{:S(2)}) copy-start(bf16[32,64,384]{2,1,0:T(8,128)(2,1)} %all-gather.9.cloned.1.call-done) | copy-start | bytes 4718596
  170.9 13.6 %all-to-all-start.4 = ((f32[8,8,128]{2,1,0:T(8,128)}), f32[8,8,128]{2,1,0:T(8,128)S(1)}, u32[]{:S(2)}, u32[]{:S(2)}) async-start(f32[8,8,128]{2,1,0:T(8,128)} %broadcast_in_dim.12), calls=%async_computation.5 | async-start | bytes 65536 | tf_op jit(solution)/shard_map/all_to_all | solution.py:30
Sparse Core Ops, SparseCore 0:
  24.9 45.6 all-gather.6
  73.0 35.9 all-gather.4
  110.8 29.1 all-gather.8
  143.0 33.0 reduce-scatter.1

commit v2 on v1

v2 whole, which is shorter than its diff:
```python
import math

import jax
import jax.numpy as jnp
from jax import lax
from jax.sharding import PartitionSpec as P

D = 6144
FF = 24576

BF = jnp.bfloat16
F32 = jnp.float32

gelu_scale = 0.7978845608
cubic_coef = 0.044715
norm_eps = 1e-06


def gelu_parts(preact):
    inside_term = gelu_scale * (preact + cubic_coef * preact * preact * preact)
    tanh_term = jnp.tanh(inside_term)
    activation = 0.5 * preact * (1.0 + tanh_term)
    slope_term = 0.5 * (1.0 + tanh_term) + 0.5 * preact * (
        1.0 - tanh_term * tanh_term
    ) * gelu_scale * (1.0 + 3.0 * cubic_coef * preact * preact)
    return (activation, slope_term)


def sum_axes(value, axes):
    n = lax.axis_size(axes)
    tiles = jnp.broadcast_to(value, (n, 1, 128))
    got = lax.all_to_all(tiles, axes, split_axis=0, concat_axis=0, tiled=True)
    return jnp.sum(got[:, 0, 0])


def shift_row(value, k):
    n = lax.axis_size("row")
    return lax.ppermute(value, "row", [(i, (i + 2 * k) % n) for i in range(n)])


def swap_core(value):
    n = lax.axis_size("row")
    return lax.ppermute(value, "row", [(i, i ^ 1) for i in range(n)])


def shift_col(value, k):
    n = lax.axis_size("col")
    return lax.ppermute(value, "col", [(i, (i + k) % n) for i in range(n)])


def add_bf(a, b):
    return (a.astype(F32) + b.astype(F32)).astype(BF)


def pick(stack, index):
    return lax.dynamic_index_in_dim(stack, index, 0, keepdims=False)


REL = (2, 1, 3, 0)


def local(tokens, weight, bias_term, cotangent):
    n_col = lax.axis_size("col")
    n_depth = lax.axis_size("depth")
    row_index = lax.axis_index("row")
    col = lax.axis_index("col")
    core = row_index % 2
    y = row_index // 2
    feat, ff = weight.shape
    share = cotangent.shape[0]
    block_ff = ff // n_depth
    tok = tokens.shape[0]
    half_feat = feat // 2
    half_ff = ff // 2

    got = [tokens] + [shift_row(tokens, k) for k in (1, 2, 3)]
    stack = jnp.stack(got)
    mine = jnp.stack([pick(stack, (y - col - k) % 4) for k in REL])
    other = swap_core(mine)
    first = jnp.where(core == 0, mine, other)
    second = jnp.where(core == 0, other, mine)
    slice_x = jnp.stack([first, second], axis=1).reshape(n_col * share, feat)

    half = lax.dynamic_slice_in_dim(slice_x, core * half_feat, half_feat, axis=1)
    all_mine = lax.all_gather(half, "depth", axis=0, tiled=False)
    all_other = swap_core(all_mine)

    p1 = jnp.dot(slice_x, weight[:, :half_ff], preferred_element_type=F32).astype(BF)
    p1 = p1.reshape(n_col, share, half_ff)
    s1 = shift_col(p1[0], 1)
    s2 = shift_col(p1[2], 3)
    p2 = jnp.dot(slice_x, weight[:, half_ff:], preferred_element_type=F32).astype(BF)
    p2 = p2.reshape(n_col, share, half_ff)
    s3 = shift_col(p2[0], 3)
    s4 = shift_col(p2[1], 1)
    s5 = shift_col(add_bf(s1, p1[1]), 1)
    s6 = shift_col(add_bf(s3, p2[2]), 3)
    o1 = p1[3].astype(F32) + s5.astype(F32) + s2.astype(F32)
    o2 = p2[3].astype(F32) + s6.astype(F32) + s4.astype(F32)
    preact = jnp.concatenate([o1, o2], axis=1) + bias_term
    activation, slope_term = gelu_parts(preact)
    grad_share = (cotangent.astype(F32) * slope_term).astype(BF)
    hidden_out = activation.astype(BF)

    columns = lax.all_to_all(
        grad_share.reshape(share, n_depth, block_ff).transpose(1, 0, 2),
        "depth",
        split_axis=0,
        concat_axis=0,
        tiled=True,
    )

    b1 = shift_col(grad_share, 1)
    b3 = shift_col(grad_share, 3)
    b2 = shift_col(grad_share, 2)
    grad_slice = jnp.concatenate([b2, b3, b1, grad_share], axis=0)
    input_part = lax.dot_general(
        grad_slice, weight, (((1,), (1,)), ((), ())), preferred_element_type=F32
    ).reshape(n_col, 2, tok, feat)
    keep = lax.dynamic_index_in_dim(input_part, core, 1, keepdims=False)
    send = lax.dynamic_index_in_dim(input_part, 1 - core, 1, keepdims=False).astype(BF)
    chip = keep + swap_core(send).astype(F32)

    def rel_pos(k):
        d = (y + k - col) % 4
        return jnp.where(d == 2, 0, jnp.where(d == 1, 1, jnp.where(d == 3, 2, 3)))

    input_grad = pick(chip, rel_pos(0))
    for k in (1, 3, 2):
        input_grad = input_grad + shift_row(pick(chip, rel_pos(k)).astype(BF), k).astype(F32)
    input_grad = input_grad.astype(BF)

    hz = n_depth // 2
    lo, hi = columns[:hz], columns[hz:]
    a1 = shift_col(lo, 1)
    d1 = shift_col(hi, 3)
    a2 = shift_col(hi, 1)
    d2 = shift_col(lo, 3)
    a3 = shift_col(a1, 1)
    d3 = shift_col(d1, 3)
    blocks = {
        0: columns,
        3: jnp.concatenate([a1, a2], axis=0),
        1: jnp.concatenate([d2, d1], axis=0),
        2: jnp.concatenate([a3, d3], axis=0),
    }

    def meet(t, k):
        i = REL.index(k)
        return lax.dot_general(
            t[:, i * share : (i + 1) * share],
            blocks[k],
            (((0, 1), (0, 1)), ((), ())),
            preferred_element_type=F32,
        )

    raw_mine = meet(all_mine, 0) + meet(all_mine, 3) + meet(all_mine, 1) + meet(all_mine, 2)
    raw_other = meet(all_other, 0) + meet(all_other, 3) + meet(all_other, 1) + meet(all_other, 2)
    raw_bias = sum(jnp.sum(g.astype(F32), axis=(0, 1)) for g in blocks.values())
    first_col = (col == 0).astype(F32)
    local_sq = (
        jnp.sum(raw_mine * raw_mine)
        + jnp.sum(raw_other * raw_other)
        + first_col * jnp.sum(raw_bias * raw_bias)
    )
    total_sq = sum_axes(sum_axes(local_sq, ("row", "col")), "depth")
    grad_norm = jnp.sqrt(total_sq + norm_eps)
    factor = jnp.minimum(1.0, math.sqrt(D * FF) / grad_norm)
    weight_grad = jnp.concatenate(
        [
            jnp.where(core == 0, raw_mine, raw_other) * factor,
            jnp.where(core == 0, raw_other, raw_mine) * factor,
        ],
        axis=0,
    )
    return (input_grad, hidden_out, weight_grad, raw_bias * factor, grad_norm)


def solution(mesh):
    in_specs = (P(("depth", "row"), "col"), P("col", "row"), P("row"), P(("depth", "col"), "row"))
    out_specs = (
        P(("depth", "row"), "col"),
        P(("depth", "col"), "row"),
        P("col", ("row", "depth")),
        P(("row", "depth")),
        P(),
    )
    return jax.shard_map(local, mesh=mesh, in_specs=in_specs, out_specs=out_specs, check_vma=False)
```

time: 197 us -> 153 us (0.78)
  blocking collectives: 78.9 us -> 0 us
  starting transfers between devices: 8.64 us -> 59 us
  waiting for transfers between devices: 55.7 us -> 36.9 us
    all_to_all x4 -> x0, blocking collectives: 62.1 us -> none  [the longest x1 23 us: local(): lax.all_to_all(partial.reshape(n_col, share, ff), 'col', split_axis=0, co...]
    all_gather x3 -> x1, waiting for transfers between devices: 50.4 us -> 0.83 us  [local(): all_mine = lax.all_gather(half, 'depth', axis=0, tiled=False)]
    ppermute x1 -> x24, starting transfers between devices: 1.74 us -> 36.1 us  [the longest x15 19.1 us: shift_col(): return lax.ppermute(value, 'col', [(i, (i + k) % n) for i in range(n)])]
    ppermute x1 -> x24, waiting for transfers between devices: 0.01 us -> 29.4 us  [the longest x15 21 us: shift_col(): return lax.ppermute(value, 'col', [(i, (i + k) % n) for i in range(n)])]
    all_gather x1 -> x0, blocking collectives: 16.8 us -> none  [local(): slice_x = lax.all_gather(tokens, 'row', axis=0, tiled=True)]
    all_to_all x1 -> x3, starting transfers between devices: 6.73 us -> 22.8 us  [the longest x2 14.5 us: sum_axes(): got = lax.all_to_all(tiles, axes, split_axis=0, concat_axis=0, tiled=True)]
    dot_general x3 -> x10, matrix products: 14 us -> 17.5 us  [the longest x8 12.1 us: meet(): lax.dot_general(t[:, i * share:(i + 1) * share], blocks[k], (((0, 1), (0,...]
    reduce_sum x6 -> x7, other arithmetic: 4.39 us -> 2.83 us  [the longest x2 1.24 us: sum_axes(): return jnp.sum(got[:, 0, 0])]
  transfers between devices with their start and end apart: 6 -> 28, of which waited for: 3 -> 16; matrix products, arithmetic and copies ran while one was open for 16% -> 16% of each run, Pallas kernels for 0% -> 0%
where the time goes in v2:
time: 153 us
  starting transfers between devices  59 us (39%)
  waiting for transfers between devices  36.9 us (24%)
  matrix products  23.8 us (16%)
  between operations  18.2 us (12%)
  other arithmetic  10.2 us (7%)
  local copies, waits for them, and re-layouts  4.7 us (3%)
    ppermute x15, waiting for transfers between devices, shift_col(): return lax.ppermute(value, 'col', [(i, (i + k) % n) for i in range(n)])  21 us
    ppermute x15, starting transfers between devices, shift_col(): return lax.ppermute(value, 'col', [(i, (i + k) % n) for i in range(n)])  19.1 us
    all_to_all x2, starting transfers between devices, sum_axes(): got = lax.all_to_all(tiles, axes, split_axis=0, concat_axis=0, tiled=True)  14.5 us
    dot_general x8, matrix products, meet(): lax.dot_general(t[:, i * share:(i + 1) * share], blocks[k], (((0, 1), (0,...  12.1 us
    ppermute x6, starting transfers between devices, shift_row(): return lax.ppermute(value, 'row', [(i, (i + 2 * k) % n) for i in range(n)])  9.04 us
    all_to_all x1, starting transfers between devices, local(): lax.all_to_all(grad_share.reshape(share, n_depth, block_ff).transpose(1,...  8.3 us
    ppermute x3, starting transfers between devices, swap_core(): return lax.ppermute(value, 'row', [(i, i ^ 1) for i in range(n)])  7.96 us
    ppermute x6, waiting for transfers between devices, shift_row(): return lax.ppermute(value, 'row', [(i, (i + 2 * k) % n) for i in range(n)])  6.98 us
  transfers between devices with their start and end apart: 28, of which 16 were waited for; matrix products, arithmetic and copies ran while one was open for 16% of the time, Pallas kernels for 0%

profile of v2, /device:TPU:1, one launch (start us, length us, event | category | flops | bytes accessed | tf_op | source)
XLA Modules:
  0.0 152.9 jit_solution(5148883278541811124)
XLA Ops:
  7.2 3.6 %collective-permute-start.2 = (bf16[32,1536]{1,0:T(8,128)(2,1)}, bf16[32,1536]{1,0:T(8,128)(2,1)S(1)}, u32[]{:S(2)}, u32[]{:S(2)}) collective-permute-start(bf16[32,1536]{1,0:T(8,128)(2,1)} %param.4), channel_id=1, source_target_pairs={{0,192},{32,224},{64,0},{96,32},{128,64},{160,96},{192,128},{224,1... | collective-permute-start | bytes 294920 | tf_op jit(solution)/shard_map/ppermute | solution.py:38
  13.4 2.8 %collective-permute-done.1 = bf16[32,1536]{1,0:T(8,128)(2,1)S(1)} collective-permute-done((bf16[32,1536]{1,0:T(8,128)(2,1)}, bf16[32,1536]{1,0:T(8,128)(2,1)S(1)}, u32[]{:S(2)}, u32[]{:S(2)}) %collective-permute-start.1) | collective-permute-done | bytes 98336 | tf_op jit(solution)/shard_map/ppermute | solution.py:38
  16.1 2.7 %collective-permute-done = bf16[32,1536]{1,0:T(8,128)(2,1)S(1)} collective-permute-done((bf16[32,1536]{1,0:T(8,128)(2,1)}, bf16[32,1536]{1,0:T(8,128)(2,1)S(1)}, u32[]{:S(2)}, u32[]{:S(2)}) %collective-permute-start) | collective-permute-done | bytes 98336 | tf_op jit(solution)/shard_map/ppermute | solution.py:38
  23.3 3.9 %fusion.7 = bf16[256,1536]{1,0:T(8,128)(2,1)S(1)} fusion(bf16[256,1536]{1,0:T(8,128)(2,1)S(1)} %bitcast.82, bf16[1536,3072]{1,0:T(8,128)(2,1)} %param.5), kind=kOutput, calls=%fused_computation.5 | convolution fusion | flops 1208352768 | bytes 6291456 | tf_op jit(solution)/shard_map/dot_general | solution.py:92
  34.4 2.8 %collective-permute-start.8 = (bf16[64,1536]{1,0:T(8,128)(2,1)S(1)}, bf16[64,1536]{1,0:T(8,128)(2,1)S(1)}, u32[]{:S(2)}, u32[]{:S(2)}) collective-permute-start(bf16[64,1536]{1,0:T(8,128)(2,1)S(1)} %add_convert_fusion), channel_id=1, source_target_pairs={{0,24},{8,0},{16,8},{24,16},{1,25},{9,1},{17,9},{25,17},{2,26},{10... | collective-permute-start | bytes 589832 | tf_op jit(solution)/shard_map/ppermute | solution.py:48
  37.1 2.1 %collective-permute-done.4 = bf16[64,1536]{1,0:T(8,128)(2,1)S(1)} collective-permute-done((bf16[64,1536]{1,0:T(8,128)(2,1)S(1)}, bf16[64,1536]{1,0:T(8,128)(2,1)S(1)}, u32[]{:S(2)}, u32[]{:S(2)}) %collective-permute-start.4) | collective-permute-done | bytes 196640 | tf_op jit(solution)/shard_map/ppermute | solution.py:48
  39.4 3.4 %collective-permute-done.8 = bf16[64,1536]{1,0:T(8,128)(2,1)S(1)} collective-permute-done((bf16[64,1536]{1,0:T(8,128)(2,1)S(1)}, bf16[64,1536]{1,0:T(8,128)(2,1)S(1)}, u32[]{:S(2)}, u32[]{:S(2)}) %collective-permute-start.8) | collective-permute-done | bytes 196640 | tf_op jit(solution)/shard_map/ppermute | solution.py:48
  42.9 2.6 %collective-permute-done.5 = bf16[64,1536]{1,0:T(8,128)(2,1)S(1)} collective-permute-done((bf16[64,1536]{1,0:T(8,128)(2,1)S(1)}, bf16[64,1536]{1,0:T(8,128)(2,1)S(1)}, u32[]{:S(2)}, u32[]{:S(2)}) %collective-permute-start.5) | collective-permute-done | bytes 196640 | tf_op jit(solution)/shard_map/ppermute | solution.py:48
  47.0 2.7 %collective-permute-start.11 = (bf16[64,3072]{1,0:T(8,128)(2,1)S(1)}, bf16[64,3072]{1,0:T(8,128)(2,1)S(1)}, u32[]{:S(2)}, u32[]{:S(2)}) collective-permute-start(bf16[64,3072]{1,0:T(8,128)(2,1)S(1)} %get-tuple-element.10), channel_id=1, source_target_pairs={{0,24},{8,0},{16,8},{24,16},{1,25},{9,1},{17,9},{25,17},{2,26},{10... | collective-permute-start | bytes 1179656 | tf_op jit(solution)/shard_map/ppermute | solution.py:48
  50.4 8.3 %all-to-all-start = ((bf16[8,64,384]{2,1,0:T(8,128)(2,1)}), bf16[8,64,384]{2,1,0:T(8,128)(2,1)S(1)}, u32[]{:S(2)}, u32[]{:S(2)}) async-start(bf16[8,64,384]{2,1,0:T(8,128)(2,1)} %bitcast.80), calls=%async_computation | async-start | bytes 786432 | tf_op jit(solution)/shard_map/all_to_all | solution.py:105
  58.7 3.6 %collective-permute-done.10 = bf16[64,3072]{1,0:T(8,128)(2,1)S(1)} collective-permute-done((bf16[64,3072]{1,0:T(8,128)(2,1)S(1)}, bf16[64,3072]{1,0:T(8,128)(2,1)S(1)}, u32[]{:S(2)}, u32[]{:S(2)}) %collective-permute-start.10) | collective-permute-done | bytes 393248 | tf_op jit(solution)/shard_map/ppermute | solution.py:48
  62.3 6.4 %fusion.10 = f32[256,1536]{1,0:T(8,128)S(1)} fusion(bf16[1536,3072]{1,0:T(8,128)(2,1)} %param.5, bf16[64,3072]{1,0:T(8,128)(2,1)S(1)} %get-tuple-element.10, bf16[64,3072]{1,0:T(8,128)(2,1)S(1)} %collective-permute-done.12, bf16[64,3072]{1,0:T(8,128)(2,1)S(1)} %collective-permute-done.11, bf16[64,3072]{1,0:T(8,128)(2,1)S(1)} %collective-permute-done.10), kind=kOutput, calls=%fused_computation.7 | convolution fusion | flops 2422210560 | bytes 12582912 | tf_op jit(solution)/shard_map/dot_general | solution.py:117
  68.7 5.9 %collective-permute-start.13 = (bf16[4,32,1536]{2,1,0:T(8,128)(2,1)S(1)}, bf16[4,32,1536]{2,1,0:T(8,128)(2,1)S(1)}, u32[]{:S(2)}, u32[]{:S(2)}) collective-permute-start(bf16[4,32,1536]{2,1,0:T(8,128)(2,1)S(1)} %fusion.39), channel_id=1, source_target_pairs={{0,32},{32,0},{64,96},{96,64},{128,160},{160,128},{192,224},{224,1... | collective-permute-start | bytes 1179656 | tf_op jit(solution)/shard_map/ppermute | solution.py:43
  76.5 3.2 %collective-permute-start.19 = (bf16[4,64,384]{2,1,0:T(8,128)(2,1)S(1)}, bf16[4,64,384]{2,1,0:T(8,128)(2,1)S(1)}, u32[]{:S(2)}, u32[]{:S(2)}) collective-permute-start(bf16[4,64,384]{2,1,0:T(8,128)(2,1)S(1)} %get-tuple-element.21), channel_id=1, source_target_pairs={{0,24},{8,0},{16,8},{24,16},{1,25},{9,1},{17,9},{25,17},{2,26},{10... | collective-permute-start | bytes 589832 | tf_op jit(solution)/shard_map/ppermute | solution.py:48
  79.7 2.7 %collective-permute-start.20 = (bf16[4,64,384]{2,1,0:T(8,128)(2,1)S(1)}, bf16[4,64,384]{2,1,0:T(8,128)(2,1)S(1)}, u32[]{:S(2)}, u32[]{:S(2)}) collective-permute-start(bf16[4,64,384]{2,1,0:T(8,128)(2,1)S(1)} %get-tuple-element.20), channel_id=1, source_target_pairs={{0,24},{8,0},{16,8},{24,16},{1,25},{9,1},{17,9},{25,17},{2,26},{10... | collective-permute-start | bytes 589832 | tf_op jit(solution)/shard_map/ppermute | solution.py:48
  82.6 2.8 %collective-permute-done.17 = bf16[4,64,384]{2,1,0:T(8,128)(2,1)S(1)} collective-permute-done((bf16[4,64,384]{2,1,0:T(8,128)(2,1)S(1)}, bf16[4,64,384]{2,1,0:T(8,128)(2,1)S(1)}, u32[]{:S(2)}, u32[]{:S(2)}) %collective-permute-start.17) | collective-permute-done | bytes 196640 | tf_op jit(solution)/shard_map/ppermute | solution.py:48
  87.1 3.4 %collective-permute-start.22 = (bf16[4,64,384]{2,1,0:T(8,128)(2,1)S(1)}, bf16[4,64,384]{2,1,0:T(8,128)(2,1)S(1)}, u32[]{:S(2)}, u32[]{:S(2)}) collective-permute-start(bf16[4,64,384]{2,1,0:T(8,128)(2,1)S(1)} %collective-permute-done.20), channel_id=1, source_target_pairs={{0,24},{8,0},{16,8},{24,16},{1,25},{9,1},{17,9},{25,17},{2,26},{10... | collective-permute-start | bytes 589832 | tf_op jit(solution)/shard_map/ppermute | solution.py:48
  90.8 3.6 %collective-permute-done.21 = bf16[4,64,384]{2,1,0:T(8,128)(2,1)S(1)} collective-permute-done((bf16[4,64,384]{2,1,0:T(8,128)(2,1)S(1)}, bf16[4,64,384]{2,1,0:T(8,128)(2,1)S(1)}, u32[]{:S(2)}, u32[]{:S(2)}) %collective-permute-start.21) | collective-permute-done | bytes 196640 | tf_op jit(solution)/shard_map/ppermute | solution.py:48
  96.5 1.9 %convolution_bitcast_fusion.5 = f32[768,384]{1,0:T(8,128)S(1)} fusion(bf16[8,64,384]{2,1,0:T(8,128)(2,1)S(1)} %constant_dynamic-update-slice_fusion.2, bf16[8,256,768]{2,1,0:T(8,128)(2,1)} %bitcast.92), kind=kOutput, calls=%fused_computation.20 | convolution fusion | flops 301989888 | bytes 2359296 | tf_op jit(solution)/shard_map/dot_general | solution.py:150
  106.4 2.5 %multiply_reduce_fusion = (f32[]{:T(128)}, f32[768,384]{1,0:T(8,128)S(1)}) fusion(f32[768,384]{1,0:T(8,128)S(1)} %fusion.22, bf16[8,64,384]{2,1,0:T(8,128)(2,1)S(1)} %copy-done.1, bf16[8,256,768]{2,1,0:T(8,128)(2,1)} %collective-permute-done.23), kind=kOutput, calls=%fused_computation.32 | convolution fusion | flops 302874624 | bytes 3538948 | tf_op jit(solution)/shard_map/dot_general | solution.py:150
  110.8 10.5 %all-to-all-start.1 = ((f32[32,1,128]{2,1,0:T(1,128)}), f32[32,1,128]{2,1,0:T(1,128)S(1)}, u32[]{:S(2)}, u32[]{:S(2)}) async-start(f32[32,1,128]{2,1,0:T(1,128)} %broadcast_in_dim.7), calls=%async_computation.1 | async-start | bytes 32768 | tf_op jit(solution)/shard_map/all_to_all | solution.py:32
  122.0 2.9 %collective-permute-start.16 = (bf16[32,1536]{1,0:T(8,128)(2,1)}, bf16[32,1536]{1,0:T(8,128)(2,1)S(1)}, u32[]{:S(2)}, u32[]{:S(2)}) collective-permute-start(bf16[32,1536]{1,0:T(8,128)(2,1)} %get-tuple-element.12), channel_id=1, source_target_pairs={{0,128},{32,160},{64,192},{96,224},{128,0},{160,32},{192,64},{224,... | collective-permute-start | bytes 294920 | tf_op jit(solution)/shard_map/ppermute | solution.py:38
  130.0 4.1 %all-to-all-start.2 = ((f32[8,1,128]{2,1,0:T(1,128)}), f32[8,1,128]{2,1,0:T(1,128)S(1)}, u32[]{:S(2)}, u32[]{:S(2)}) async-start(f32[8,1,128]{2,1,0:T(1,128)} %broadcast_in_dim.8), calls=%async_computation.2 | async-start | bytes 8192 | tf_op jit(solution)/shard_map/all_to_all | solution.py:32
  135.7 4.8 %all-to-all-done.2 = f32[8,1,128]{2,1,0:T(1,128)S(1)} async-done(((f32[8,1,128]{2,1,0:T(1,128)}), f32[8,1,128]{2,1,0:T(1,128)S(1)}, u32[]{:S(2)}, u32[]{:S(2)}) %all-to-all-start.2) | async-done | bytes 4128 | tf_op jit(solution)/shard_map/all_to_all | solution.py:32
  (93 shorter events, 41.8 us)
Async XLA Ops:
  7.2 68.3 %all-gather.3.cloned.1.call-start = ((), (), s32[]{:S(2)}) async-start(), calls=%async_computation.3 | async-start | bytes 3538944 | tf_op jit(solution)/shard_map/all_gather | solution.py:85
  7.2 6.2 %collective-permute-start.2 = (bf16[32,1536]{1,0:T(8,128)(2,1)}, bf16[32,1536]{1,0:T(8,128)(2,1)S(1)}, u32[]{:S(2)}, u32[]{:S(2)}) collective-permute-start(bf16[32,1536]{1,0:T(8,128)(2,1)} %param.4), channel_id=1, source_target_pairs={{0,192},{32,224},{64,0},{96,32},{128,64},{160,96},{192,128},{224,1... | collective-permute-start | bytes 294920 | tf_op jit(solution)/shard_map/ppermute | solution.py:38
  11.2 7.7 %collective-permute-start = (bf16[32,1536]{1,0:T(8,128)(2,1)}, bf16[32,1536]{1,0:T(8,128)(2,1)S(1)}, u32[]{:S(2)}, u32[]{:S(2)}) collective-permute-start(bf16[32,1536]{1,0:T(8,128)(2,1)} %param.4), channel_id=1, source_target_pairs={{0,64},{32,96},{64,128},{96,160},{128,192},{160,224},{192,0},{224,... | collective-permute-start | bytes 294920 | tf_op jit(solution)/shard_map/ppermute | solution.py:38
  27.3 12.2 %collective-permute-start.9 = (bf16[64,1536]{1,0:T(8,128)(2,1)S(1)}, bf16[64,1536]{1,0:T(8,128)(2,1)S(1)}, u32[]{:S(2)}, u32[]{:S(2)}) collective-permute-start(bf16[64,1536]{1,0:T(8,128)(2,1)S(1)} %get-tuple-element.17), channel_id=1, source_target_pairs={{0,8},{8,16},{16,24},{24,0},{1,9},{9,17},{17,25},{25,1},{2,10},{10... | collective-permute-start | bytes 589832 | tf_op jit(solution)/shard_map/ppermute | solution.py:48
  31.5 11.4 %collective-permute-start.6 = (bf16[64,1536]{1,0:T(8,128)(2,1)S(1)}, bf16[64,1536]{1,0:T(8,128)(2,1)S(1)}, u32[]{:S(2)}, u32[]{:S(2)}) collective-permute-start(bf16[64,1536]{1,0:T(8,128)(2,1)S(1)} %get-tuple-element.15), channel_id=1, source_target_pairs={{0,24},{8,0},{16,8},{24,16},{1,25},{9,1},{17,9},{25,17},{2,26},{10... | collective-permute-start | bytes 589832 | tf_op jit(solution)/shard_map/ppermute | solution.py:48
  32.9 6.4 %collective-permute-start.4 = (bf16[64,1536]{1,0:T(8,128)(2,1)S(1)}, bf16[64,1536]{1,0:T(8,128)(2,1)S(1)}, u32[]{:S(2)}, u32[]{:S(2)}) collective-permute-start(bf16[64,1536]{1,0:T(8,128)(2,1)S(1)} %get-tuple-element.14), channel_id=1, source_target_pairs={{0,8},{8,16},{16,24},{24,0},{1,9},{9,17},{17,25},{25,1},{2,10},{10... | collective-permute-start | bytes 589832 | tf_op jit(solution)/shard_map/ppermute | solution.py:48
  34.4 8.5 %collective-permute-start.8 = (bf16[64,1536]{1,0:T(8,128)(2,1)S(1)}, bf16[64,1536]{1,0:T(8,128)(2,1)S(1)}, u32[]{:S(2)}, u32[]{:S(2)}) collective-permute-start(bf16[64,1536]{1,0:T(8,128)(2,1)S(1)} %add_convert_fusion), channel_id=1, source_target_pairs={{0,24},{8,0},{16,8},{24,16},{1,25},{9,1},{17,9},{25,17},{2,26},{10... | collective-permute-start | bytes 589832 | tf_op jit(solution)/shard_map/ppermute | solution.py:48
  39.3 6.2 %collective-permute-start.5 = (bf16[64,1536]{1,0:T(8,128)(2,1)S(1)}, bf16[64,1536]{1,0:T(8,128)(2,1)S(1)}, u32[]{:S(2)}, u32[]{:S(2)}) collective-permute-start(bf16[64,1536]{1,0:T(8,128)(2,1)S(1)} %add_convert_fusion.1), channel_id=1, source_target_pairs={{0,8},{8,16},{16,24},{24,0},{1,9},{9,17},{17,25},{25,1},{2,10},{10... | collective-permute-start | bytes 589832 | tf_op jit(solution)/shard_map/ppermute | solution.py:48
  46.9 11.8 %collective-permute-start.12 = (bf16[64,3072]{1,0:T(8,128)(2,1)S(1)}, bf16[64,3072]{1,0:T(8,128)(2,1)S(1)}, u32[]{:S(2)}, u32[]{:S(2)}) collective-permute-start(bf16[64,3072]{1,0:T(8,128)(2,1)S(1)} %get-tuple-element.10), channel_id=1, source_target_pairs={{0,8},{8,16},{16,24},{24,0},{1,9},{9,17},{17,25},{25,1},{2,10},{10... | collective-permute-start | bytes 1179656 | tf_op jit(solution)/shard_map/ppermute | solution.py:48
  47.0 11.8 %collective-permute-start.11 = (bf16[64,3072]{1,0:T(8,128)(2,1)S(1)}, bf16[64,3072]{1,0:T(8,128)(2,1)S(1)}, u32[]{:S(2)}, u32[]{:S(2)}) collective-permute-start(bf16[64,3072]{1,0:T(8,128)(2,1)S(1)} %get-tuple-element.10), channel_id=1, source_target_pairs={{0,24},{8,0},{16,8},{24,16},{1,25},{9,1},{17,9},{25,17},{2,26},{10... | collective-permute-start | bytes 1179656 | tf_op jit(solution)/shard_map/ppermute | solution.py:48
  49.6 12.7 %collective-permute-start.10 = (bf16[64,3072]{1,0:T(8,128)(2,1)S(1)}, bf16[64,3072]{1,0:T(8,128)(2,1)S(1)}, u32[]{:S(2)}, u32[]{:S(2)}) collective-permute-start(bf16[64,3072]{1,0:T(8,128)(2,1)S(1)} %get-tuple-element.10), channel_id=1, source_target_pairs={{0,16},{8,24},{16,0},{24,8},{1,17},{9,25},{17,1},{25,9},{2,18},{10... | collective-permute-start | bytes 1179656 | tf_op jit(solution)/shard_map/ppermute | solution.py:48
  50.4 26.1 %all-to-all-start = ((bf16[8,64,384]{2,1,0:T(8,128)(2,1)}), bf16[8,64,384]{2,1,0:T(8,128)(2,1)S(1)}, u32[]{:S(2)}, u32[]{:S(2)}) async-start(bf16[8,64,384]{2,1,0:T(8,128)(2,1)} %bitcast.80), calls=%async_computation | async-start | bytes 786432 | tf_op jit(solution)/shard_map/all_to_all | solution.py:105
  68.7 13.7 %collective-permute-start.13 = (bf16[4,32,1536]{2,1,0:T(8,128)(2,1)S(1)}, bf16[4,32,1536]{2,1,0:T(8,128)(2,1)S(1)}, u32[]{:S(2)}, u32[]{:S(2)}) collective-permute-start(bf16[4,32,1536]{2,1,0:T(8,128)(2,1)S(1)} %fusion.39), channel_id=1, source_target_pairs={{0,32},{32,0},{64,96},{96,64},{128,160},{160,128},{192,224},{224,1... | collective-permute-start | bytes 1179656 | tf_op jit(solution)/shard_map/ppermute | solution.py:43
  75.4 25.7 %collective-permute-start.23 = (bf16[8,256,768]{2,1,0:T(8,128)(2,1)}, bf16[8,256,768]{2,1,0:T(8,128)(2,1)}, u32[]{:S(2)}, u32[]{:S(2)}) collective-permute-start(bf16[8,256,768]{2,1,0:T(8,128)(2,1)} %bitcast.91), channel_id=1, source_target_pairs={{0,32},{32,0},{64,96},{96,64},{128,160},{160,128},{192,224},{224,1... | collective-permute-start | bytes 9437192 | tf_op jit(solution)/shard_map/ppermute | solution.py:43
  76.5 14.0 %collective-permute-start.19 = (bf16[4,64,384]{2,1,0:T(8,128)(2,1)S(1)}, bf16[4,64,384]{2,1,0:T(8,128)(2,1)S(1)}, u32[]{:S(2)}, u32[]{:S(2)}) collective-permute-start(bf16[4,64,384]{2,1,0:T(8,128)(2,1)S(1)} %get-tuple-element.21), channel_id=1, source_target_pairs={{0,24},{8,0},{16,8},{24,16},{1,25},{9,1},{17,9},{25,17},{2,26},{10... | collective-permute-start | bytes 589832 | tf_op jit(solution)/shard_map/ppermute | solution.py:48
  79.7 7.4 %collective-permute-start.20 = (bf16[4,64,384]{2,1,0:T(8,128)(2,1)S(1)}, bf16[4,64,384]{2,1,0:T(8,128)(2,1)S(1)}, u32[]{:S(2)}, u32[]{:S(2)}) collective-permute-start(bf16[4,64,384]{2,1,0:T(8,128)(2,1)S(1)} %get-tuple-element.20), channel_id=1, source_target_pairs={{0,24},{8,0},{16,8},{24,16},{1,25},{9,1},{17,9},{25,17},{2,26},{10... | collective-permute-start | bytes 589832 | tf_op jit(solution)/shard_map/ppermute | solution.py:48
  82.5 8.2 %collective-permute-start.18 = (bf16[4,64,384]{2,1,0:T(8,128)(2,1)S(1)}, bf16[4,64,384]{2,1,0:T(8,128)(2,1)S(1)}, u32[]{:S(2)}, u32[]{:S(2)}) collective-permute-start(bf16[4,64,384]{2,1,0:T(8,128)(2,1)S(1)} %get-tuple-element.20), channel_id=1, source_target_pairs={{0,8},{8,16},{16,24},{24,0},{1,9},{9,17},{17,25},{25,1},{2,10},{10... | collective-permute-start | bytes 589832 | tf_op jit(solution)/shard_map/ppermute | solution.py:48
  85.4 9.0 %collective-permute-start.21 = (bf16[4,64,384]{2,1,0:T(8,128)(2,1)S(1)}, bf16[4,64,384]{2,1,0:T(8,128)(2,1)S(1)}, u32[]{:S(2)}, u32[]{:S(2)}) collective-permute-start(bf16[4,64,384]{2,1,0:T(8,128)(2,1)S(1)} %collective-permute-done.17), channel_id=1, source_target_pairs={{0,8},{8,16},{16,24},{24,0},{1,9},{9,17},{17,25},{25,1},{2,10},{10... | collective-permute-start | bytes 589832 | tf_op jit(solution)/shard_map/ppermute | solution.py:48
  87.1 7.4 %collective-permute-start.22 = (bf16[4,64,384]{2,1,0:T(8,128)(2,1)S(1)}, bf16[4,64,384]{2,1,0:T(8,128)(2,1)S(1)}, u32[]{:S(2)}, u32[]{:S(2)}) collective-permute-start(bf16[4,64,384]{2,1,0:T(8,128)(2,1)S(1)} %collective-permute-done.20), channel_id=1, source_target_pairs={{0,24},{8,0},{16,8},{24,16},{1,25},{9,1},{17,9},{25,17},{2,26},{10... | collective-permute-start | bytes 589832 | tf_op jit(solution)/shard_map/ppermute | solution.py:48
  110.8 17.3 %all-to-all-start.1 = ((f32[32,1,128]{2,1,0:T(1,128)}), f32[32,1,128]{2,1,0:T(1,128)S(1)}, u32[]{:S(2)}, u32[]{:S(2)}) async-start(f32[32,1,128]{2,1,0:T(1,128)} %broadcast_in_dim.7), calls=%async_computation.1 | async-start | bytes 32768 | tf_op jit(solution)/shard_map/all_to_all | solution.py:32
  122.0 12.1 %collective-permute-start.16 = (bf16[32,1536]{1,0:T(8,128)(2,1)}, bf16[32,1536]{1,0:T(8,128)(2,1)S(1)}, u32[]{:S(2)}, u32[]{:S(2)}) collective-permute-start(bf16[32,1536]{1,0:T(8,128)(2,1)} %get-tuple-element.12), channel_id=1, source_target_pairs={{0,128},{32,160},{64,192},{96,224},{128,0},{160,32},{192,64},{224,... | collective-permute-start | bytes 294920 | tf_op jit(solution)/shard_map/ppermute | solution.py:38
  124.9 9.2 %collective-permute-start.15 = (bf16[32,1536]{1,0:T(8,128)(2,1)S(1)}, bf16[32,1536]{1,0:T(8,128)(2,1)S(1)}, u32[]{:S(2)}, u32[]{:S(2)}) collective-permute-start(bf16[32,1536]{1,0:T(8,128)(2,1)S(1)} %get-tuple-element.13), channel_id=1, source_target_pairs={{0,192},{32,224},{64,0},{96,32},{128,64},{160,96},{192,128},{224,1... | collective-permute-start | bytes 294920 | tf_op jit(solution)/shard_map/ppermute | solution.py:38
  125.7 8.3 %collective-permute-start.14 = (bf16[32,1536]{1,0:T(8,128)(2,1)S(1)}, bf16[32,1536]{1,0:T(8,128)(2,1)}, u32[]{:S(2)}, u32[]{:S(2)}) collective-permute-start(bf16[32,1536]{1,0:T(8,128)(2,1)S(1)} %get-tuple-element.11), channel_id=1, source_target_pairs={{0,64},{32,96},{64,128},{96,160},{128,192},{160,224},{192,0},{224,... | collective-permute-start | bytes 294920 | tf_op jit(solution)/shard_map/ppermute | solution.py:38
  130.0 10.5 %all-to-all-start.2 = ((f32[8,1,128]{2,1,0:T(1,128)}), f32[8,1,128]{2,1,0:T(1,128)S(1)}, u32[]{:S(2)}, u32[]{:S(2)}) async-start(f32[8,1,128]{2,1,0:T(1,128)} %broadcast_in_dim.8), calls=%async_computation.2 | async-start | bytes 8192 | tf_op jit(solution)/shard_map/all_to_all | solution.py:32
  (10 other events, 60.6 us)
Sparse Core Ops, SparseCore 0:
  23.5 51.9 all-gather.2

commit v3 on v2

v3 whole, which is shorter than its diff:
```python
import math

import jax
import jax.numpy as jnp
from jax import lax
from jax.experimental import pallas as pl
from jax.experimental.pallas import tpu as pltpu
from jax.sharding import PartitionSpec as P

D = 6144
FF = 24576

BF = jnp.bfloat16
F32 = jnp.float32
LANES = 128

gelu_scale = 0.7978845608
cubic_coef = 0.044715
norm_eps = 1e-06


def gelu_parts(preact):
    inside_term = gelu_scale * (preact + cubic_coef * preact * preact * preact)
    tanh_term = jnp.tanh(inside_term)
    activation = 0.5 * preact * (1.0 + tanh_term)
    slope_term = 0.5 * (1.0 + tanh_term) + 0.5 * preact * (
        1.0 - tanh_term * tanh_term
    ) * gelu_scale * (1.0 + 3.0 * cubic_coef * preact * preact)
    return (activation, slope_term)


def shift_row(value, k):
    n = lax.axis_size("row")
    return lax.ppermute(value, "row", [(i, (i + 2 * k) % n) for i in range(n)])


def swap_core(value):
    n = lax.axis_size("row")
    return lax.ppermute(value, "row", [(i, i ^ 1) for i in range(n)])


def shift_col(value, k):
    n = lax.axis_size("col")
    return lax.ppermute(value, "col", [(i, (i + k) % n) for i in range(n)])


def shift_depth(value, k):
    n = lax.axis_size("depth")
    return lax.ppermute(value, "depth", [(i, (i + k) % n) for i in range(n)])


def after(value, *others):
    return lax.optimization_barrier((value, *others))[0]


def add_bf(a, b):
    return (a.astype(F32) + b.astype(F32)).astype(BF)


def pick(stack, index):
    return lax.dynamic_index_in_dim(stack, index, 0, keepdims=False)


def choose(options, index):
    res = options[-1]
    for i in range(len(options) - 1):
        res = jnp.where(index == i, options[i], res)
    return res


def stack_kernel(*refs):
    *srcs, dst, held, sems = refs
    n_share = held.shape[1]
    ins, outs, low = [], [], 0
    for i, src in enumerate(srcs):
        size = src.shape[0]
        slot = held.at[low // n_share, low % n_share : low % n_share + size]
        out = dst.at[low // n_share, low % n_share : low % n_share + size]
        ins.append(pltpu.make_async_copy(src, slot, sems.at[0, i]))
        outs.append(pltpu.make_async_copy(slot, out, sems.at[1, i]))
        low += size
    for c in ins:
        c.start()
    for c, d in zip(ins, outs):
        c.wait()
        d.start()
    for d in outs:
        d.wait()


def stack_up(pieces):
    one = pieces[0]
    shape = (sum(p.shape[0] for p in pieces) // one.shape[0],) + one.shape
    return pl.pallas_call(
        stack_kernel,
        in_specs=[pl.BlockSpec(memory_space=pl.ANY)] * len(pieces),
        out_specs=pl.BlockSpec(memory_space=pl.ANY),
        out_shape=jax.ShapeDtypeStruct(shape, one.dtype),
        scratch_shapes=[
            pltpu.VMEM(shape, one.dtype),
            pltpu.SemaphoreType.DMA((2, len(pieces))),
        ],
        compiler_params=pltpu.CompilerParams(vmem_limit_bytes=56 * 2**20),
        cost_estimate=pl.CostEstimate(
            flops=0, bytes_accessed=4 * math.prod(shape), transcendentals=0
        ),
        name="stack_up",
    )(*pieces)


REL = (2, 1, 3, 0)


def grad_step(t_mine, t_other, pieces, acc, depth, first_col=None):
    n_depth, n_share, rows, feat = t_mine.shape
    block_ff = pieces[0][1][0].shape[-1]
    width = 512
    kdim = n_depth * rows
    n_p = len(pieces)
    counts = [len(p[1]) for p in pieces]
    flat = [b for p in pieces for b in p[1]]
    final = first_col is not None
    have = acc is not None

    def body(*refs):
        refs = list(refs)
        depth_ref = refs.pop(0)
        first_ref = refs.pop(0) if final else None
        t_refs = [(refs.pop(0), refs.pop(0)) for _ in range(n_p)]
        g_refs = [refs.pop(0) for _ in flat]
        acc_ref, bias_in = (refs.pop(0), refs.pop(0)) if have else (None, None)
        out_ref, bias_out = refs.pop(0), refs.pop(0)
        sq_out = refs.pop(0) if final else None
        stage, gt = refs.pop(0), refs.pop(0)
        total = refs.pop(0) if final else None
        step = pl.program_id(0)

        @pl.when(step == 0)
        def _():
            me = depth_ref[0]
            bias = jnp.zeros((1, block_ff), F32)
            if have:
                bias = bias_in[...]
            at = 0
            for i in range(n_p):
                low = 0
                for _ in range(counts[i]):
                    g = g_refs[at]
                    at += 1
                    size = g.shape[0]
                    stage[low : low + size] = g[...]
                    low += size
                whole = stage[...].reshape(n_depth * 2 * rows, block_ff)
                bias = bias + jnp.sum(whole.astype(F32), axis=0, keepdims=True)
                for half in range(2):
                    parts = []
                    for d in range(n_depth):
                        z = lax.rem(me + n_depth - d, n_depth)
                        parts.append(stage[z, half * rows : (half + 1) * rows, :])
                    gt[2 * i + half] = jnp.concatenate(parts, axis=0).T
            bias_out[...] = bias

        res = acc_ref[...] if have else None
        for i in range(n_p):
            for half in range(2):
                t = t_refs[i][half][...].reshape(kdim, width)
                one = jnp.dot(gt[2 * i + half], t, preferred_element_type=F32)
                res = one if res is None else res + one
        out_ref[...] = res
        if final:
            here = jnp.sum(res * res, keepdims=True)

            @pl.when(step == 0)
            def _():
                b = bias_out[...]
                total[...] = here + first_ref[0] * jnp.sum(b * b, keepdims=True)

            @pl.when(step > 0)
            def _():
                total[...] += here

            sq_out[...] = jnp.broadcast_to(total[...].reshape(1, 1, 1), sq_out.shape)

    smem = pl.BlockSpec(memory_space=pltpu.SMEM)

    def whole_spec(shape):
        return pl.BlockSpec(shape, lambda j: (0,) * len(shape))

    def t_spec(pos):
        return pl.BlockSpec((n_depth, 1, rows, width), lambda j: (0, pos, 0, j))

    acc_spec = pl.BlockSpec((block_ff, width), lambda j: (0, j))
    bias_spec = whole_spec((1, block_ff))
    ins = [depth] + ([first_col] if final else [])
    specs = [smem] * len(ins)
    for pos, _ in pieces:
        ins += [t_mine, t_other]
        specs += [t_spec(pos)] * 2
    ins += flat
    specs += [whole_spec(b.shape) for b in flat]
    if have:
        ins += list(acc)
        specs += [acc_spec, bias_spec]
    out_shape = [
        jax.ShapeDtypeStruct((block_ff, feat), F32),
        jax.ShapeDtypeStruct((1, block_ff), F32),
    ]
    out_specs = [acc_spec, bias_spec]
    scratch = [
        pltpu.VMEM((n_depth, 2 * rows, block_ff), BF),
        pltpu.VMEM((2 * n_p, block_ff, kdim), BF),
    ]
    if final:
        n_sq = lax.axis_size(("row", "col"))
        out_shape.append(jax.ShapeDtypeStruct((n_sq, 1, LANES), F32))
        out_specs.append(whole_spec((n_sq, 1, LANES)))
        scratch.append(pltpu.VMEM((1, 1), F32))
    return pl.pallas_call(
        body,
        grid=(feat // width,),
        in_specs=specs,
        out_specs=out_specs,
        out_shape=out_shape,
        scratch_shapes=scratch,
        compiler_params=pltpu.CompilerParams(vmem_limit_bytes=12 * 2**20),
        cost_estimate=pl.CostEstimate(
            flops=n_p * 4 * kdim * block_ff * feat,
            bytes_accessed=n_p * 4 * kdim * feat + 8 * block_ff * feat,
            transcendentals=0,
        ),
        name="grad_step",
    )(*ins)


def clip(parts, raw, bias):
    block_ff, feat = raw.shape
    width = 256

    def body(p, r, b, o, ob, on):
        total = jnp.sum(p[...], axis=0)[:, :1]
        norm = jnp.sqrt(total + norm_eps)
        factor = jnp.minimum(1.0, math.sqrt(D * FF) / norm)
        o[...] = r[...].T * factor
        ob[...] = (b[...] * factor).reshape(block_ff)
        on[0] = norm[0, 0]

    def whole_spec(shape):
        return pl.BlockSpec(shape, lambda j: (0,) * len(shape))

    return pl.pallas_call(
        body,
        grid=(feat // width,),
        in_specs=[
            whole_spec(parts.shape),
            pl.BlockSpec((block_ff, width), lambda j: (0, j)),
            whole_spec((1, block_ff)),
        ],
        out_specs=[
            pl.BlockSpec((width, block_ff), lambda j: (j, 0)),
            whole_spec((block_ff,)),
            pl.BlockSpec(memory_space=pltpu.SMEM),
        ],
        out_shape=[
            jax.ShapeDtypeStruct((feat, block_ff), F32),
            jax.ShapeDtypeStruct((block_ff,), F32),
            jax.ShapeDtypeStruct((1,), F32),
        ],
        compiler_params=pltpu.CompilerParams(vmem_limit_bytes=4 * 2**20),
        name="clip",
    )(parts, raw, bias)


def exchange(value, axes):
    return lax.all_to_all(value, axes, split_axis=0, concat_axis=0, tiled=True)


def local(tokens, weight, bias_term, cotangent):
    n_col = lax.axis_size("col")
    n_depth = lax.axis_size("depth")
    row_index = lax.axis_index("row")
    col = lax.axis_index("col")
    depth = lax.axis_index("depth")
    core = row_index % 2
    y = row_index // 2
    feat, ff = weight.shape
    share = cotangent.shape[0]
    block_ff = ff // n_depth
    tok = tokens.shape[0]
    half_ff = ff // 2

    def own_first(v):
        return jnp.where(core == 0, v, jnp.concatenate([v[tok:], v[:tok]], axis=0))

    got = [tokens] + [shift_row(tokens, k) for k in (1, 2, 3)]
    mine = jnp.stack([choose(got, (y - col - k) % 4) for k in REL])
    other = swap_core(mine)
    slice_x = jnp.concatenate([mine, other], axis=1).reshape(n_col * share, feat)

    up1, dn1 = shift_depth(mine, 1), shift_depth(mine, n_depth - 1)
    up2, dn2 = shift_depth(up1, 1), shift_depth(dn1, n_depth - 1)
    up3, dn3 = shift_depth(up2, 1), shift_depth(dn2, n_depth - 1)
    up4 = shift_depth(up3[: n_col // 2], 1)
    dn4 = shift_depth(dn3[n_col // 2 :], n_depth - 1)

    p1 = jnp.dot(slice_x, weight[:, :half_ff], preferred_element_type=F32).astype(BF)
    p1 = p1.reshape(n_col, share, half_ff)
    p2 = jnp.dot(slice_x, weight[:, half_ff:], preferred_element_type=F32).astype(BF)
    p2 = p2.reshape(n_col, share, half_ff)
    s1 = shift_col(p1[0], 1)
    s3 = shift_col(p2[0], 3)
    s5 = shift_col(jnp.concatenate([add_bf(s1, p1[1]), p2[1]], axis=1), 1)
    s6 = shift_col(jnp.concatenate([p1[2], add_bf(s3, p2[2])], axis=1), 3)
    o1 = p1[3].astype(F32) + s5[:, :half_ff].astype(F32) + s6[:, :half_ff].astype(F32)
    o2 = p2[3].astype(F32) + s6[:, half_ff:].astype(F32) + s5[:, half_ff:].astype(F32)
    preact = jnp.concatenate([o1, o2], axis=1) + bias_term
    activation, slope_term = gelu_parts(preact)
    grad_share = (own_first(cotangent).astype(F32) * slope_term).astype(BF)
    hidden_out = own_first(activation.astype(BF))

    later = after(grad_share, up3, dn3)
    b1 = shift_col(later, 1)
    b3 = shift_col(later, 3)
    b2 = shift_col(b1[:tok], 1)
    b4 = shift_col(b3[tok:], 3)
    columns = exchange(after(grad_share, up2, dn2).reshape(share, n_depth, block_ff).transpose(1, 0, 2), "depth")

    columns, b1, b2, b3, b4 = lax.optimization_barrier((columns, b1, b2, b3, b4))
    t_mine = stack_up([after(mine, columns), up1, up2, up3, up4, dn4, dn3, dn2, dn1])
    t_other = swap_core(t_mine)

    hz = n_depth // 2
    a1 = shift_col(columns, 1)
    d1 = shift_col(columns, 3)
    depth_arr = depth.astype(jnp.int32).reshape(1)
    at = {k: REL.index(k) for k in REL}
    grad_slice = jnp.concatenate([b2, b4, b3, b1, grad_share], axis=0)
    input_part = lax.dot_general(
        grad_slice, weight, (((1,), (1,)), ((), ())), preferred_element_type=F32
    ).reshape(n_col, 2, tok, feat)
    a1, d1, input_part = lax.optimization_barrier((a1, d1, input_part))
    a3 = shift_col(a1[:hz], 1)
    d3 = shift_col(d1[hz:], 3)
    acc = grad_step(
        t_mine,
        t_other,
        [(at[0], [columns]), (at[3], [a1]), (at[1], [d1])],
        None,
        depth_arr,
    )
    chip = input_part[:, 0] + swap_core(input_part[:, 1].astype(BF)).astype(F32)

    def rel_pos(k):
        d = (y + k - col) % 4
        return jnp.where(d == 2, 0, jnp.where(d == 1, 1, jnp.where(d == 3, 2, 3)))

    came = [shift_row(pick(chip, rel_pos(k)).astype(BF), k) for k in (1, 3, 2)]
    a3, d3, acc, came = lax.optimization_barrier((a3, d3, acc, came))
    first_col = (col == 0).astype(F32).reshape(1)
    raw, raw_bias, squares = grad_step(
        t_mine, t_other, [(at[2], [a3, d3])], acc, depth_arr, first_col
    )

    input_grad = pick(chip, rel_pos(0))
    for part in came:
        input_grad = input_grad + part.astype(F32)
    input_grad = input_grad.astype(BF)

    squares = jnp.sum(exchange(squares, ("row", "col")), axis=0, keepdims=True)
    squares = jnp.broadcast_to(squares, (n_depth,) + squares.shape[1:])
    weight_grad, bias_grad, grad_norm = clip(exchange(squares, "depth"), raw, raw_bias)
    return (input_grad, hidden_out, weight_grad, bias_grad, grad_norm[0])


def solution(mesh):
    in_specs = (P(("depth", "row"), "col"), P("col", "row"), P("row"), P(("depth", "col"), "row"))
    out_specs = (
        P(("depth", "row"), "col"),
        P(("depth", "col"), "row"),
        P("col", ("row", "depth")),
        P(("row", "depth")),
        P(),
    )
    return jax.shard_map(local, mesh=mesh, in_specs=in_specs, out_specs=out_specs, check_vma=False)
```

time: 153 us -> 134 us (0.88)
  between operations: 18.2 us -> 1.04 us
  matrix products: 23.8 us -> 10.5 us
  Pallas kernels: 0 us -> 12.7 us
  starting transfers between devices: 59 us -> 65.5 us
  waiting for transfers between devices: 36.9 us -> 30.6 us
  other arithmetic: 10.2 us -> 6.38 us
  local copies, waits for them, and re-layouts: 4.7 us -> 7.15 us
    ppermute x0 -> x8, starting transfers between devices: none -> 12.9 us  [shift_depth(): return lax.ppermute(value, 'depth', [(i, (i + k) % n) for i in range(n)])]
    pallas_call x0 -> x4, Pallas kernels: none -> 12.7 us  [the longest x2 6.64 us: grad_step(): pl.pallas_call(body, grid=(feat // width,), in_specs=specs, out_specs=out...]
    dot_general x8 -> x0, matrix products: 12.1 us -> none  [meet(): lax.dot_general(t[:, i * share:(i + 1) * share], blocks[k], (((0, 1), (0,...]
    ppermute x15 -> x12, waiting for transfers between devices: 21 us -> 10.5 us  [shift_col(): return lax.ppermute(value, 'col', [(i, (i + k) % n) for i in range(n)])]
    all_to_all x3, starting transfers between devices: 22.8 us -> 16.7 us  [exchange(): return lax.all_to_all(value, axes, split_axis=0, concat_axis=0, tiled=True)]
    ppermute x0 -> x8, waiting for transfers between devices: none -> 4.86 us  [shift_depth(): return lax.ppermute(value, 'depth', [(i, (i + k) % n) for i in range(n)])]
    slice x2 -> x9, local copies, waits for them, and re-layouts: 0.07 us -> 3.62 us  [the longest x2 0.79 us: own_first(): return jnp.where(core == 0, v, jnp.concatenate([v[tok:], v[:tok]], axis=0))]
    all_to_all x3, waiting for transfers between devices: 6.7 us -> 9.99 us  [exchange(): return lax.all_to_all(value, axes, split_axis=0, concat_axis=0, tiled=True)]
  transfers between devices with their start and end apart: 28 -> 32, of which waited for: 16 -> 12; matrix products, arithmetic and copies ran while one was open for 16% -> 15% of each run, Pallas kernels for 0% -> 5%
where the time goes in v3:
time: 134 us
  starting transfers between devices  65.5 us (49%)
  waiting for transfers between devices  30.6 us (23%)
  Pallas kernels  12.7 us (9%)
  matrix products  10.5 us (8%)
  local copies, waits for them, and re-layouts  7.15 us (5%)
  other arithmetic  6.38 us (5%)
    ppermute x12, starting transfers between devices, shift_col(): return lax.ppermute(value, 'col', [(i, (i + k) % n) for i in range(n)])  17.2 us
    all_to_all x3, starting transfers between devices, exchange(): return lax.all_to_all(value, axes, split_axis=0, concat_axis=0, tiled=True)  16.7 us
    ppermute x8, starting transfers between devices, shift_depth(): return lax.ppermute(value, 'depth', [(i, (i + k) % n) for i in range(n)])  12.9 us
    ppermute x6, starting transfers between devices, shift_row(): return lax.ppermute(value, 'row', [(i, (i + 2 * k) % n) for i in range(n)])  10.9 us
    ppermute x12, waiting for transfers between devices, shift_col(): return lax.ppermute(value, 'col', [(i, (i + k) % n) for i in range(n)])  10.5 us
    all_to_all x3, waiting for transfers between devices, exchange(): return lax.all_to_all(value, axes, split_axis=0, concat_axis=0, tiled=True)  9.99 us
    ppermute x3, starting transfers between devices, swap_core(): return lax.ppermute(value, 'row', [(i, i ^ 1) for i in range(n)])  7.81 us
    pallas_call x2, Pallas kernels, grad_step(): pl.pallas_call(body, grid=(feat // width,), in_specs=specs, out_specs=out...  6.64 us
  transfers between devices with their start and end apart: 32, of which 12 were waited for; matrix products, arithmetic and copies ran while one was open for 15% of the time, Pallas kernels for 5%

profile of v3, /device:TPU:1, one launch (start us, length us, event | category | flops | bytes accessed | tf_op | source)
XLA Modules:
  0.0 133.8 jit_solution(6132573677887006237)
XLA Ops:
  0.6 3.8 %collective-permute-start = (bf16[32,1536]{1,0:T(8,128)(2,1)}, bf16[32,1536]{1,0:T(8,128)(2,1)S(1)}, u32[]{:S(2)}, u32[]{:S(2)}) collective-permute-start(bf16[32,1536]{1,0:T(8,128)(2,1)} %param.4), channel_id=1, source_target_pairs={{0,128},{32,160},{64,192},{96,224},{128,0},{160,32},{192,64},{224,... | collective-permute-start | bytes 294920 | tf_op jit(solution)/shard_map/ppermute | solution.py:34
  7.1 4.2 %collective-permute-done.1 = bf16[32,1536]{1,0:T(8,128)(2,1)S(1)} collective-permute-done((bf16[32,1536]{1,0:T(8,128)(2,1)}, bf16[32,1536]{1,0:T(8,128)(2,1)S(1)}, u32[]{:S(2)}, u32[]{:S(2)}) %collective-permute-start.1) | collective-permute-done | bytes 98336 | tf_op jit(solution)/shard_map/ppermute | solution.py:34
  14.2 3.9 %collective-permute-start.10 = (bf16[4,32,1536]{2,1,0:T(8,128)(2,1)S(1)}, bf16[4,32,1536]{2,1,0:T(8,128)(2,1)S(1)}, u32[]{:S(2)}, u32[]{:S(2)}) collective-permute-start(bf16[4,32,1536]{2,1,0:T(8,128)(2,1)S(1)} %pad_maximum_fusion.1.refs_0_), channel_id=1, source_target_pairs={{0,7},{1,0},{2,1},{3,2},{4,3},{5,4},{6,5},{7,6},{8,15},{9,8},{10,9... | collective-permute-start | bytes 1179656 | tf_op jit(solution)/shard_map/ppermute | solution.py:49
  18.2 3.9 %fusion.7 = bf16[256,1536]{1,0:T(8,128)(2,1)S(1)} fusion(bf16[256,1536]{1,0:T(8,128)(2,1)S(1)} %bitcast.47, bf16[1536,3072]{1,0:T(8,128)(2,1)} %param.5), kind=kOutput, calls=%fused_computation.5 | convolution fusion | flops 1208352768 | bytes 6291456 | tf_op jit(solution)/shard_map/dot_general | solution.py:307
  27.6 2.7 %collective-permute-start.11 = (bf16[4,32,1536]{2,1,0:T(8,128)(2,1)S(1)}, bf16[4,32,1536]{2,1,0:T(8,128)(2,1)}, u32[]{:S(2)}, u32[]{:S(2)}) collective-permute-start(bf16[4,32,1536]{2,1,0:T(8,128)(2,1)S(1)} %collective-permute-done.10.refs_8_), channel_id=1, source_target_pairs={{0,7},{1,0},{2,1},{3,2},{4,3},{5,4},{6,5},{7,6},{8,15},{9,8},{10,9... | collective-permute-start | bytes 1179656 | tf_op jit(solution)/shard_map/ppermute | solution.py:49
  31.1 3.5 %collective-permute-start.7 = (bf16[64,3072]{1,0:T(8,128)(2,1)S(1)}, bf16[64,3072]{1,0:T(8,128)(2,1)S(1)}, u32[]{:S(2)}, u32[]{:S(2)}) collective-permute-start(bf16[64,3072]{1,0:T(8,128)(2,1)S(1)} %pad_maximum_fusion.3), channel_id=1, source_target_pairs={{0,24},{8,0},{16,8},{24,16},{1,25},{9,1},{17,9},{25,17},{2,26},{10... | collective-permute-start | bytes 1179656 | tf_op jit(solution)/shard_map/ppermute | solution.py:44
  34.9 3.9 %collective-permute-done.9.refs_2_ = bf16[4,32,1536]{2,1,0:T(8,128)(2,1)} collective-permute-done((bf16[4,32,1536]{2,1,0:T(8,128)(2,1)S(1)}, bf16[4,32,1536]{2,1,0:T(8,128)(2,1)}, u32[]{:S(2)}, u32[]{:S(2)}) %collective-permute-start.9) | collective-permute-done | bytes 393248 | tf_op jit(solution)/shard_map/ppermute | solution.py:49
  38.8 2.7 %collective-permute-start.13 = (bf16[4,32,1536]{2,1,0:T(8,128)(2,1)}, bf16[4,32,1536]{2,1,0:T(8,128)(2,1)S(1)}, u32[]{:S(2)}, u32[]{:S(2)}) collective-permute-start(bf16[4,32,1536]{2,1,0:T(8,128)(2,1)} %collective-permute-done.11.refs_7_), channel_id=1, source_target_pairs={{0,7},{1,0},{2,1},{3,2},{4,3},{5,4},{6,5},{7,6},{8,15},{9,8},{10,9... | collective-permute-start | bytes 1179656 | tf_op jit(solution)/shard_map/ppermute | solution.py:49
  41.7 3.3 %collective-permute-done.5 = bf16[64,3072]{1,0:T(8,128)(2,1)S(1)} collective-permute-done((bf16[64,3072]{1,0:T(8,128)(2,1)S(1)}, bf16[64,3072]{1,0:T(8,128)(2,1)S(1)}, u32[]{:S(2)}, u32[]{:S(2)}) %collective-permute-start.5) | collective-permute-done | bytes 393248 | tf_op jit(solution)/shard_map/ppermute | solution.py:44
  46.6 4.9 %all-to-all-start = ((bf16[8,64,384]{2,1,0:T(8,128)(2,1)}), bf16[8,64,384]{2,1,0:T(8,128)(2,1)S(1)}, u32[]{:S(2)}, u32[]{:S(2)}) async-start(bf16[8,64,384]{2,1,0:T(8,128)(2,1)} %bitcast.43), calls=%async_computation | async-start | bytes 786432 | tf_op jit(solution)/shard_map/all_to_all | solution.py:274
  51.7 2.7 %collective-permute-start.16 = (bf16[64,3072]{1,0:T(8,128)(2,1)S(1)}, bf16[64,3072]{1,0:T(8,128)(2,1)S(1)}, u32[]{:S(2)}, u32[]{:S(2)}) collective-permute-start(bf16[64,3072]{1,0:T(8,128)(2,1)S(1)} %get-tuple-element.32), channel_id=1, source_target_pairs={{0,24},{8,0},{16,8},{24,16},{1,25},{9,1},{17,9},{25,17},{2,26},{10... | collective-permute-start | bytes 1179656 | tf_op jit(solution)/shard_map/ppermute | solution.py:44
  54.3 6.2 %collective-permute-done.14 = bf16[64,3072]{1,0:T(8,128)(2,1)S(1)} collective-permute-done((bf16[64,3072]{1,0:T(8,128)(2,1)S(1)}, bf16[64,3072]{1,0:T(8,128)(2,1)S(1)}, u32[]{:S(2)}, u32[]{:S(2)}) %collective-permute-start.14) | collective-permute-done | bytes 393248 | tf_op jit(solution)/shard_map/ppermute | solution.py:44
  61.9 2.7 %collective-permute-start.17 = (bf16[32,3072]{1,0:T(8,128)(2,1)}, bf16[32,3072]{1,0:T(8,128)(2,1)S(1)}, u32[]{:S(2)}, u32[]{:S(2)}) collective-permute-start(bf16[32,3072]{1,0:T(8,128)(2,1)} %slice.126), channel_id=1, source_target_pairs={{0,24},{8,0},{16,8},{24,16},{1,25},{9,1},{17,9},{25,17},{2,26},{10... | collective-permute-start | bytes 589832 | tf_op jit(solution)/shard_map/ppermute | solution.py:44
  68.7 2.7 %collective-permute-start.19 = (bf16[8,64,384]{2,1,0:T(8,128)(2,1)S(1)}, bf16[8,64,384]{2,1,0:T(8,128)(2,1)S(1)}, u32[]{:S(2)}, u32[]{:S(2)}) collective-permute-start(bf16[8,64,384]{2,1,0:T(8,128)(2,1)S(1)} %all-to-all-done.refs_7_), channel_id=1, source_target_pairs={{0,24},{8,0},{16,8},{24,16},{1,25},{9,1},{17,9},{25,17},{2,26},{10... | collective-permute-start | bytes 1179656 | tf_op jit(solution)/shard_map/ppermute | solution.py:44
  72.8 2.8 %stack_up.1.refs_1_.refs_3_.refs_5_.refs_2_ = bf16[8,4,32,1536]{3,2,1,0:T(8,128)(2,1)} custom-call(bf16[4,32,1536]{2,1,0:T(8,128)(2,1)} %copy-done.1, bf16[4,32,1536]{2,1,0:T(8,128)(2,1)} %copy-done.5, bf16[4,32,1536]{2,1,0:T(8,128)(2,1)} %collective-permute-done.9.refs_2_, bf16[4,32,1536]{2,1,0:T(8,128)(2,1)} %copy-done.3, bf16[2,32,1536]{2,1,0:T(8,128)(2,1)} %copy-done.7, ...), custom_call_target="tpu_custom_call" | custom-call | bytes 6291456 | tf_op jit(solution)/shard_map/stack_up/pallas_call | solution.py:94
  75.6 6.8 %collective-permute-start.25 = (bf16[8,4,32,1536]{3,2,1,0:T(8,128)(2,1)}, bf16[8,4,32,1536]{3,2,1,0:T(8,128)(2,1)S(1)}, u32[]{:S(2)}, u32[]{:S(2)}) collective-permute-start(bf16[8,4,32,1536]{3,2,1,0:T(8,128)(2,1)} %stack_up.1.refs_1_.refs_3_.refs_5_.refs_2_), channel_id=1, source_target_pairs={{0,32},{32,0},{64,96},{96,64},{128,160},{160,128},{192,224},{224,1... | collective-permute-start | bytes 9437192 | tf_op jit(solution)/shard_map/ppermute | solution.py:39
  82.5 5.2 %fusion.29 = f32[256,1536]{1,0:T(8,128)S(1)} fusion(bf16[256,3072]{1,0:T(8,128)(2,1)S(1)} %constant_dynamic-update-slice_fusion, bf16[1536,3072]{1,0:T(8,128)(2,1)} %param.5), kind=kOutput, calls=%fused_computation.55 | convolution fusion | flops 2415919104 | bytes 12582912 | tf_op jit(solution)/shard_map/dot_general | solution.py:337
  96.2 3.5 %grad_step.2 = (f32[384,1536]{1,0:T(8,128)S(1)}, f32[1,384]{1,0:T(1,128)S(1)}) custom-call(s32[1]{0:T(128)} %bitcast.10.refs_0_, bf16[8,4,32,1536]{3,2,1,0:T(8,128)(2,1)S(1)} %copy-done, bf16[8,4,32,1536]{3,2,1,0:T(8,128)(2,1)S(1)} %collective-permute-done.25.refs_2_.refs_4_.refs_6_.refs_3_, bf16[8,4,32,1536]{3,2,1,0:T(8,128)(2,1)S(1)} %copy-done, ...), custom_call_target="tpu_custom_call" | custom-call | flops 1811939328 | bytes 9437184 | tf_op jit(solution)/shard_map/grad_step/pallas_call | solution.py:218
  100.7 3.2 %grad_step.3 = (f32[384,1536]{1,0:T(8,128)S(1)}, f32[1,384]{1,0:T(1,128)S(1)}, f32[32,1,128]{2,1,0:T(1,128)}) custom-call(s32[1]{0:T(128)} %bitcast.10.refs_0_, f32[1]{0:T(128)} %bitcast.14.refs_1_, bf16[8,4,32,1536]{3,2,1,0:T(8,128)(2,1)S(1)} %copy-done, bf16[8,4,32,1536]{3,2,1,0:T(8,128)(2,1)S(1)} %collective-permute-done.25.refs_2_.refs_4_.refs_6_.refs_3_, ...), custom_call_target="tpu_custom_call" | custom-call | flops 603979776 | bytes 6291456 | tf_op jit(solution)/shard_map/grad_step/pallas_call | solution.py:218
  103.9 5.9 %all-to-all-start.1 = ((f32[32,1,128]{2,1,0:T(1,128)}), f32[32,1,128]{2,1,0:T(1,128)}, u32[]{:S(2)}, u32[]{:S(2)}) async-start(f32[32,1,128]{2,1,0:T(1,128)} %get-tuple-element.51), calls=%async_computation.1 | async-start | bytes 32768 | tf_op jit(solution)/shard_map/all_to_all | solution.py:274
  111.7 5.2 %all-to-all-done.1 = f32[32,1,128]{2,1,0:T(1,128)} async-done(((f32[32,1,128]{2,1,0:T(1,128)}), f32[32,1,128]{2,1,0:T(1,128)}, u32[]{:S(2)}, u32[]{:S(2)}) %all-to-all-start.1) | async-done | bytes 16416 | tf_op jit(solution)/shard_map/all_to_all | solution.py:274
  118.3 5.8 %all-to-all-start.2 = ((f32[8,1,128]{2,1,0:T(1,128)}), f32[8,1,128]{2,1,0:T(1,128)S(1)}, u32[]{:S(2)}, u32[]{:S(2)}) async-start(f32[8,1,128]{2,1,0:T(1,128)} %broadcast_in_dim.2), calls=%async_computation.2 | async-start | bytes 8192 | tf_op jit(solution)/shard_map/all_to_all | solution.py:274
  125.8 4.8 %all-to-all-done.2.p = f32[8,1,128]{2,1,0:T(1,128)S(1)} async-done(((f32[8,1,128]{2,1,0:T(1,128)}), f32[8,1,128]{2,1,0:T(1,128)S(1)}, u32[]{:S(2)}, u32[]{:S(2)}) %all-to-all-start.2) | async-done | bytes 4128 | tf_op jit(solution)/shard_map/all_to_all | solution.py:274
  130.6 3.3 %clip.1 = (f32[1536,384]{1,0:T(8,128)}, f32[384]{0:T(512)}, f32[1]{0:T(128)}) custom-call(f32[8,1,128]{2,1,0:T(1,128)S(1)} %all-to-all-done.2.p, f32[384,1536]{1,0:T(8,128)S(1)} %get-tuple-element.52.r, f32[1,384]{1,0:T(1,128)S(1)} %get-tuple-element.53.b), custom_call_target="tpu_custom_call" | custom-call | tf_op jit(solution)/shard_map/clip/pallas_call | solution.py:250
  (107 shorter events, 35.4 us)
Async XLA Ops:
  4.5 6.9 %collective-permute-start.1 = (bf16[32,1536]{1,0:T(8,128)(2,1)}, bf16[32,1536]{1,0:T(8,128)(2,1)S(1)}, u32[]{:S(2)}, u32[]{:S(2)}) collective-permute-start(bf16[32,1536]{1,0:T(8,128)(2,1)} %param.4), channel_id=1, source_target_pairs={{0,64},{32,96},{64,128},{96,160},{128,192},{160,224},{192,0},{224,... | collective-permute-start | bytes 294920 | tf_op jit(solution)/shard_map/ppermute | solution.py:34
  13.3 14.3 %collective-permute-start.8 = (bf16[4,32,1536]{2,1,0:T(8,128)(2,1)S(1)}, bf16[4,32,1536]{2,1,0:T(8,128)(2,1)S(1)}, u32[]{:S(2)}, u32[]{:S(2)}) collective-permute-start(bf16[4,32,1536]{2,1,0:T(8,128)(2,1)S(1)} %pad_maximum_fusion.1.refs_0_), channel_id=1, source_target_pairs={{0,1},{1,2},{2,3},{3,4},{4,5},{5,6},{6,7},{7,0},{8,9},{9,10},{10,1... | collective-permute-start | bytes 1179656 | tf_op jit(solution)/shard_map/ppermute | solution.py:49
  14.2 13.3 %collective-permute-start.10 = (bf16[4,32,1536]{2,1,0:T(8,128)(2,1)S(1)}, bf16[4,32,1536]{2,1,0:T(8,128)(2,1)S(1)}, u32[]{:S(2)}, u32[]{:S(2)}) collective-permute-start(bf16[4,32,1536]{2,1,0:T(8,128)(2,1)S(1)} %pad_maximum_fusion.1.refs_0_), channel_id=1, source_target_pairs={{0,7},{1,0},{2,1},{3,2},{4,3},{5,4},{6,5},{7,6},{8,15},{9,8},{10,9... | collective-permute-start | bytes 1179656 | tf_op jit(solution)/shard_map/ppermute | solution.py:49
  27.3 7.3 %collective-permute-start.4 = (bf16[64,1536]{1,0:T(8,128)(2,1)S(1)}, bf16[64,1536]{1,0:T(8,128)(2,1)S(1)}, u32[]{:S(2)}, u32[]{:S(2)}) collective-permute-start(bf16[64,1536]{1,0:T(8,128)(2,1)S(1)} %get-tuple-element.65), channel_id=1, source_target_pairs={{0,8},{8,16},{16,24},{24,0},{1,9},{9,17},{17,25},{25,1},{2,10},{10... | collective-permute-start | bytes 589832 | tf_op jit(solution)/shard_map/ppermute | solution.py:44
  27.5 11.3 %collective-permute-start.9 = (bf16[4,32,1536]{2,1,0:T(8,128)(2,1)S(1)}, bf16[4,32,1536]{2,1,0:T(8,128)(2,1)}, u32[]{:S(2)}, u32[]{:S(2)}) collective-permute-start(bf16[4,32,1536]{2,1,0:T(8,128)(2,1)S(1)} %collective-permute-done.8.refs_1_), channel_id=1, source_target_pairs={{0,1},{1,2},{2,3},{3,4},{4,5},{5,6},{6,7},{7,0},{8,9},{9,10},{10,1... | collective-permute-start | bytes 1179656 | tf_op jit(solution)/shard_map/ppermute | solution.py:49
  27.6 11.3 %collective-permute-start.11 = (bf16[4,32,1536]{2,1,0:T(8,128)(2,1)S(1)}, bf16[4,32,1536]{2,1,0:T(8,128)(2,1)}, u32[]{:S(2)}, u32[]{:S(2)}) collective-permute-start(bf16[4,32,1536]{2,1,0:T(8,128)(2,1)S(1)} %collective-permute-done.10.refs_8_), channel_id=1, source_target_pairs={{0,7},{1,0},{2,1},{3,2},{4,3},{5,4},{6,5},{7,6},{8,15},{9,8},{10,9... | collective-permute-start | bytes 1179656 | tf_op jit(solution)/shard_map/ppermute | solution.py:49
  31.1 10.6 %collective-permute-start.7 = (bf16[64,3072]{1,0:T(8,128)(2,1)S(1)}, bf16[64,3072]{1,0:T(8,128)(2,1)S(1)}, u32[]{:S(2)}, u32[]{:S(2)}) collective-permute-start(bf16[64,3072]{1,0:T(8,128)(2,1)S(1)} %pad_maximum_fusion.3), channel_id=1, source_target_pairs={{0,24},{8,0},{16,8},{24,16},{1,25},{9,1},{17,9},{25,17},{2,26},{10... | collective-permute-start | bytes 1179656 | tf_op jit(solution)/shard_map/ppermute | solution.py:44
  34.7 10.3 %collective-permute-start.5 = (bf16[64,3072]{1,0:T(8,128)(2,1)S(1)}, bf16[64,3072]{1,0:T(8,128)(2,1)S(1)}, u32[]{:S(2)}, u32[]{:S(2)}) collective-permute-start(bf16[64,3072]{1,0:T(8,128)(2,1)S(1)} %pad_maximum_fusion.2), channel_id=1, source_target_pairs={{0,8},{8,16},{16,24},{24,0},{1,9},{9,17},{17,25},{25,1},{2,10},{10... | collective-permute-start | bytes 1179656 | tf_op jit(solution)/shard_map/ppermute | solution.py:44
  38.8 12.7 %collective-permute-start.12 = (bf16[4,32,1536]{2,1,0:T(8,128)(2,1)}, bf16[4,32,1536]{2,1,0:T(8,128)(2,1)S(1)}, u32[]{:S(2)}, u32[]{:S(2)}) collective-permute-start(bf16[4,32,1536]{2,1,0:T(8,128)(2,1)} %collective-permute-done.9.refs_2_), channel_id=1, source_target_pairs={{0,1},{1,2},{2,3},{3,4},{4,5},{5,6},{6,7},{7,0},{8,9},{9,10},{10,1... | collective-permute-start | bytes 1179656 | tf_op jit(solution)/shard_map/ppermute | solution.py:49
  38.8 12.7 %collective-permute-start.13 = (bf16[4,32,1536]{2,1,0:T(8,128)(2,1)}, bf16[4,32,1536]{2,1,0:T(8,128)(2,1)S(1)}, u32[]{:S(2)}, u32[]{:S(2)}) collective-permute-start(bf16[4,32,1536]{2,1,0:T(8,128)(2,1)} %collective-permute-done.11.refs_7_), channel_id=1, source_target_pairs={{0,7},{1,0},{2,1},{3,2},{4,3},{5,4},{6,5},{7,6},{8,15},{9,8},{10,9... | collective-permute-start | bytes 1179656 | tf_op jit(solution)/shard_map/ppermute | solution.py:49
  46.6 22.0 %all-to-all-start = ((bf16[8,64,384]{2,1,0:T(8,128)(2,1)}), bf16[8,64,384]{2,1,0:T(8,128)(2,1)S(1)}, u32[]{:S(2)}, u32[]{:S(2)}) async-start(bf16[8,64,384]{2,1,0:T(8,128)(2,1)} %bitcast.43), calls=%async_computation | async-start | bytes 786432 | tf_op jit(solution)/shard_map/all_to_all | solution.py:274
  51.6 8.9 %collective-permute-start.14 = (bf16[64,3072]{1,0:T(8,128)(2,1)S(1)}, bf16[64,3072]{1,0:T(8,128)(2,1)S(1)}, u32[]{:S(2)}, u32[]{:S(2)}) collective-permute-start(bf16[64,3072]{1,0:T(8,128)(2,1)S(1)} %get-tuple-element.32), channel_id=1, source_target_pairs={{0,8},{8,16},{16,24},{24,0},{1,9},{9,17},{17,25},{25,1},{2,10},{10... | collective-permute-start | bytes 1179656 | tf_op jit(solution)/shard_map/ppermute | solution.py:44
  51.7 9.5 %collective-permute-start.16 = (bf16[64,3072]{1,0:T(8,128)(2,1)S(1)}, bf16[64,3072]{1,0:T(8,128)(2,1)S(1)}, u32[]{:S(2)}, u32[]{:S(2)}) collective-permute-start(bf16[64,3072]{1,0:T(8,128)(2,1)S(1)} %get-tuple-element.32), channel_id=1, source_target_pairs={{0,24},{8,0},{16,8},{24,16},{1,25},{9,1},{17,9},{25,17},{2,26},{10... | collective-permute-start | bytes 1179656 | tf_op jit(solution)/shard_map/ppermute | solution.py:44
  61.2 7.4 %collective-permute-start.15 = (bf16[32,3072]{1,0:T(8,128)(2,1)}, bf16[32,3072]{1,0:T(8,128)(2,1)S(1)}, u32[]{:S(2)}, u32[]{:S(2)}) collective-permute-start(bf16[32,3072]{1,0:T(8,128)(2,1)} %slice.125), channel_id=1, source_target_pairs={{0,8},{8,16},{16,24},{24,0},{1,9},{9,17},{17,25},{25,1},{2,10},{10... | collective-permute-start | bytes 589832 | tf_op jit(solution)/shard_map/ppermute | solution.py:44
  61.9 6.7 %collective-permute-start.17 = (bf16[32,3072]{1,0:T(8,128)(2,1)}, bf16[32,3072]{1,0:T(8,128)(2,1)S(1)}, u32[]{:S(2)}, u32[]{:S(2)}) collective-permute-start(bf16[32,3072]{1,0:T(8,128)(2,1)} %slice.126), channel_id=1, source_target_pairs={{0,24},{8,0},{16,8},{24,16},{1,25},{9,1},{17,9},{25,17},{2,26},{10... | collective-permute-start | bytes 589832 | tf_op jit(solution)/shard_map/ppermute | solution.py:44
  68.6 19.2 %collective-permute-start.18 = (bf16[8,64,384]{2,1,0:T(8,128)(2,1)S(1)}, bf16[8,64,384]{2,1,0:T(8,128)(2,1)S(1)}, u32[]{:S(2)}, u32[]{:S(2)}) collective-permute-start(bf16[8,64,384]{2,1,0:T(8,128)(2,1)S(1)} %all-to-all-done.refs_7_), channel_id=1, source_target_pairs={{0,8},{8,16},{16,24},{24,0},{1,9},{9,17},{17,25},{25,1},{2,10},{10... | collective-permute-start | bytes 1179656 | tf_op jit(solution)/shard_map/ppermute | solution.py:44
  68.7 19.1 %collective-permute-start.19 = (bf16[8,64,384]{2,1,0:T(8,128)(2,1)S(1)}, bf16[8,64,384]{2,1,0:T(8,128)(2,1)S(1)}, u32[]{:S(2)}, u32[]{:S(2)}) collective-permute-start(bf16[8,64,384]{2,1,0:T(8,128)(2,1)S(1)} %all-to-all-done.refs_7_), channel_id=1, source_target_pairs={{0,24},{8,0},{16,8},{24,16},{1,25},{9,1},{17,9},{25,17},{2,26},{10... | collective-permute-start | bytes 1179656 | tf_op jit(solution)/shard_map/ppermute | solution.py:44
  75.6 19.5 %collective-permute-start.25 = (bf16[8,4,32,1536]{3,2,1,0:T(8,128)(2,1)}, bf16[8,4,32,1536]{3,2,1,0:T(8,128)(2,1)S(1)}, u32[]{:S(2)}, u32[]{:S(2)}) collective-permute-start(bf16[8,4,32,1536]{3,2,1,0:T(8,128)(2,1)} %stack_up.1.refs_1_.refs_3_.refs_5_.refs_2_), channel_id=1, source_target_pairs={{0,32},{32,0},{64,96},{96,64},{128,160},{160,128},{192,224},{224,1... | collective-permute-start | bytes 9437192 | tf_op jit(solution)/shard_map/ppermute | solution.py:39
  88.7 10.9 %collective-permute-start.21 = (bf16[4,64,384]{2,1,0:T(8,128)(2,1)S(1)}, bf16[4,64,384]{2,1,0:T(8,128)(2,1)S(1)}, u32[]{:S(2)}, u32[]{:S(2)}) collective-permute-start(bf16[4,64,384]{2,1,0:T(8,128)(2,1)S(1)} %slice.107), channel_id=1, source_target_pairs={{0,8},{8,16},{16,24},{24,0},{1,9},{9,17},{17,25},{25,1},{2,10},{10... | collective-permute-start | bytes 589832 | tf_op jit(solution)/shard_map/ppermute | solution.py:44
  89.9 9.7 %collective-permute-start.22 = (bf16[4,64,384]{2,1,0:T(8,128)(2,1)S(1)}, bf16[4,64,384]{2,1,0:T(8,128)(2,1)S(1)}, u32[]{:S(2)}, u32[]{:S(2)}) collective-permute-start(bf16[4,64,384]{2,1,0:T(8,128)(2,1)S(1)} %slice.108), channel_id=1, source_target_pairs={{0,24},{8,0},{16,8},{24,16},{1,25},{9,1},{17,9},{25,17},{2,26},{10... | collective-permute-start | bytes 589832 | tf_op jit(solution)/shard_map/ppermute | solution.py:44
  91.7 7.9 %collective-permute-start.26 = (bf16[32,1536]{1,0:T(8,128)(2,1)S(1)}, bf16[32,1536]{1,0:T(8,128)(2,1)S(1)}, u32[]{:S(2)}, u32[]{:S(2)}) collective-permute-start(bf16[32,1536]{1,0:T(8,128)(2,1)S(1)} %get-tuple-element.61), channel_id=1, source_target_pairs={{0,64},{32,96},{64,128},{96,160},{128,192},{160,224},{192,0},{224,... | collective-permute-start | bytes 294920 | tf_op jit(solution)/shard_map/ppermute | solution.py:34
  92.6 7.1 %collective-permute-start.27 = (bf16[32,1536]{1,0:T(8,128)(2,1)S(1)}, bf16[32,1536]{1,0:T(8,128)(2,1)S(1)}, u32[]{:S(2)}, u32[]{:S(2)}) collective-permute-start(bf16[32,1536]{1,0:T(8,128)(2,1)S(1)} %get-tuple-element.60), channel_id=1, source_target_pairs={{0,192},{32,224},{64,0},{96,32},{128,64},{160,96},{192,128},{224,1... | collective-permute-start | bytes 294920 | tf_op jit(solution)/shard_map/ppermute | solution.py:34
  103.9 13.0 %all-to-all-start.1 = ((f32[32,1,128]{2,1,0:T(1,128)}), f32[32,1,128]{2,1,0:T(1,128)}, u32[]{:S(2)}, u32[]{:S(2)}) async-start(f32[32,1,128]{2,1,0:T(1,128)} %get-tuple-element.51), calls=%async_computation.1 | async-start | bytes 32768 | tf_op jit(solution)/shard_map/all_to_all | solution.py:274
  118.3 12.3 %all-to-all-start.2 = ((f32[8,1,128]{2,1,0:T(1,128)}), f32[8,1,128]{2,1,0:T(1,128)S(1)}, u32[]{:S(2)}, u32[]{:S(2)}) async-start(f32[8,1,128]{2,1,0:T(1,128)} %broadcast_in_dim.2), calls=%async_computation.2 | async-start | bytes 8192 | tf_op jit(solution)/shard_map/all_to_all | solution.py:274
  (22 other events, 155.0 us)

commit v4 on v3

--- a/solution.py
+++ b/solution.py
@@ -324,7 +324,7 @@
     b4 = shift_col(b3[tok:], 3)
     columns = exchange(after(grad_share, up2, dn2).reshape(share, n_depth, block_ff).transpose(1, 0, 2), "depth")
 
-    columns, b1, b2, b3, b4 = lax.optimization_barrier((columns, b1, b2, b3, b4))
+    columns, b1, b3 = lax.optimization_barrier((columns, b1, b3))
     t_mine = stack_up([after(mine, columns), up1, up2, up3, up4, dn4, dn3, dn2, dn1])
     t_other = swap_core(t_mine)
 

time: 134 us -> 129 us (0.963)
  starting transfers between devices: 65.5 us -> 61.5 us
  waiting for transfers between devices: 30.6 us -> 28.3 us
    ppermute x12, waiting for transfers between devices: 10.5 us -> 6.44 us  [shift_col(): return lax.ppermute(value, 'col', [(i, (i + k) % n) for i in range(n)])]
    ppermute x12, starting transfers between devices: 17.2 us -> 14.5 us  [shift_col(): return lax.ppermute(value, 'col', [(i, (i + k) % n) for i in range(n)])]
    ppermute x8, waiting for transfers between devices: 4.86 us -> 6.66 us  [shift_depth(): return lax.ppermute(value, 'depth', [(i, (i + k) % n) for i in range(n)])]
    ppermute x3, starting transfers between devices: 7.81 us -> 6.32 us  [swap_core(): return lax.ppermute(value, 'row', [(i, i ^ 1) for i in range(n)])]
    unnamed x32, local copies, waits for them, and re-layouts: 1.98 us -> 3.39 us
  transfers between devices with their start and end apart: 32 -> 32, of which waited for: 12 -> 11; matrix products, arithmetic and copies ran while one was open for 15% -> 16% of each run, Pallas kernels for 5% -> 5%
where the time goes in v4:
time: 129 us; the launch traced here: 128 us
  starting transfers between devices  61.5 us (48%)
  waiting for transfers between devices  28.3 us (22%)
  Pallas kernels  12.7 us (10%)
  matrix products  10.5 us (8%)
  local copies, waits for them, and re-layouts  7.91 us (6%)
  other arithmetic  6.38 us (5%)
    all_to_all x3, starting transfers between devices, exchange(): return lax.all_to_all(value, axes, split_axis=0, concat_axis=0, tiled=True)  16.8 us
    ppermute x12, starting transfers between devices, shift_col(): return lax.ppermute(value, 'col', [(i, (i + k) % n) for i in range(n)])  14.5 us
    ppermute x8, starting transfers between devices, shift_depth(): return lax.ppermute(value, 'depth', [(i, (i + k) % n) for i in range(n)])  12.9 us
    ppermute x6, starting transfers between devices, shift_row(): return lax.ppermute(value, 'row', [(i, (i + 2 * k) % n) for i in range(n)])  10.9 us
    all_to_all x3, waiting for transfers between devices, exchange(): return lax.all_to_all(value, axes, split_axis=0, concat_axis=0, tiled=True)  9.99 us
    ppermute x8, waiting for transfers between devices, shift_depth(): return lax.ppermute(value, 'depth', [(i, (i + k) % n) for i in range(n)])  6.66 us
    pallas_call x2, Pallas kernels, grad_step(): pl.pallas_call(body, grid=(feat // width,), in_specs=specs, out_specs=out...  6.64 us
    ppermute x12, waiting for transfers between devices, shift_col(): return lax.ppermute(value, 'col', [(i, (i + k) % n) for i in range(n)])  6.44 us
  transfers between devices with their start and end apart: 32, of which 11 were waited for; matrix products, arithmetic and copies ran while one was open for 16% of the time, Pallas kernels for 5%

profile of v4, /device:TPU:1, one launch (start us, length us, event | category | flops | bytes accessed | tf_op | source)
XLA Modules:
  0.0 128.4 jit_solution(10763877624329990448)
XLA Ops:
  0.6 3.8 %collective-permute-start = (bf16[32,1536]{1,0:T(8,128)(2,1)}, bf16[32,1536]{1,0:T(8,128)(2,1)S(1)}, u32[]{:S(2)}, u32[]{:S(2)}) collective-permute-start(bf16[32,1536]{1,0:T(8,128)(2,1)} %param.4), channel_id=1, source_target_pairs={{0,128},{32,160},{64,192},{96,224},{128,0},{160,32},{192,64},{224,... | collective-permute-start | bytes 294920 | tf_op jit(solution)/shard_map/ppermute | solution.py:34
  7.1 4.2 %collective-permute-done.1 = bf16[32,1536]{1,0:T(8,128)(2,1)S(1)} collective-permute-done((bf16[32,1536]{1,0:T(8,128)(2,1)}, bf16[32,1536]{1,0:T(8,128)(2,1)S(1)}, u32[]{:S(2)}, u32[]{:S(2)}) %collective-permute-start.1) | collective-permute-done | bytes 98336 | tf_op jit(solution)/shard_map/ppermute | solution.py:34
  14.2 3.9 %collective-permute-start.10 = (bf16[4,32,1536]{2,1,0:T(8,128)(2,1)S(1)}, bf16[4,32,1536]{2,1,0:T(8,128)(2,1)S(1)}, u32[]{:S(2)}, u32[]{:S(2)}) collective-permute-start(bf16[4,32,1536]{2,1,0:T(8,128)(2,1)S(1)} %pad_maximum_fusion.1.refs_0_), channel_id=1, source_target_pairs={{0,7},{1,0},{2,1},{3,2},{4,3},{5,4},{6,5},{7,6},{8,15},{9,8},{10,9... | collective-permute-start | bytes 1179656 | tf_op jit(solution)/shard_map/ppermute | solution.py:49
  18.2 3.9 %fusion.7 = bf16[256,1536]{1,0:T(8,128)(2,1)S(1)} fusion(bf16[256,1536]{1,0:T(8,128)(2,1)S(1)} %bitcast.47, bf16[1536,3072]{1,0:T(8,128)(2,1)} %param.5), kind=kOutput, calls=%fused_computation.5 | convolution fusion | flops 1208352768 | bytes 6291456 | tf_op jit(solution)/shard_map/dot_general | solution.py:307
  24.7 2.6 %collective-permute-start.6 = (bf16[64,1536]{1,0:T(8,128)(2,1)S(1)}, bf16[64,1536]{1,0:T(8,128)(2,1)S(1)}, u32[]{:S(2)}, u32[]{:S(2)}) collective-permute-start(bf16[64,1536]{1,0:T(8,128)(2,1)S(1)} %get-tuple-element.62), channel_id=1, source_target_pairs={{0,24},{8,0},{16,8},{24,16},{1,25},{9,1},{17,9},{25,17},{2,26},{10... | collective-permute-start | bytes 589832 | tf_op jit(solution)/shard_map/ppermute | solution.py:44
  27.6 2.7 %collective-permute-start.11 = (bf16[4,32,1536]{2,1,0:T(8,128)(2,1)S(1)}, bf16[4,32,1536]{2,1,0:T(8,128)(2,1)}, u32[]{:S(2)}, u32[]{:S(2)}) collective-permute-start(bf16[4,32,1536]{2,1,0:T(8,128)(2,1)S(1)} %collective-permute-done.10.refs_8_), channel_id=1, source_target_pairs={{0,7},{1,0},{2,1},{3,2},{4,3},{5,4},{6,5},{7,6},{8,15},{9,8},{10,9... | collective-permute-start | bytes 1179656 | tf_op jit(solution)/shard_map/ppermute | solution.py:49
  31.1 3.5 %collective-permute-start.7 = (bf16[64,3072]{1,0:T(8,128)(2,1)S(1)}, bf16[64,3072]{1,0:T(8,128)(2,1)S(1)}, u32[]{:S(2)}, u32[]{:S(2)}) collective-permute-start(bf16[64,3072]{1,0:T(8,128)(2,1)S(1)} %pad_maximum_fusion.3), channel_id=1, source_target_pairs={{0,24},{8,0},{16,8},{24,16},{1,25},{9,1},{17,9},{25,17},{2,26},{10... | collective-permute-start | bytes 1179656 | tf_op jit(solution)/shard_map/ppermute | solution.py:44
  34.9 3.9 %collective-permute-done.9.refs_2_ = bf16[4,32,1536]{2,1,0:T(8,128)(2,1)} collective-permute-done((bf16[4,32,1536]{2,1,0:T(8,128)(2,1)S(1)}, bf16[4,32,1536]{2,1,0:T(8,128)(2,1)}, u32[]{:S(2)}, u32[]{:S(2)}) %collective-permute-start.9) | collective-permute-done | bytes 393248 | tf_op jit(solution)/shard_map/ppermute | solution.py:49
  38.8 2.7 %collective-permute-start.13 = (bf16[4,32,1536]{2,1,0:T(8,128)(2,1)}, bf16[4,32,1536]{2,1,0:T(8,128)(2,1)S(1)}, u32[]{:S(2)}, u32[]{:S(2)}) collective-permute-start(bf16[4,32,1536]{2,1,0:T(8,128)(2,1)} %collective-permute-done.11.refs_7_), channel_id=1, source_target_pairs={{0,7},{1,0},{2,1},{3,2},{4,3},{5,4},{6,5},{7,6},{8,15},{9,8},{10,9... | collective-permute-start | bytes 1179656 | tf_op jit(solution)/shard_map/ppermute | solution.py:49
  41.7 3.3 %collective-permute-done.5 = bf16[64,3072]{1,0:T(8,128)(2,1)S(1)} collective-permute-done((bf16[64,3072]{1,0:T(8,128)(2,1)S(1)}, bf16[64,3072]{1,0:T(8,128)(2,1)S(1)}, u32[]{:S(2)}, u32[]{:S(2)}) %collective-permute-start.5) | collective-permute-done | bytes 393248 | tf_op jit(solution)/shard_map/ppermute | solution.py:44
  46.6 4.9 %all-to-all-start = ((bf16[8,64,384]{2,1,0:T(8,128)(2,1)}), bf16[8,64,384]{2,1,0:T(8,128)(2,1)S(1)}, u32[]{:S(2)}, u32[]{:S(2)}) async-start(bf16[8,64,384]{2,1,0:T(8,128)(2,1)} %bitcast.43), calls=%async_computation | async-start | bytes 786432 | tf_op jit(solution)/shard_map/all_to_all | solution.py:274
  51.7 2.7 %collective-permute-start.15 = (bf16[64,3072]{1,0:T(8,128)(2,1)S(1)}, bf16[64,3072]{1,0:T(8,128)(2,1)S(1)}, u32[]{:S(2)}, u32[]{:S(2)}) collective-permute-start(bf16[64,3072]{1,0:T(8,128)(2,1)S(1)} %get-tuple-element.30), channel_id=1, source_target_pairs={{0,24},{8,0},{16,8},{24,16},{1,25},{9,1},{17,9},{25,17},{2,26},{10... | collective-permute-start | bytes 1179656 | tf_op jit(solution)/shard_map/ppermute | solution.py:44
  61.4 2.5 %collective-permute-start.19 = (bf16[32,3072]{1,0:T(8,128)(2,1)}, bf16[32,3072]{1,0:T(8,128)(2,1)}, u32[]{:S(2)}, u32[]{:S(2)}) collective-permute-start(bf16[32,3072]{1,0:T(8,128)(2,1)} %slice.126), channel_id=1, source_target_pairs={{0,24},{8,0},{16,8},{24,16},{1,25},{9,1},{17,9},{25,17},{2,26},{10... | collective-permute-start | bytes 589832 | tf_op jit(solution)/shard_map/ppermute | solution.py:44
  67.9 2.8 %stack_up.1.refs_1_.refs_3_.refs_5_.refs_2_ = bf16[8,4,32,1536]{3,2,1,0:T(8,128)(2,1)} custom-call(bf16[4,32,1536]{2,1,0:T(8,128)(2,1)} %copy-done.1, bf16[4,32,1536]{2,1,0:T(8,128)(2,1)} %copy-done.5, bf16[4,32,1536]{2,1,0:T(8,128)(2,1)} %collective-permute-done.9.refs_2_, bf16[4,32,1536]{2,1,0:T(8,128)(2,1)} %copy-done.3, bf16[2,32,1536]{2,1,0:T(8,128)(2,1)} %copy-done.7, ...), custom_call_target="tpu_custom_call" | custom-call | bytes 6291456 | tf_op jit(solution)/shard_map/stack_up/pallas_call | solution.py:94
  70.6 5.3 %collective-permute-start.25 = (bf16[8,4,32,1536]{3,2,1,0:T(8,128)(2,1)}, bf16[8,4,32,1536]{3,2,1,0:T(8,128)(2,1)S(1)}, u32[]{:S(2)}, u32[]{:S(2)}) collective-permute-start(bf16[8,4,32,1536]{3,2,1,0:T(8,128)(2,1)} %stack_up.1.refs_1_.refs_3_.refs_5_.refs_2_), channel_id=1, source_target_pairs={{0,32},{32,0},{64,96},{96,64},{128,160},{160,128},{192,224},{224,1... | collective-permute-start | bytes 9437192 | tf_op jit(solution)/shard_map/ppermute | solution.py:39
  77.0 5.2 %fusion.29 = f32[256,1536]{1,0:T(8,128)S(1)} fusion(bf16[256,3072]{1,0:T(8,128)(2,1)S(1)} %constant_dynamic-update-slice_fusion, bf16[1536,3072]{1,0:T(8,128)(2,1)} %param.5), kind=kOutput, calls=%fused_computation.55 | convolution fusion | flops 2415919104 | bytes 12582912 | tf_op jit(solution)/shard_map/dot_general | solution.py:337
  83.3 2.7 %collective-permute-start.22 = (bf16[4,64,384]{2,1,0:T(8,128)(2,1)S(1)}, bf16[4,64,384]{2,1,0:T(8,128)(2,1)S(1)}, u32[]{:S(2)}, u32[]{:S(2)}) collective-permute-start(bf16[4,64,384]{2,1,0:T(8,128)(2,1)S(1)} %slice.108), channel_id=1, source_target_pairs={{0,24},{8,0},{16,8},{24,16},{1,25},{9,1},{17,9},{25,17},{2,26},{10... | collective-permute-start | bytes 589832 | tf_op jit(solution)/shard_map/ppermute | solution.py:44
  90.7 3.5 %grad_step.2 = (f32[384,1536]{1,0:T(8,128)S(1)}, f32[1,384]{1,0:T(1,128)S(1)}) custom-call(s32[1]{0:T(128)} %bitcast.10.refs_0_, bf16[8,4,32,1536]{3,2,1,0:T(8,128)(2,1)S(1)} %copy-done, bf16[8,4,32,1536]{3,2,1,0:T(8,128)(2,1)S(1)} %collective-permute-done.25.refs_2_.refs_4_.refs_6_.refs_3_, bf16[8,4,32,1536]{3,2,1,0:T(8,128)(2,1)S(1)} %copy-done, ...), custom_call_target="tpu_custom_call" | custom-call | flops 1811939328 | bytes 9437184 | tf_op jit(solution)/shard_map/grad_step/pallas_call | solution.py:218
  95.2 3.2 %grad_step.3 = (f32[384,1536]{1,0:T(8,128)S(1)}, f32[1,384]{1,0:T(1,128)S(1)}, f32[32,1,128]{2,1,0:T(1,128)}) custom-call(s32[1]{0:T(128)} %bitcast.10.refs_0_, f32[1]{0:T(128)} %bitcast.14.refs_1_, bf16[8,4,32,1536]{3,2,1,0:T(8,128)(2,1)S(1)} %copy-done, bf16[8,4,32,1536]{3,2,1,0:T(8,128)(2,1)S(1)} %collective-permute-done.25.refs_2_.refs_4_.refs_6_.refs_3_, ...), custom_call_target="tpu_custom_call" | custom-call | flops 603979776 | bytes 6291456 | tf_op jit(solution)/shard_map/grad_step/pallas_call | solution.py:218
  98.4 5.9 %all-to-all-start.1 = ((f32[32,1,128]{2,1,0:T(1,128)}), f32[32,1,128]{2,1,0:T(1,128)}, u32[]{:S(2)}, u32[]{:S(2)}) async-start(f32[32,1,128]{2,1,0:T(1,128)} %get-tuple-element.47), calls=%async_computation.1 | async-start | bytes 32768 | tf_op jit(solution)/shard_map/all_to_all | solution.py:274
  106.2 5.2 %all-to-all-done.1 = f32[32,1,128]{2,1,0:T(1,128)} async-done(((f32[32,1,128]{2,1,0:T(1,128)}), f32[32,1,128]{2,1,0:T(1,128)}, u32[]{:S(2)}, u32[]{:S(2)}) %all-to-all-start.1) | async-done | bytes 16416 | tf_op jit(solution)/shard_map/all_to_all | solution.py:274
  112.7 6.0 %all-to-all-start.2 = ((f32[8,1,128]{2,1,0:T(1,128)}), f32[8,1,128]{2,1,0:T(1,128)S(1)}, u32[]{:S(2)}, u32[]{:S(2)}) async-start(f32[8,1,128]{2,1,0:T(1,128)} %broadcast_in_dim.2), calls=%async_computation.2 | async-start | bytes 8192 | tf_op jit(solution)/shard_map/all_to_all | solution.py:274
  120.4 4.8 %all-to-all-done.2.p = f32[8,1,128]{2,1,0:T(1,128)S(1)} async-done(((f32[8,1,128]{2,1,0:T(1,128)}), f32[8,1,128]{2,1,0:T(1,128)S(1)}, u32[]{:S(2)}, u32[]{:S(2)}) %all-to-all-start.2) | async-done | bytes 4128 | tf_op jit(solution)/shard_map/all_to_all | solution.py:274
  125.2 3.3 %clip.1 = (f32[1536,384]{1,0:T(8,128)}, f32[384]{0:T(512)}, f32[1]{0:T(128)}) custom-call(f32[8,1,128]{2,1,0:T(1,128)S(1)} %all-to-all-done.2.p, f32[384,1536]{1,0:T(8,128)S(1)} %get-tuple-element.48.r, f32[1,384]{1,0:T(1,128)S(1)} %get-tuple-element.49.b), custom_call_target="tpu_custom_call" | custom-call | tf_op jit(solution)/shard_map/clip/pallas_call | solution.py:250
  (107 shorter events, 34.9 us)
Async XLA Ops:
  13.3 14.3 %collective-permute-start.8 = (bf16[4,32,1536]{2,1,0:T(8,128)(2,1)S(1)}, bf16[4,32,1536]{2,1,0:T(8,128)(2,1)S(1)}, u32[]{:S(2)}, u32[]{:S(2)}) collective-permute-start(bf16[4,32,1536]{2,1,0:T(8,128)(2,1)S(1)} %pad_maximum_fusion.1.refs_0_), channel_id=1, source_target_pairs={{0,1},{1,2},{2,3},{3,4},{4,5},{5,6},{6,7},{7,0},{8,9},{9,10},{10,1... | collective-permute-start | bytes 1179656 | tf_op jit(solution)/shard_map/ppermute | solution.py:49
  14.2 13.3 %collective-permute-start.10 = (bf16[4,32,1536]{2,1,0:T(8,128)(2,1)S(1)}, bf16[4,32,1536]{2,1,0:T(8,128)(2,1)S(1)}, u32[]{:S(2)}, u32[]{:S(2)}) collective-permute-start(bf16[4,32,1536]{2,1,0:T(8,128)(2,1)S(1)} %pad_maximum_fusion.1.refs_0_), channel_id=1, source_target_pairs={{0,7},{1,0},{2,1},{3,2},{4,3},{5,4},{6,5},{7,6},{8,15},{9,8},{10,9... | collective-permute-start | bytes 1179656 | tf_op jit(solution)/shard_map/ppermute | solution.py:49
  27.3 7.3 %collective-permute-start.4 = (bf16[64,1536]{1,0:T(8,128)(2,1)S(1)}, bf16[64,1536]{1,0:T(8,128)(2,1)S(1)}, u32[]{:S(2)}, u32[]{:S(2)}) collective-permute-start(bf16[64,1536]{1,0:T(8,128)(2,1)S(1)} %get-tuple-element.61), channel_id=1, source_target_pairs={{0,8},{8,16},{16,24},{24,0},{1,9},{9,17},{17,25},{25,1},{2,10},{10... | collective-permute-start | bytes 589832 | tf_op jit(solution)/shard_map/ppermute | solution.py:44
  27.5 11.3 %collective-permute-start.9 = (bf16[4,32,1536]{2,1,0:T(8,128)(2,1)S(1)}, bf16[4,32,1536]{2,1,0:T(8,128)(2,1)}, u32[]{:S(2)}, u32[]{:S(2)}) collective-permute-start(bf16[4,32,1536]{2,1,0:T(8,128)(2,1)S(1)} %collective-permute-done.8.refs_1_), channel_id=1, source_target_pairs={{0,1},{1,2},{2,3},{3,4},{4,5},{5,6},{6,7},{7,0},{8,9},{9,10},{10,1... | collective-permute-start | bytes 1179656 | tf_op jit(solution)/shard_map/ppermute | solution.py:49
  27.6 11.3 %collective-permute-start.11 = (bf16[4,32,1536]{2,1,0:T(8,128)(2,1)S(1)}, bf16[4,32,1536]{2,1,0:T(8,128)(2,1)}, u32[]{:S(2)}, u32[]{:S(2)}) collective-permute-start(bf16[4,32,1536]{2,1,0:T(8,128)(2,1)S(1)} %collective-permute-done.10.refs_8_), channel_id=1, source_target_pairs={{0,7},{1,0},{2,1},{3,2},{4,3},{5,4},{6,5},{7,6},{8,15},{9,8},{10,9... | collective-permute-start | bytes 1179656 | tf_op jit(solution)/shard_map/ppermute | solution.py:49
  31.1 10.6 %collective-permute-start.7 = (bf16[64,3072]{1,0:T(8,128)(2,1)S(1)}, bf16[64,3072]{1,0:T(8,128)(2,1)S(1)}, u32[]{:S(2)}, u32[]{:S(2)}) collective-permute-start(bf16[64,3072]{1,0:T(8,128)(2,1)S(1)} %pad_maximum_fusion.3), channel_id=1, source_target_pairs={{0,24},{8,0},{16,8},{24,16},{1,25},{9,1},{17,9},{25,17},{2,26},{10... | collective-permute-start | bytes 1179656 | tf_op jit(solution)/shard_map/ppermute | solution.py:44
  34.7 10.3 %collective-permute-start.5 = (bf16[64,3072]{1,0:T(8,128)(2,1)S(1)}, bf16[64,3072]{1,0:T(8,128)(2,1)S(1)}, u32[]{:S(2)}, u32[]{:S(2)}) collective-permute-start(bf16[64,3072]{1,0:T(8,128)(2,1)S(1)} %pad_maximum_fusion.2), channel_id=1, source_target_pairs={{0,8},{8,16},{16,24},{24,0},{1,9},{9,17},{17,25},{25,1},{2,10},{10... | collective-permute-start | bytes 1179656 | tf_op jit(solution)/shard_map/ppermute | solution.py:44
  38.8 12.7 %collective-permute-start.12 = (bf16[4,32,1536]{2,1,0:T(8,128)(2,1)}, bf16[4,32,1536]{2,1,0:T(8,128)(2,1)S(1)}, u32[]{:S(2)}, u32[]{:S(2)}) collective-permute-start(bf16[4,32,1536]{2,1,0:T(8,128)(2,1)} %collective-permute-done.9.refs_2_), channel_id=1, source_target_pairs={{0,1},{1,2},{2,3},{3,4},{4,5},{5,6},{6,7},{7,0},{8,9},{9,10},{10,1... | collective-permute-start | bytes 1179656 | tf_op jit(solution)/shard_map/ppermute | solution.py:49
  38.8 12.7 %collective-permute-start.13 = (bf16[4,32,1536]{2,1,0:T(8,128)(2,1)}, bf16[4,32,1536]{2,1,0:T(8,128)(2,1)S(1)}, u32[]{:S(2)}, u32[]{:S(2)}) collective-permute-start(bf16[4,32,1536]{2,1,0:T(8,128)(2,1)} %collective-permute-done.11.refs_7_), channel_id=1, source_target_pairs={{0,7},{1,0},{2,1},{3,2},{4,3},{5,4},{6,5},{7,6},{8,15},{9,8},{10,9... | collective-permute-start | bytes 1179656 | tf_op jit(solution)/shard_map/ppermute | solution.py:49
  46.6 17.4 %all-to-all-start = ((bf16[8,64,384]{2,1,0:T(8,128)(2,1)}), bf16[8,64,384]{2,1,0:T(8,128)(2,1)S(1)}, u32[]{:S(2)}, u32[]{:S(2)}) async-start(bf16[8,64,384]{2,1,0:T(8,128)(2,1)} %bitcast.43), calls=%async_computation | async-start | bytes 786432 | tf_op jit(solution)/shard_map/all_to_all | solution.py:274
  51.6 8.9 %collective-permute-start.14 = (bf16[64,3072]{1,0:T(8,128)(2,1)S(1)}, bf16[64,3072]{1,0:T(8,128)(2,1)S(1)}, u32[]{:S(2)}, u32[]{:S(2)}) collective-permute-start(bf16[64,3072]{1,0:T(8,128)(2,1)S(1)} %get-tuple-element.30), channel_id=1, source_target_pairs={{0,8},{8,16},{16,24},{24,0},{1,9},{9,17},{17,25},{25,1},{2,10},{10... | collective-permute-start | bytes 1179656 | tf_op jit(solution)/shard_map/ppermute | solution.py:44
  51.7 9.0 %collective-permute-start.15 = (bf16[64,3072]{1,0:T(8,128)(2,1)S(1)}, bf16[64,3072]{1,0:T(8,128)(2,1)S(1)}, u32[]{:S(2)}, u32[]{:S(2)}) collective-permute-start(bf16[64,3072]{1,0:T(8,128)(2,1)S(1)} %get-tuple-element.30), channel_id=1, source_target_pairs={{0,24},{8,0},{16,8},{24,16},{1,25},{9,1},{17,9},{25,17},{2,26},{10... | collective-permute-start | bytes 1179656 | tf_op jit(solution)/shard_map/ppermute | solution.py:44
  55.0 11.5 %collective-permute-start.23 = (bf16[2,32,1536]{2,1,0:T(8,128)(2,1)}, bf16[2,32,1536]{2,1,0:T(8,128)(2,1)S(1)}, u32[]{:S(2)}, u32[]{:S(2)}) collective-permute-start(bf16[2,32,1536]{2,1,0:T(8,128)(2,1)} %slice.129), channel_id=1, source_target_pairs={{0,1},{1,2},{2,3},{3,4},{4,5},{5,6},{6,7},{7,0},{8,9},{9,10},{10,1... | collective-permute-start | bytes 589832 | tf_op jit(solution)/shard_map/ppermute | solution.py:49
  57.2 9.5 %collective-permute-start.24 = (bf16[2,32,1536]{2,1,0:T(8,128)(2,1)}, bf16[2,32,1536]{2,1,0:T(8,128)(2,1)S(1)}, u32[]{:S(2)}, u32[]{:S(2)}) collective-permute-start(bf16[2,32,1536]{2,1,0:T(8,128)(2,1)} %slice.130), channel_id=1, source_target_pairs={{0,7},{1,0},{2,1},{3,2},{4,3},{5,4},{6,5},{7,6},{8,15},{9,8},{10,9... | collective-permute-start | bytes 589832 | tf_op jit(solution)/shard_map/ppermute | solution.py:49
  60.5 15.4 %collective-permute-start.18 = (bf16[32,3072]{1,0:T(8,128)(2,1)S(1)}, bf16[32,3072]{1,0:T(8,128)(2,1)S(1)}, u32[]{:S(2)}, u32[]{:S(2)}) collective-permute-start(bf16[32,3072]{1,0:T(8,128)(2,1)S(1)} %slice.125), channel_id=1, source_target_pairs={{0,8},{8,16},{16,24},{24,0},{1,9},{9,17},{17,25},{25,1},{2,10},{10... | collective-permute-start | bytes 589832 | tf_op jit(solution)/shard_map/ppermute | solution.py:44
  61.4 14.5 %collective-permute-start.19 = (bf16[32,3072]{1,0:T(8,128)(2,1)}, bf16[32,3072]{1,0:T(8,128)(2,1)}, u32[]{:S(2)}, u32[]{:S(2)}) collective-permute-start(bf16[32,3072]{1,0:T(8,128)(2,1)} %slice.126), channel_id=1, source_target_pairs={{0,24},{8,0},{16,8},{24,16},{1,25},{9,1},{17,9},{25,17},{2,26},{10... | collective-permute-start | bytes 589832 | tf_op jit(solution)/shard_map/ppermute | solution.py:44
  64.0 18.3 %collective-permute-start.16 = (bf16[8,64,384]{2,1,0:T(8,128)(2,1)S(1)}, bf16[8,64,384]{2,1,0:T(8,128)(2,1)S(1)}, u32[]{:S(2)}, u32[]{:S(2)}) collective-permute-start(bf16[8,64,384]{2,1,0:T(8,128)(2,1)S(1)} %all-to-all-done.refs_7_), channel_id=1, source_target_pairs={{0,8},{8,16},{16,24},{24,0},{1,9},{9,17},{17,25},{25,1},{2,10},{10... | collective-permute-start | bytes 1179656 | tf_op jit(solution)/shard_map/ppermute | solution.py:44
  66.5 15.7 %collective-permute-start.17 = (bf16[8,64,384]{2,1,0:T(8,128)(2,1)S(1)}, bf16[8,64,384]{2,1,0:T(8,128)(2,1)S(1)}, u32[]{:S(2)}, u32[]{:S(2)}) collective-permute-start(bf16[8,64,384]{2,1,0:T(8,128)(2,1)S(1)} %all-to-all-done.refs_7_), channel_id=1, source_target_pairs={{0,24},{8,0},{16,8},{24,16},{1,25},{9,1},{17,9},{25,17},{2,26},{10... | collective-permute-start | bytes 1179656 | tf_op jit(solution)/shard_map/ppermute | solution.py:44
  70.6 18.9 %collective-permute-start.25 = (bf16[8,4,32,1536]{3,2,1,0:T(8,128)(2,1)}, bf16[8,4,32,1536]{3,2,1,0:T(8,128)(2,1)S(1)}, u32[]{:S(2)}, u32[]{:S(2)}) collective-permute-start(bf16[8,4,32,1536]{3,2,1,0:T(8,128)(2,1)} %stack_up.1.refs_1_.refs_3_.refs_5_.refs_2_), channel_id=1, source_target_pairs={{0,32},{32,0},{64,96},{96,64},{128,160},{160,128},{192,224},{224,1... | collective-permute-start | bytes 9437192 | tf_op jit(solution)/shard_map/ppermute | solution.py:39
  83.2 10.9 %collective-permute-start.21 = (bf16[4,64,384]{2,1,0:T(8,128)(2,1)S(1)}, bf16[4,64,384]{2,1,0:T(8,128)(2,1)S(1)}, u32[]{:S(2)}, u32[]{:S(2)}) collective-permute-start(bf16[4,64,384]{2,1,0:T(8,128)(2,1)S(1)} %slice.107), channel_id=1, source_target_pairs={{0,8},{8,16},{16,24},{24,0},{1,9},{9,17},{17,25},{25,1},{2,10},{10... | collective-permute-start | bytes 589832 | tf_op jit(solution)/shard_map/ppermute | solution.py:44
  83.3 10.8 %collective-permute-start.22 = (bf16[4,64,384]{2,1,0:T(8,128)(2,1)S(1)}, bf16[4,64,384]{2,1,0:T(8,128)(2,1)S(1)}, u32[]{:S(2)}, u32[]{:S(2)}) collective-permute-start(bf16[4,64,384]{2,1,0:T(8,128)(2,1)S(1)} %slice.108), channel_id=1, source_target_pairs={{0,24},{8,0},{16,8},{24,16},{1,25},{9,1},{17,9},{25,17},{2,26},{10... | collective-permute-start | bytes 589832 | tf_op jit(solution)/shard_map/ppermute | solution.py:44
  86.2 7.9 %collective-permute-start.26 = (bf16[32,1536]{1,0:T(8,128)(2,1)S(1)}, bf16[32,1536]{1,0:T(8,128)(2,1)S(1)}, u32[]{:S(2)}, u32[]{:S(2)}) collective-permute-start(bf16[32,1536]{1,0:T(8,128)(2,1)S(1)} %get-tuple-element.57), channel_id=1, source_target_pairs={{0,64},{32,96},{64,128},{96,160},{128,192},{160,224},{192,0},{224,... | collective-permute-start | bytes 294920 | tf_op jit(solution)/shard_map/ppermute | solution.py:34
  98.4 13.0 %all-to-all-start.1 = ((f32[32,1,128]{2,1,0:T(1,128)}), f32[32,1,128]{2,1,0:T(1,128)}, u32[]{:S(2)}, u32[]{:S(2)}) async-start(f32[32,1,128]{2,1,0:T(1,128)} %get-tuple-element.47), calls=%async_computation.1 | async-start | bytes 32768 | tf_op jit(solution)/shard_map/all_to_all | solution.py:274
  112.7 12.4 %all-to-all-start.2 = ((f32[8,1,128]{2,1,0:T(1,128)}), f32[8,1,128]{2,1,0:T(1,128)S(1)}, u32[]{:S(2)}, u32[]{:S(2)}) async-start(f32[8,1,128]{2,1,0:T(1,128)} %broadcast_in_dim.2), calls=%async_computation.2 | async-start | bytes 8192 | tf_op jit(solution)/shard_map/all_to_all | solution.py:274
  (22 other events, 146.6 us)

commit v5 on v4

--- a/solution.py
+++ b/solution.py
@@ -114,7 +114,7 @@
 def grad_step(t_mine, t_other, pieces, acc, depth, first_col=None):
     n_depth, n_share, rows, feat = t_mine.shape
     block_ff = pieces[0][1][0].shape[-1]
-    width = 512
+    width = 1536
     kdim = n_depth * rows
     n_p = len(pieces)
     counts = [len(p[1]) for p in pieces]
@@ -222,7 +222,7 @@
         out_specs=out_specs,
         out_shape=out_shape,
         scratch_shapes=scratch,
-        compiler_params=pltpu.CompilerParams(vmem_limit_bytes=12 * 2**20),
+        compiler_params=pltpu.CompilerParams(vmem_limit_bytes=24 * 2**20),
         cost_estimate=pl.CostEstimate(
             flops=n_p * 4 * kdim * block_ff * feat,
             bytes_accessed=n_p * 4 * kdim * feat + 8 * block_ff * feat,
@@ -234,7 +234,7 @@
 
 def clip(parts, raw, bias):
     block_ff, feat = raw.shape
-    width = 256
+    width = 768
 
     def body(p, r, b, o, ob, on):
         total = jnp.sum(p[...], axis=0)[:, :1]
@@ -265,7 +265,7 @@
             jax.ShapeDtypeStruct((block_ff,), F32),
             jax.ShapeDtypeStruct((1,), F32),
         ],
-        compiler_params=pltpu.CompilerParams(vmem_limit_bytes=4 * 2**20),
+        compiler_params=pltpu.CompilerParams(vmem_limit_bytes=8 * 2**20),
         name="clip",
     )(parts, raw, bias)
 

time: 129 us -> 127 us (0.984)
  Pallas kernels: 12.7 us -> 9.2 us
    pallas_call x2, Pallas kernels: 6.64 us -> 4.36 us  [grad_step(): pl.pallas_call(body, grid=(feat // width,), in_specs=specs, out_specs=out...]
  transfers between devices with their start and end apart: 32 -> 32, of which waited for: 11 -> 11; matrix products, arithmetic and copies ran while one was open for 16% -> 16% of each run, Pallas kernels for 5% -> 4%
where the time goes in v5:
time: 127 us; the launch traced here: 126 us
  starting transfers between devices  61.5 us (48%)
  waiting for transfers between devices  29.5 us (23%)
  matrix products  10.5 us (8%)
  Pallas kernels  9.2 us (7%)
  local copies, waits for them, and re-layouts  7.91 us (6%)
  other arithmetic  6.36 us (5%)
    all_to_all x3, starting transfers between devices, exchange(): return lax.all_to_all(value, axes, split_axis=0, concat_axis=0, tiled=True)  16.8 us
    ppermute x12, starting transfers between devices, shift_col(): return lax.ppermute(value, 'col', [(i, (i + k) % n) for i in range(n)])  14.5 us
    ppermute x8, starting transfers between devices, shift_depth(): return lax.ppermute(value, 'depth', [(i, (i + k) % n) for i in range(n)])  12.9 us
    ppermute x6, starting transfers between devices, shift_row(): return lax.ppermute(value, 'row', [(i, (i + 2 * k) % n) for i in range(n)])  10.9 us
    all_to_all x3, waiting for transfers between devices, exchange(): return lax.all_to_all(value, axes, split_axis=0, concat_axis=0, tiled=True)  9.99 us
    ppermute x8, waiting for transfers between devices, shift_depth(): return lax.ppermute(value, 'depth', [(i, (i + k) % n) for i in range(n)])  6.66 us
    ppermute x6, waiting for transfers between devices, shift_row(): return lax.ppermute(value, 'row', [(i, (i + 2 * k) % n) for i in range(n)])  6.44 us
    ppermute x12, waiting for transfers between devices, shift_col(): return lax.ppermute(value, 'col', [(i, (i + k) % n) for i in range(n)])  6.44 us
  transfers between devices with their start and end apart: 32, of which 11 were waited for; matrix products, arithmetic and copies ran while one was open for 16% of the time, Pallas kernels for 4%

profile of v5, /device:TPU:1, one launch (start us, length us, event | category | flops | bytes accessed | tf_op | source)
XLA Modules:
  0.0 126.2 jit_solution(2321301537143283991)
XLA Ops:
  0.6 3.8 %collective-permute-start = (bf16[32,1536]{1,0:T(8,128)(2,1)}, bf16[32,1536]{1,0:T(8,128)(2,1)S(1)}, u32[]{:S(2)}, u32[]{:S(2)}) collective-permute-start(bf16[32,1536]{1,0:T(8,128)(2,1)} %param.4), channel_id=1, source_target_pairs={{0,128},{32,160},{64,192},{96,224},{128,0},{160,32},{192,64},{224,... | collective-permute-start | bytes 294920 | tf_op jit(solution)/shard_map/ppermute | solution.py:34
  4.9 2.3 %collective-permute-start.2 = (bf16[32,1536]{1,0:T(8,128)(2,1)}, bf16[32,1536]{1,0:T(8,128)(2,1)S(1)}, u32[]{:S(2)}, u32[]{:S(2)}) collective-permute-start(bf16[32,1536]{1,0:T(8,128)(2,1)} %param.4), channel_id=1, source_target_pairs={{0,192},{32,224},{64,0},{96,32},{128,64},{160,96},{192,128},{224,1... | collective-permute-start | bytes 294920 | tf_op jit(solution)/shard_map/ppermute | solution.py:34
  7.1 4.2 %collective-permute-done.1 = bf16[32,1536]{1,0:T(8,128)(2,1)S(1)} collective-permute-done((bf16[32,1536]{1,0:T(8,128)(2,1)}, bf16[32,1536]{1,0:T(8,128)(2,1)S(1)}, u32[]{:S(2)}, u32[]{:S(2)}) %collective-permute-start.1) | collective-permute-done | bytes 98336 | tf_op jit(solution)/shard_map/ppermute | solution.py:34
  14.2 3.9 %collective-permute-start.10 = (bf16[4,32,1536]{2,1,0:T(8,128)(2,1)S(1)}, bf16[4,32,1536]{2,1,0:T(8,128)(2,1)S(1)}, u32[]{:S(2)}, u32[]{:S(2)}) collective-permute-start(bf16[4,32,1536]{2,1,0:T(8,128)(2,1)S(1)} %pad_maximum_fusion.1.refs_0_), channel_id=1, source_target_pairs={{0,7},{1,0},{2,1},{3,2},{4,3},{5,4},{6,5},{7,6},{8,15},{9,8},{10,9... | collective-permute-start | bytes 1179656 | tf_op jit(solution)/shard_map/ppermute | solution.py:49
  18.2 3.9 %fusion.7 = bf16[256,1536]{1,0:T(8,128)(2,1)S(1)} fusion(bf16[256,1536]{1,0:T(8,128)(2,1)S(1)} %bitcast.47, bf16[1536,3072]{1,0:T(8,128)(2,1)} %param.5), kind=kOutput, calls=%fused_computation.5 | convolution fusion | flops 1208352768 | bytes 6291456 | tf_op jit(solution)/shard_map/dot_general | solution.py:307
  24.7 2.6 %collective-permute-start.6 = (bf16[64,1536]{1,0:T(8,128)(2,1)S(1)}, bf16[64,1536]{1,0:T(8,128)(2,1)S(1)}, u32[]{:S(2)}, u32[]{:S(2)}) collective-permute-start(bf16[64,1536]{1,0:T(8,128)(2,1)S(1)} %get-tuple-element.62), channel_id=1, source_target_pairs={{0,24},{8,0},{16,8},{24,16},{1,25},{9,1},{17,9},{25,17},{2,26},{10... | collective-permute-start | bytes 589832 | tf_op jit(solution)/shard_map/ppermute | solution.py:44
  27.6 2.7 %collective-permute-start.11 = (bf16[4,32,1536]{2,1,0:T(8,128)(2,1)S(1)}, bf16[4,32,1536]{2,1,0:T(8,128)(2,1)}, u32[]{:S(2)}, u32[]{:S(2)}) collective-permute-start(bf16[4,32,1536]{2,1,0:T(8,128)(2,1)S(1)} %collective-permute-done.10.refs_8_), channel_id=1, source_target_pairs={{0,7},{1,0},{2,1},{3,2},{4,3},{5,4},{6,5},{7,6},{8,15},{9,8},{10,9... | collective-permute-start | bytes 1179656 | tf_op jit(solution)/shard_map/ppermute | solution.py:49
  31.1 3.5 %collective-permute-start.7 = (bf16[64,3072]{1,0:T(8,128)(2,1)S(1)}, bf16[64,3072]{1,0:T(8,128)(2,1)S(1)}, u32[]{:S(2)}, u32[]{:S(2)}) collective-permute-start(bf16[64,3072]{1,0:T(8,128)(2,1)S(1)} %pad_maximum_fusion.3), channel_id=1, source_target_pairs={{0,24},{8,0},{16,8},{24,16},{1,25},{9,1},{17,9},{25,17},{2,26},{10... | collective-permute-start | bytes 1179656 | tf_op jit(solution)/shard_map/ppermute | solution.py:44
  34.9 3.9 %collective-permute-done.9.refs_2_ = bf16[4,32,1536]{2,1,0:T(8,128)(2,1)} collective-permute-done((bf16[4,32,1536]{2,1,0:T(8,128)(2,1)S(1)}, bf16[4,32,1536]{2,1,0:T(8,128)(2,1)}, u32[]{:S(2)}, u32[]{:S(2)}) %collective-permute-start.9) | collective-permute-done | bytes 393248 | tf_op jit(solution)/shard_map/ppermute | solution.py:49
  38.8 2.7 %collective-permute-start.13 = (bf16[4,32,1536]{2,1,0:T(8,128)(2,1)}, bf16[4,32,1536]{2,1,0:T(8,128)(2,1)S(1)}, u32[]{:S(2)}, u32[]{:S(2)}) collective-permute-start(bf16[4,32,1536]{2,1,0:T(8,128)(2,1)} %collective-permute-done.11.refs_7_), channel_id=1, source_target_pairs={{0,7},{1,0},{2,1},{3,2},{4,3},{5,4},{6,5},{7,6},{8,15},{9,8},{10,9... | collective-permute-start | bytes 1179656 | tf_op jit(solution)/shard_map/ppermute | solution.py:49
  41.7 3.3 %collective-permute-done.5 = bf16[64,3072]{1,0:T(8,128)(2,1)S(1)} collective-permute-done((bf16[64,3072]{1,0:T(8,128)(2,1)S(1)}, bf16[64,3072]{1,0:T(8,128)(2,1)S(1)}, u32[]{:S(2)}, u32[]{:S(2)}) %collective-permute-start.5) | collective-permute-done | bytes 393248 | tf_op jit(solution)/shard_map/ppermute | solution.py:44
  46.6 4.9 %all-to-all-start = ((bf16[8,64,384]{2,1,0:T(8,128)(2,1)}), bf16[8,64,384]{2,1,0:T(8,128)(2,1)S(1)}, u32[]{:S(2)}, u32[]{:S(2)}) async-start(bf16[8,64,384]{2,1,0:T(8,128)(2,1)} %bitcast.43), calls=%async_computation | async-start | bytes 786432 | tf_op jit(solution)/shard_map/all_to_all | solution.py:274
  51.7 2.7 %collective-permute-start.15 = (bf16[64,3072]{1,0:T(8,128)(2,1)S(1)}, bf16[64,3072]{1,0:T(8,128)(2,1)S(1)}, u32[]{:S(2)}, u32[]{:S(2)}) collective-permute-start(bf16[64,3072]{1,0:T(8,128)(2,1)S(1)} %get-tuple-element.30), channel_id=1, source_target_pairs={{0,24},{8,0},{16,8},{24,16},{1,25},{9,1},{17,9},{25,17},{2,26},{10... | collective-permute-start | bytes 1179656 | tf_op jit(solution)/shard_map/ppermute | solution.py:44
  61.4 2.5 %collective-permute-start.19 = (bf16[32,3072]{1,0:T(8,128)(2,1)}, bf16[32,3072]{1,0:T(8,128)(2,1)}, u32[]{:S(2)}, u32[]{:S(2)}) collective-permute-start(bf16[32,3072]{1,0:T(8,128)(2,1)} %slice.126), channel_id=1, source_target_pairs={{0,24},{8,0},{16,8},{24,16},{1,25},{9,1},{17,9},{25,17},{2,26},{10... | collective-permute-start | bytes 589832 | tf_op jit(solution)/shard_map/ppermute | solution.py:44
  64.0 2.5 %collective-permute-done.23.refs_4_ = bf16[2,32,1536]{2,1,0:T(8,128)(2,1)S(1)} collective-permute-done((bf16[2,32,1536]{2,1,0:T(8,128)(2,1)}, bf16[2,32,1536]{2,1,0:T(8,128)(2,1)S(1)}, u32[]{:S(2)}, u32[]{:S(2)}) %collective-permute-start.23) | collective-permute-done | bytes 196640 | tf_op jit(solution)/shard_map/ppermute | solution.py:49
  67.9 2.8 %stack_up.1.refs_1_.refs_3_.refs_5_.refs_2_ = bf16[8,4,32,1536]{3,2,1,0:T(8,128)(2,1)} custom-call(bf16[4,32,1536]{2,1,0:T(8,128)(2,1)} %copy-done.1, bf16[4,32,1536]{2,1,0:T(8,128)(2,1)} %copy-done.5, bf16[4,32,1536]{2,1,0:T(8,128)(2,1)} %collective-permute-done.9.refs_2_, bf16[4,32,1536]{2,1,0:T(8,128)(2,1)} %copy-done.3, bf16[2,32,1536]{2,1,0:T(8,128)(2,1)} %copy-done.7, ...), custom_call_target="tpu_custom_call" | custom-call | bytes 6291456 | tf_op jit(solution)/shard_map/stack_up/pallas_call | solution.py:94
  70.6 5.3 %collective-permute-start.25 = (bf16[8,4,32,1536]{3,2,1,0:T(8,128)(2,1)}, bf16[8,4,32,1536]{3,2,1,0:T(8,128)(2,1)S(1)}, u32[]{:S(2)}, u32[]{:S(2)}) collective-permute-start(bf16[8,4,32,1536]{3,2,1,0:T(8,128)(2,1)} %stack_up.1.refs_1_.refs_3_.refs_5_.refs_2_), channel_id=1, source_target_pairs={{0,32},{32,0},{64,96},{96,64},{128,160},{160,128},{192,224},{224,1... | collective-permute-start | bytes 9437192 | tf_op jit(solution)/shard_map/ppermute | solution.py:39
  77.0 5.2 %fusion.29 = f32[256,1536]{1,0:T(8,128)S(1)} fusion(bf16[256,3072]{1,0:T(8,128)(2,1)S(1)} %constant_dynamic-update-slice_fusion, bf16[1536,3072]{1,0:T(8,128)(2,1)} %param.5), kind=kOutput, calls=%fused_computation.55 | convolution fusion | flops 2415919104 | bytes 12582912 | tf_op jit(solution)/shard_map/dot_general | solution.py:337
  83.3 2.7 %collective-permute-start.22 = (bf16[4,64,384]{2,1,0:T(8,128)(2,1)S(1)}, bf16[4,64,384]{2,1,0:T(8,128)(2,1)S(1)}, u32[]{:S(2)}, u32[]{:S(2)}) collective-permute-start(bf16[4,64,384]{2,1,0:T(8,128)(2,1)S(1)} %slice.108), channel_id=1, source_target_pairs={{0,24},{8,0},{16,8},{24,16},{1,25},{9,1},{17,9},{25,17},{2,26},{10... | collective-permute-start | bytes 589832 | tf_op jit(solution)/shard_map/ppermute | solution.py:44
  87.1 2.5 %collective-permute-start.27 = (bf16[32,1536]{1,0:T(8,128)(2,1)S(1)}, bf16[32,1536]{1,0:T(8,128)(2,1)S(1)}, u32[]{:S(2)}, u32[]{:S(2)}) collective-permute-start(bf16[32,1536]{1,0:T(8,128)(2,1)S(1)} %get-tuple-element.56), channel_id=1, source_target_pairs={{0,192},{32,224},{64,0},{96,32},{128,64},{160,96},{192,128},{224,1... | collective-permute-start | bytes 294920 | tf_op jit(solution)/shard_map/ppermute | solution.py:34
  97.4 5.9 %all-to-all-start.1 = ((f32[32,1,128]{2,1,0:T(1,128)}), f32[32,1,128]{2,1,0:T(1,128)}, u32[]{:S(2)}, u32[]{:S(2)}) async-start(f32[32,1,128]{2,1,0:T(1,128)} %get-tuple-element.47), calls=%async_computation.1 | async-start | bytes 32768 | tf_op jit(solution)/shard_map/all_to_all | solution.py:274
  105.1 5.2 %all-to-all-done.1 = f32[32,1,128]{2,1,0:T(1,128)} async-done(((f32[32,1,128]{2,1,0:T(1,128)}), f32[32,1,128]{2,1,0:T(1,128)}, u32[]{:S(2)}, u32[]{:S(2)}) %all-to-all-start.1) | async-done | bytes 16416 | tf_op jit(solution)/shard_map/all_to_all | solution.py:274
  111.7 6.0 %all-to-all-start.2 = ((f32[8,1,128]{2,1,0:T(1,128)}), f32[8,1,128]{2,1,0:T(1,128)S(1)}, u32[]{:S(2)}, u32[]{:S(2)}) async-start(f32[8,1,128]{2,1,0:T(1,128)} %broadcast_in_dim.2), calls=%async_computation.2 | async-start | bytes 8192 | tf_op jit(solution)/shard_map/all_to_all | solution.py:274
  119.4 4.8 %all-to-all-done.2.p = f32[8,1,128]{2,1,0:T(1,128)S(1)} async-done(((f32[8,1,128]{2,1,0:T(1,128)}), f32[8,1,128]{2,1,0:T(1,128)S(1)}, u32[]{:S(2)}, u32[]{:S(2)}) %all-to-all-start.2) | async-done | bytes 4128 | tf_op jit(solution)/shard_map/all_to_all | solution.py:274
  (107 shorter events, 35.3 us)
Async XLA Ops:
  4.5 6.9 %collective-permute-start.1 = (bf16[32,1536]{1,0:T(8,128)(2,1)}, bf16[32,1536]{1,0:T(8,128)(2,1)S(1)}, u32[]{:S(2)}, u32[]{:S(2)}) collective-permute-start(bf16[32,1536]{1,0:T(8,128)(2,1)} %param.4), channel_id=1, source_target_pairs={{0,64},{32,96},{64,128},{96,160},{128,192},{160,224},{192,0},{224,... | collective-permute-start | bytes 294920 | tf_op jit(solution)/shard_map/ppermute | solution.py:34
  13.3 14.3 %collective-permute-start.8 = (bf16[4,32,1536]{2,1,0:T(8,128)(2,1)S(1)}, bf16[4,32,1536]{2,1,0:T(8,128)(2,1)S(1)}, u32[]{:S(2)}, u32[]{:S(2)}) collective-permute-start(bf16[4,32,1536]{2,1,0:T(8,128)(2,1)S(1)} %pad_maximum_fusion.1.refs_0_), channel_id=1, source_target_pairs={{0,1},{1,2},{2,3},{3,4},{4,5},{5,6},{6,7},{7,0},{8,9},{9,10},{10,1... | collective-permute-start | bytes 1179656 | tf_op jit(solution)/shard_map/ppermute | solution.py:49
  14.2 13.3 %collective-permute-start.10 = (bf16[4,32,1536]{2,1,0:T(8,128)(2,1)S(1)}, bf16[4,32,1536]{2,1,0:T(8,128)(2,1)S(1)}, u32[]{:S(2)}, u32[]{:S(2)}) collective-permute-start(bf16[4,32,1536]{2,1,0:T(8,128)(2,1)S(1)} %pad_maximum_fusion.1.refs_0_), channel_id=1, source_target_pairs={{0,7},{1,0},{2,1},{3,2},{4,3},{5,4},{6,5},{7,6},{8,15},{9,8},{10,9... | collective-permute-start | bytes 1179656 | tf_op jit(solution)/shard_map/ppermute | solution.py:49
  27.3 7.3 %collective-permute-start.4 = (bf16[64,1536]{1,0:T(8,128)(2,1)S(1)}, bf16[64,1536]{1,0:T(8,128)(2,1)S(1)}, u32[]{:S(2)}, u32[]{:S(2)}) collective-permute-start(bf16[64,1536]{1,0:T(8,128)(2,1)S(1)} %get-tuple-element.61), channel_id=1, source_target_pairs={{0,8},{8,16},{16,24},{24,0},{1,9},{9,17},{17,25},{25,1},{2,10},{10... | collective-permute-start | bytes 589832 | tf_op jit(solution)/shard_map/ppermute | solution.py:44
  27.5 11.3 %collective-permute-start.9 = (bf16[4,32,1536]{2,1,0:T(8,128)(2,1)S(1)}, bf16[4,32,1536]{2,1,0:T(8,128)(2,1)}, u32[]{:S(2)}, u32[]{:S(2)}) collective-permute-start(bf16[4,32,1536]{2,1,0:T(8,128)(2,1)S(1)} %collective-permute-done.8.refs_1_), channel_id=1, source_target_pairs={{0,1},{1,2},{2,3},{3,4},{4,5},{5,6},{6,7},{7,0},{8,9},{9,10},{10,1... | collective-permute-start | bytes 1179656 | tf_op jit(solution)/shard_map/ppermute | solution.py:49
  27.6 11.3 %collective-permute-start.11 = (bf16[4,32,1536]{2,1,0:T(8,128)(2,1)S(1)}, bf16[4,32,1536]{2,1,0:T(8,128)(2,1)}, u32[]{:S(2)}, u32[]{:S(2)}) collective-permute-start(bf16[4,32,1536]{2,1,0:T(8,128)(2,1)S(1)} %collective-permute-done.10.refs_8_), channel_id=1, source_target_pairs={{0,7},{1,0},{2,1},{3,2},{4,3},{5,4},{6,5},{7,6},{8,15},{9,8},{10,9... | collective-permute-start | bytes 1179656 | tf_op jit(solution)/shard_map/ppermute | solution.py:49
  31.1 10.6 %collective-permute-start.7 = (bf16[64,3072]{1,0:T(8,128)(2,1)S(1)}, bf16[64,3072]{1,0:T(8,128)(2,1)S(1)}, u32[]{:S(2)}, u32[]{:S(2)}) collective-permute-start(bf16[64,3072]{1,0:T(8,128)(2,1)S(1)} %pad_maximum_fusion.3), channel_id=1, source_target_pairs={{0,24},{8,0},{16,8},{24,16},{1,25},{9,1},{17,9},{25,17},{2,26},{10... | collective-permute-start | bytes 1179656 | tf_op jit(solution)/shard_map/ppermute | solution.py:44
  34.7 10.3 %collective-permute-start.5 = (bf16[64,3072]{1,0:T(8,128)(2,1)S(1)}, bf16[64,3072]{1,0:T(8,128)(2,1)S(1)}, u32[]{:S(2)}, u32[]{:S(2)}) collective-permute-start(bf16[64,3072]{1,0:T(8,128)(2,1)S(1)} %pad_maximum_fusion.2), channel_id=1, source_target_pairs={{0,8},{8,16},{16,24},{24,0},{1,9},{9,17},{17,25},{25,1},{2,10},{10... | collective-permute-start | bytes 1179656 | tf_op jit(solution)/shard_map/ppermute | solution.py:44
  38.8 12.7 %collective-permute-start.12 = (bf16[4,32,1536]{2,1,0:T(8,128)(2,1)}, bf16[4,32,1536]{2,1,0:T(8,128)(2,1)S(1)}, u32[]{:S(2)}, u32[]{:S(2)}) collective-permute-start(bf16[4,32,1536]{2,1,0:T(8,128)(2,1)} %collective-permute-done.9.refs_2_), channel_id=1, source_target_pairs={{0,1},{1,2},{2,3},{3,4},{4,5},{5,6},{6,7},{7,0},{8,9},{9,10},{10,1... | collective-permute-start | bytes 1179656 | tf_op jit(solution)/shard_map/ppermute | solution.py:49
  38.8 12.7 %collective-permute-start.13 = (bf16[4,32,1536]{2,1,0:T(8,128)(2,1)}, bf16[4,32,1536]{2,1,0:T(8,128)(2,1)S(1)}, u32[]{:S(2)}, u32[]{:S(2)}) collective-permute-start(bf16[4,32,1536]{2,1,0:T(8,128)(2,1)} %collective-permute-done.11.refs_7_), channel_id=1, source_target_pairs={{0,7},{1,0},{2,1},{3,2},{4,3},{5,4},{6,5},{7,6},{8,15},{9,8},{10,9... | collective-permute-start | bytes 1179656 | tf_op jit(solution)/shard_map/ppermute | solution.py:49
  46.6 17.4 %all-to-all-start = ((bf16[8,64,384]{2,1,0:T(8,128)(2,1)}), bf16[8,64,384]{2,1,0:T(8,128)(2,1)S(1)}, u32[]{:S(2)}, u32[]{:S(2)}) async-start(bf16[8,64,384]{2,1,0:T(8,128)(2,1)} %bitcast.43), calls=%async_computation | async-start | bytes 786432 | tf_op jit(solution)/shard_map/all_to_all | solution.py:274
  51.6 8.9 %collective-permute-start.14 = (bf16[64,3072]{1,0:T(8,128)(2,1)S(1)}, bf16[64,3072]{1,0:T(8,128)(2,1)S(1)}, u32[]{:S(2)}, u32[]{:S(2)}) collective-permute-start(bf16[64,3072]{1,0:T(8,128)(2,1)S(1)} %get-tuple-element.30), channel_id=1, source_target_pairs={{0,8},{8,16},{16,24},{24,0},{1,9},{9,17},{17,25},{25,1},{2,10},{10... | collective-permute-start | bytes 1179656 | tf_op jit(solution)/shard_map/ppermute | solution.py:44
  51.7 9.0 %collective-permute-start.15 = (bf16[64,3072]{1,0:T(8,128)(2,1)S(1)}, bf16[64,3072]{1,0:T(8,128)(2,1)S(1)}, u32[]{:S(2)}, u32[]{:S(2)}) collective-permute-start(bf16[64,3072]{1,0:T(8,128)(2,1)S(1)} %get-tuple-element.30), channel_id=1, source_target_pairs={{0,24},{8,0},{16,8},{24,16},{1,25},{9,1},{17,9},{25,17},{2,26},{10... | collective-permute-start | bytes 1179656 | tf_op jit(solution)/shard_map/ppermute | solution.py:44
  55.0 11.5 %collective-permute-start.23 = (bf16[2,32,1536]{2,1,0:T(8,128)(2,1)}, bf16[2,32,1536]{2,1,0:T(8,128)(2,1)S(1)}, u32[]{:S(2)}, u32[]{:S(2)}) collective-permute-start(bf16[2,32,1536]{2,1,0:T(8,128)(2,1)} %slice.129), channel_id=1, source_target_pairs={{0,1},{1,2},{2,3},{3,4},{4,5},{5,6},{6,7},{7,0},{8,9},{9,10},{10,1... | collective-permute-start | bytes 589832 | tf_op jit(solution)/shard_map/ppermute | solution.py:49
  57.2 9.5 %collective-permute-start.24 = (bf16[2,32,1536]{2,1,0:T(8,128)(2,1)}, bf16[2,32,1536]{2,1,0:T(8,128)(2,1)S(1)}, u32[]{:S(2)}, u32[]{:S(2)}) collective-permute-start(bf16[2,32,1536]{2,1,0:T(8,128)(2,1)} %slice.130), channel_id=1, source_target_pairs={{0,7},{1,0},{2,1},{3,2},{4,3},{5,4},{6,5},{7,6},{8,15},{9,8},{10,9... | collective-permute-start | bytes 589832 | tf_op jit(solution)/shard_map/ppermute | solution.py:49
  60.5 15.4 %collective-permute-start.18 = (bf16[32,3072]{1,0:T(8,128)(2,1)S(1)}, bf16[32,3072]{1,0:T(8,128)(2,1)S(1)}, u32[]{:S(2)}, u32[]{:S(2)}) collective-permute-start(bf16[32,3072]{1,0:T(8,128)(2,1)S(1)} %slice.125), channel_id=1, source_target_pairs={{0,8},{8,16},{16,24},{24,0},{1,9},{9,17},{17,25},{25,1},{2,10},{10... | collective-permute-start | bytes 589832 | tf_op jit(solution)/shard_map/ppermute | solution.py:44
  61.4 14.5 %collective-permute-start.19 = (bf16[32,3072]{1,0:T(8,128)(2,1)}, bf16[32,3072]{1,0:T(8,128)(2,1)}, u32[]{:S(2)}, u32[]{:S(2)}) collective-permute-start(bf16[32,3072]{1,0:T(8,128)(2,1)} %slice.126), channel_id=1, source_target_pairs={{0,24},{8,0},{16,8},{24,16},{1,25},{9,1},{17,9},{25,17},{2,26},{10... | collective-permute-start | bytes 589832 | tf_op jit(solution)/shard_map/ppermute | solution.py:44
  64.0 18.3 %collective-permute-start.16 = (bf16[8,64,384]{2,1,0:T(8,128)(2,1)S(1)}, bf16[8,64,384]{2,1,0:T(8,128)(2,1)S(1)}, u32[]{:S(2)}, u32[]{:S(2)}) collective-permute-start(bf16[8,64,384]{2,1,0:T(8,128)(2,1)S(1)} %all-to-all-done.refs_7_), channel_id=1, source_target_pairs={{0,8},{8,16},{16,24},{24,0},{1,9},{9,17},{17,25},{25,1},{2,10},{10... | collective-permute-start | bytes 1179656 | tf_op jit(solution)/shard_map/ppermute | solution.py:44
  66.5 15.7 %collective-permute-start.17 = (bf16[8,64,384]{2,1,0:T(8,128)(2,1)S(1)}, bf16[8,64,384]{2,1,0:T(8,128)(2,1)S(1)}, u32[]{:S(2)}, u32[]{:S(2)}) collective-permute-start(bf16[8,64,384]{2,1,0:T(8,128)(2,1)S(1)} %all-to-all-done.refs_7_), channel_id=1, source_target_pairs={{0,24},{8,0},{16,8},{24,16},{1,25},{9,1},{17,9},{25,17},{2,26},{10... | collective-permute-start | bytes 1179656 | tf_op jit(solution)/shard_map/ppermute | solution.py:44
  70.6 18.9 %collective-permute-start.25 = (bf16[8,4,32,1536]{3,2,1,0:T(8,128)(2,1)}, bf16[8,4,32,1536]{3,2,1,0:T(8,128)(2,1)S(1)}, u32[]{:S(2)}, u32[]{:S(2)}) collective-permute-start(bf16[8,4,32,1536]{3,2,1,0:T(8,128)(2,1)} %stack_up.1.refs_1_.refs_3_.refs_5_.refs_2_), channel_id=1, source_target_pairs={{0,32},{32,0},{64,96},{96,64},{128,160},{160,128},{192,224},{224,1... | collective-permute-start | bytes 9437192 | tf_op jit(solution)/shard_map/ppermute | solution.py:39
  83.2 9.7 %collective-permute-start.21 = (bf16[4,64,384]{2,1,0:T(8,128)(2,1)S(1)}, bf16[4,64,384]{2,1,0:T(8,128)(2,1)S(1)}, u32[]{:S(2)}, u32[]{:S(2)}) collective-permute-start(bf16[4,64,384]{2,1,0:T(8,128)(2,1)S(1)} %slice.107), channel_id=1, source_target_pairs={{0,8},{8,16},{16,24},{24,0},{1,9},{9,17},{17,25},{25,1},{2,10},{10... | collective-permute-start | bytes 589832 | tf_op jit(solution)/shard_map/ppermute | solution.py:44
  83.3 9.5 %collective-permute-start.22 = (bf16[4,64,384]{2,1,0:T(8,128)(2,1)S(1)}, bf16[4,64,384]{2,1,0:T(8,128)(2,1)S(1)}, u32[]{:S(2)}, u32[]{:S(2)}) collective-permute-start(bf16[4,64,384]{2,1,0:T(8,128)(2,1)S(1)} %slice.108), channel_id=1, source_target_pairs={{0,24},{8,0},{16,8},{24,16},{1,25},{9,1},{17,9},{25,17},{2,26},{10... | collective-permute-start | bytes 589832 | tf_op jit(solution)/shard_map/ppermute | solution.py:44
  97.4 13.0 %all-to-all-start.1 = ((f32[32,1,128]{2,1,0:T(1,128)}), f32[32,1,128]{2,1,0:T(1,128)}, u32[]{:S(2)}, u32[]{:S(2)}) async-start(f32[32,1,128]{2,1,0:T(1,128)} %get-tuple-element.47), calls=%async_computation.1 | async-start | bytes 32768 | tf_op jit(solution)/shard_map/all_to_all | solution.py:274
  111.7 12.4 %all-to-all-start.2 = ((f32[8,1,128]{2,1,0:T(1,128)}), f32[8,1,128]{2,1,0:T(1,128)S(1)}, u32[]{:S(2)}, u32[]{:S(2)}) async-start(f32[8,1,128]{2,1,0:T(1,128)} %broadcast_in_dim.2), calls=%async_computation.2 | async-start | bytes 8192 | tf_op jit(solution)/shard_map/all_to_all | solution.py:274
  (22 other events, 144.6 us)

commit v6 on v5

--- a/solution.py
+++ b/solution.py
@@ -291,7 +291,8 @@
     def own_first(v):
         return jnp.where(core == 0, v, jnp.concatenate([v[tok:], v[:tok]], axis=0))
 
-    got = [tokens] + [shift_row(tokens, k) for k in (1, 2, 3)]
+    far = shift_row(tokens, 2)
+    got = [tokens, shift_row(tokens, 1), far, shift_row(tokens, 3)]
     mine = jnp.stack([choose(got, (y - col - k) % 4) for k in REL])
     other = swap_core(mine)
     slice_x = jnp.concatenate([mine, other], axis=1).reshape(n_col * share, feat)
@@ -322,7 +323,7 @@
     b3 = shift_col(later, 3)
     b2 = shift_col(b1[:tok], 1)
     b4 = shift_col(b3[tok:], 3)
-    columns = exchange(after(grad_share, up2, dn2).reshape(share, n_depth, block_ff).transpose(1, 0, 2), "depth")
+    columns = exchange(grad_share.reshape(share, n_depth, block_ff).transpose(1, 0, 2), "depth")
 
     columns, b1, b3 = lax.optimization_barrier((columns, b1, b3))
     t_mine = stack_up([after(mine, columns), up1, up2, up3, up4, dn4, dn3, dn2, dn1])
@@ -353,7 +354,7 @@
         d = (y + k - col) % 4
         return jnp.where(d == 2, 0, jnp.where(d == 1, 1, jnp.where(d == 3, 2, 3)))
 
-    came = [shift_row(pick(chip, rel_pos(k)).astype(BF), k) for k in (1, 3, 2)]
+    came = [shift_row(pick(chip, rel_pos(k)).astype(BF), k) for k in (2, 1, 3)]
     a3, d3, acc, came = lax.optimization_barrier((a3, d3, acc, came))
     first_col = (col == 0).astype(F32).reshape(1)
     raw, raw_bias, squares = grad_step(

time: 127 us -> 126 us (level)
  transfers between devices with their start and end apart: 32 -> 32, of which waited for: 11 -> 12; matrix products, arithmetic and copies ran while one was open for 16% -> 16% of each run, Pallas kernels for 4% -> 4%
where the time goes in v6:
time: 126 us
  starting transfers between devices  61 us (48%)
  waiting for transfers between devices  29.4 us (23%)
  matrix products  10.5 us (8%)
  Pallas kernels  9.2 us (7%)
  local copies, waits for them, and re-layouts  7.91 us (6%)
  other arithmetic  6.36 us (5%)
    all_to_all x3, starting transfers between devices, exchange(): return lax.all_to_all(value, axes, split_axis=0, concat_axis=0, tiled=True)  16.5 us
    ppermute x12, starting transfers between devices, shift_col(): return lax.ppermute(value, 'col', [(i, (i + k) % n) for i in range(n)])  14.5 us
    ppermute x8, starting transfers between devices, shift_depth(): return lax.ppermute(value, 'depth', [(i, (i + k) % n) for i in range(n)])  12.9 us
    ppermute x6, starting transfers between devices, shift_row(): return lax.ppermute(value, 'row', [(i, (i + 2 * k) % n) for i in range(n)])  10.8 us
    all_to_all x3, waiting for transfers between devices, exchange(): return lax.all_to_all(value, axes, split_axis=0, concat_axis=0, tiled=True)  9.99 us
    ppermute x8, waiting for transfers between devices, shift_depth(): return lax.ppermute(value, 'depth', [(i, (i + k) % n) for i in range(n)])  6.66 us
    ppermute x12, waiting for transfers between devices, shift_col(): return lax.ppermute(value, 'col', [(i, (i + k) % n) for i in range(n)])  6.44 us
    ppermute x3, starting transfers between devices, swap_core(): return lax.ppermute(value, 'row', [(i, i ^ 1) for i in range(n)])  6.32 us
  transfers between devices with their start and end apart: 32, of which 12 were waited for; matrix products, arithmetic and copies ran while one was open for 16% of the time, Pallas kernels for 4%

profile of v6, /device:TPU:1, one launch (start us, length us, event | category | flops | bytes accessed | tf_op | source)
XLA Modules:
  0.0 125.5 jit_solution(29403486643685595)
XLA Ops:
  0.6 3.8 %collective-permute-start = (bf16[32,1536]{1,0:T(8,128)(2,1)}, bf16[32,1536]{1,0:T(8,128)(2,1)S(1)}, u32[]{:S(2)}, u32[]{:S(2)}) collective-permute-start(bf16[32,1536]{1,0:T(8,128)(2,1)} %param.4), channel_id=1, source_target_pairs={{0,128},{32,160},{64,192},{96,224},{128,0},{160,32},{192,64},{224,... | collective-permute-start | bytes 294920 | tf_op jit(solution)/shard_map/ppermute | solution.py:34
  4.9 2.3 %collective-permute-start.2 = (bf16[32,1536]{1,0:T(8,128)(2,1)}, bf16[32,1536]{1,0:T(8,128)(2,1)S(1)}, u32[]{:S(2)}, u32[]{:S(2)}) collective-permute-start(bf16[32,1536]{1,0:T(8,128)(2,1)} %param.4), channel_id=1, source_target_pairs={{0,192},{32,224},{64,0},{96,32},{128,64},{160,96},{192,128},{224,1... | collective-permute-start | bytes 294920 | tf_op jit(solution)/shard_map/ppermute | solution.py:34
  7.1 4.2 %collective-permute-done.1 = bf16[32,1536]{1,0:T(8,128)(2,1)S(1)} collective-permute-done((bf16[32,1536]{1,0:T(8,128)(2,1)}, bf16[32,1536]{1,0:T(8,128)(2,1)S(1)}, u32[]{:S(2)}, u32[]{:S(2)}) %collective-permute-start.1) | collective-permute-done | bytes 98336 | tf_op jit(solution)/shard_map/ppermute | solution.py:34
  14.2 3.9 %collective-permute-start.11 = (bf16[4,32,1536]{2,1,0:T(8,128)(2,1)S(1)}, bf16[4,32,1536]{2,1,0:T(8,128)(2,1)S(1)}, u32[]{:S(2)}, u32[]{:S(2)}) collective-permute-start(bf16[4,32,1536]{2,1,0:T(8,128)(2,1)S(1)} %pad_maximum_fusion.1.refs_0_), channel_id=1, source_target_pairs={{0,7},{1,0},{2,1},{3,2},{4,3},{5,4},{6,5},{7,6},{8,15},{9,8},{10,9... | collective-permute-start | bytes 1179656 | tf_op jit(solution)/shard_map/ppermute | solution.py:49
  18.2 3.9 %fusion.7 = bf16[256,1536]{1,0:T(8,128)(2,1)S(1)} fusion(bf16[256,1536]{1,0:T(8,128)(2,1)S(1)} %bitcast.47, bf16[1536,3072]{1,0:T(8,128)(2,1)} %param.5), kind=kOutput, calls=%fused_computation.5 | convolution fusion | flops 1208352768 | bytes 6291456 | tf_op jit(solution)/shard_map/dot_general | solution.py:308
  24.7 2.6 %collective-permute-start.6 = (bf16[64,1536]{1,0:T(8,128)(2,1)S(1)}, bf16[64,1536]{1,0:T(8,128)(2,1)S(1)}, u32[]{:S(2)}, u32[]{:S(2)}) collective-permute-start(bf16[64,1536]{1,0:T(8,128)(2,1)S(1)} %get-tuple-element.60), channel_id=1, source_target_pairs={{0,24},{8,0},{16,8},{24,16},{1,25},{9,1},{17,9},{25,17},{2,26},{10... | collective-permute-start | bytes 589832 | tf_op jit(solution)/shard_map/ppermute | solution.py:44
  27.6 2.7 %collective-permute-start.12 = (bf16[4,32,1536]{2,1,0:T(8,128)(2,1)S(1)}, bf16[4,32,1536]{2,1,0:T(8,128)(2,1)}, u32[]{:S(2)}, u32[]{:S(2)}) collective-permute-start(bf16[4,32,1536]{2,1,0:T(8,128)(2,1)S(1)} %collective-permute-done.11.refs_8_), channel_id=1, source_target_pairs={{0,7},{1,0},{2,1},{3,2},{4,3},{5,4},{6,5},{7,6},{8,15},{9,8},{10,9... | collective-permute-start | bytes 1179656 | tf_op jit(solution)/shard_map/ppermute | solution.py:49
  31.1 3.5 %collective-permute-start.7 = (bf16[64,3072]{1,0:T(8,128)(2,1)S(1)}, bf16[64,3072]{1,0:T(8,128)(2,1)S(1)}, u32[]{:S(2)}, u32[]{:S(2)}) collective-permute-start(bf16[64,3072]{1,0:T(8,128)(2,1)S(1)} %pad_maximum_fusion.3), channel_id=1, source_target_pairs={{0,24},{8,0},{16,8},{24,16},{1,25},{9,1},{17,9},{25,17},{2,26},{10... | collective-permute-start | bytes 1179656 | tf_op jit(solution)/shard_map/ppermute | solution.py:44
  34.9 3.9 %collective-permute-done.9.refs_2_ = bf16[4,32,1536]{2,1,0:T(8,128)(2,1)} collective-permute-done((bf16[4,32,1536]{2,1,0:T(8,128)(2,1)S(1)}, bf16[4,32,1536]{2,1,0:T(8,128)(2,1)}, u32[]{:S(2)}, u32[]{:S(2)}) %collective-permute-start.9) | collective-permute-done | bytes 393248 | tf_op jit(solution)/shard_map/ppermute | solution.py:49
  38.8 2.7 %collective-permute-start.13 = (bf16[4,32,1536]{2,1,0:T(8,128)(2,1)}, bf16[4,32,1536]{2,1,0:T(8,128)(2,1)S(1)}, u32[]{:S(2)}, u32[]{:S(2)}) collective-permute-start(bf16[4,32,1536]{2,1,0:T(8,128)(2,1)} %collective-permute-done.12.refs_7_), channel_id=1, source_target_pairs={{0,7},{1,0},{2,1},{3,2},{4,3},{5,4},{6,5},{7,6},{8,15},{9,8},{10,9... | collective-permute-start | bytes 1179656 | tf_op jit(solution)/shard_map/ppermute | solution.py:49
  41.7 3.3 %collective-permute-done.5 = bf16[64,3072]{1,0:T(8,128)(2,1)S(1)} collective-permute-done((bf16[64,3072]{1,0:T(8,128)(2,1)S(1)}, bf16[64,3072]{1,0:T(8,128)(2,1)S(1)}, u32[]{:S(2)}, u32[]{:S(2)}) %collective-permute-start.5) | collective-permute-done | bytes 393248 | tf_op jit(solution)/shard_map/ppermute | solution.py:44
  46.6 4.9 %all-to-all-start = ((bf16[8,64,384]{2,1,0:T(8,128)(2,1)}), bf16[8,64,384]{2,1,0:T(8,128)(2,1)S(1)}, u32[]{:S(2)}, u32[]{:S(2)}) async-start(bf16[8,64,384]{2,1,0:T(8,128)(2,1)} %bitcast.43), calls=%async_computation | async-start | bytes 786432 | tf_op jit(solution)/shard_map/all_to_all | solution.py:274
  51.7 2.7 %collective-permute-start.15 = (bf16[64,3072]{1,0:T(8,128)(2,1)S(1)}, bf16[64,3072]{1,0:T(8,128)(2,1)S(1)}, u32[]{:S(2)}, u32[]{:S(2)}) collective-permute-start(bf16[64,3072]{1,0:T(8,128)(2,1)S(1)} %get-tuple-element.28), channel_id=1, source_target_pairs={{0,24},{8,0},{16,8},{24,16},{1,25},{9,1},{17,9},{25,17},{2,26},{10... | collective-permute-start | bytes 1179656 | tf_op jit(solution)/shard_map/ppermute | solution.py:44
  61.4 2.5 %collective-permute-start.19 = (bf16[32,3072]{1,0:T(8,128)(2,1)}, bf16[32,3072]{1,0:T(8,128)(2,1)}, u32[]{:S(2)}, u32[]{:S(2)}) collective-permute-start(bf16[32,3072]{1,0:T(8,128)(2,1)} %slice.126), channel_id=1, source_target_pairs={{0,24},{8,0},{16,8},{24,16},{1,25},{9,1},{17,9},{25,17},{2,26},{10... | collective-permute-start | bytes 589832 | tf_op jit(solution)/shard_map/ppermute | solution.py:44
  64.0 2.5 %collective-permute-done.23.refs_4_ = bf16[2,32,1536]{2,1,0:T(8,128)(2,1)S(1)} collective-permute-done((bf16[2,32,1536]{2,1,0:T(8,128)(2,1)}, bf16[2,32,1536]{2,1,0:T(8,128)(2,1)S(1)}, u32[]{:S(2)}, u32[]{:S(2)}) %collective-permute-start.23) | collective-permute-done | bytes 196640 | tf_op jit(solution)/shard_map/ppermute | solution.py:49
  67.9 2.8 %stack_up.1.refs_1_.refs_3_.refs_5_.refs_2_ = bf16[8,4,32,1536]{3,2,1,0:T(8,128)(2,1)} custom-call(bf16[4,32,1536]{2,1,0:T(8,128)(2,1)} %copy-done.1, bf16[4,32,1536]{2,1,0:T(8,128)(2,1)} %copy-done.5, bf16[4,32,1536]{2,1,0:T(8,128)(2,1)} %collective-permute-done.9.refs_2_, bf16[4,32,1536]{2,1,0:T(8,128)(2,1)} %copy-done.3, bf16[2,32,1536]{2,1,0:T(8,128)(2,1)} %copy-done.7, ...), custom_call_target="tpu_custom_call" | custom-call | bytes 6291456 | tf_op jit(solution)/shard_map/stack_up/pallas_call | solution.py:94
  70.6 5.3 %collective-permute-start.25 = (bf16[8,4,32,1536]{3,2,1,0:T(8,128)(2,1)}, bf16[8,4,32,1536]{3,2,1,0:T(8,128)(2,1)S(1)}, u32[]{:S(2)}, u32[]{:S(2)}) collective-permute-start(bf16[8,4,32,1536]{3,2,1,0:T(8,128)(2,1)} %stack_up.1.refs_1_.refs_3_.refs_5_.refs_2_), channel_id=1, source_target_pairs={{0,32},{32,0},{64,96},{96,64},{128,160},{160,128},{192,224},{224,1... | collective-permute-start | bytes 9437192 | tf_op jit(solution)/shard_map/ppermute | solution.py:39
  77.0 5.2 %fusion.29 = f32[256,1536]{1,0:T(8,128)S(1)} fusion(bf16[256,3072]{1,0:T(8,128)(2,1)S(1)} %constant_dynamic-update-slice_fusion, bf16[1536,3072]{1,0:T(8,128)(2,1)} %param.5), kind=kOutput, calls=%fused_computation.55 | convolution fusion | flops 2415919104 | bytes 12582912 | tf_op jit(solution)/shard_map/dot_general | solution.py:338
  83.3 2.7 %collective-permute-start.22 = (bf16[4,64,384]{2,1,0:T(8,128)(2,1)S(1)}, bf16[4,64,384]{2,1,0:T(8,128)(2,1)S(1)}, u32[]{:S(2)}, u32[]{:S(2)}) collective-permute-start(bf16[4,64,384]{2,1,0:T(8,128)(2,1)S(1)} %slice.108), channel_id=1, source_target_pairs={{0,24},{8,0},{16,8},{24,16},{1,25},{9,1},{17,9},{25,17},{2,26},{10... | collective-permute-start | bytes 589832 | tf_op jit(solution)/shard_map/ppermute | solution.py:44
  87.8 2.2 %collective-permute-start.27 = (bf16[32,1536]{1,0:T(8,128)(2,1)S(1)}, bf16[32,1536]{1,0:T(8,128)(2,1)S(1)}, u32[]{:S(2)}, u32[]{:S(2)}) collective-permute-start(bf16[32,1536]{1,0:T(8,128)(2,1)S(1)} %get-tuple-element.54), channel_id=1, source_target_pairs={{0,64},{32,96},{64,128},{96,160},{128,192},{160,224},{192,0},{224,... | collective-permute-start | bytes 294920 | tf_op jit(solution)/shard_map/ppermute | solution.py:34
  97.0 5.6 %all-to-all-start.1 = ((f32[32,1,128]{2,1,0:T(1,128)}), f32[32,1,128]{2,1,0:T(1,128)}, u32[]{:S(2)}, u32[]{:S(2)}) async-start(f32[32,1,128]{2,1,0:T(1,128)} %get-tuple-element.45), calls=%async_computation.1 | async-start | bytes 32768 | tf_op jit(solution)/shard_map/all_to_all | solution.py:274
  104.4 5.2 %all-to-all-done.1 = f32[32,1,128]{2,1,0:T(1,128)} async-done(((f32[32,1,128]{2,1,0:T(1,128)}), f32[32,1,128]{2,1,0:T(1,128)}, u32[]{:S(2)}, u32[]{:S(2)}) %all-to-all-start.1) | async-done | bytes 16416 | tf_op jit(solution)/shard_map/all_to_all | solution.py:274
  111.0 6.0 %all-to-all-start.2 = ((f32[8,1,128]{2,1,0:T(1,128)}), f32[8,1,128]{2,1,0:T(1,128)S(1)}, u32[]{:S(2)}, u32[]{:S(2)}) async-start(f32[8,1,128]{2,1,0:T(1,128)} %broadcast_in_dim.2), calls=%async_computation.2 | async-start | bytes 8192 | tf_op jit(solution)/shard_map/all_to_all | solution.py:274
  118.7 4.8 %all-to-all-done.2.p = f32[8,1,128]{2,1,0:T(1,128)S(1)} async-done(((f32[8,1,128]{2,1,0:T(1,128)}), f32[8,1,128]{2,1,0:T(1,128)S(1)}, u32[]{:S(2)}, u32[]{:S(2)}) %all-to-all-start.2) | async-done | bytes 4128 | tf_op jit(solution)/shard_map/all_to_all | solution.py:274
  (107 shorter events, 35.1 us)
Async XLA Ops:
  4.5 6.9 %collective-permute-start.1 = (bf16[32,1536]{1,0:T(8,128)(2,1)}, bf16[32,1536]{1,0:T(8,128)(2,1)S(1)}, u32[]{:S(2)}, u32[]{:S(2)}) collective-permute-start(bf16[32,1536]{1,0:T(8,128)(2,1)} %param.4), channel_id=1, source_target_pairs={{0,64},{32,96},{64,128},{96,160},{128,192},{160,224},{192,0},{224,... | collective-permute-start | bytes 294920 | tf_op jit(solution)/shard_map/ppermute | solution.py:34
  13.3 14.3 %collective-permute-start.8 = (bf16[4,32,1536]{2,1,0:T(8,128)(2,1)S(1)}, bf16[4,32,1536]{2,1,0:T(8,128)(2,1)S(1)}, u32[]{:S(2)}, u32[]{:S(2)}) collective-permute-start(bf16[4,32,1536]{2,1,0:T(8,128)(2,1)S(1)} %pad_maximum_fusion.1.refs_0_), channel_id=1, source_target_pairs={{0,1},{1,2},{2,3},{3,4},{4,5},{5,6},{6,7},{7,0},{8,9},{9,10},{10,1... | collective-permute-start | bytes 1179656 | tf_op jit(solution)/shard_map/ppermute | solution.py:49
  14.2 13.3 %collective-permute-start.11 = (bf16[4,32,1536]{2,1,0:T(8,128)(2,1)S(1)}, bf16[4,32,1536]{2,1,0:T(8,128)(2,1)S(1)}, u32[]{:S(2)}, u32[]{:S(2)}) collective-permute-start(bf16[4,32,1536]{2,1,0:T(8,128)(2,1)S(1)} %pad_maximum_fusion.1.refs_0_), channel_id=1, source_target_pairs={{0,7},{1,0},{2,1},{3,2},{4,3},{5,4},{6,5},{7,6},{8,15},{9,8},{10,9... | collective-permute-start | bytes 1179656 | tf_op jit(solution)/shard_map/ppermute | solution.py:49
  27.3 7.3 %collective-permute-start.4 = (bf16[64,1536]{1,0:T(8,128)(2,1)S(1)}, bf16[64,1536]{1,0:T(8,128)(2,1)S(1)}, u32[]{:S(2)}, u32[]{:S(2)}) collective-permute-start(bf16[64,1536]{1,0:T(8,128)(2,1)S(1)} %get-tuple-element.59), channel_id=1, source_target_pairs={{0,8},{8,16},{16,24},{24,0},{1,9},{9,17},{17,25},{25,1},{2,10},{10... | collective-permute-start | bytes 589832 | tf_op jit(solution)/shard_map/ppermute | solution.py:44
  27.5 11.3 %collective-permute-start.9 = (bf16[4,32,1536]{2,1,0:T(8,128)(2,1)S(1)}, bf16[4,32,1536]{2,1,0:T(8,128)(2,1)}, u32[]{:S(2)}, u32[]{:S(2)}) collective-permute-start(bf16[4,32,1536]{2,1,0:T(8,128)(2,1)S(1)} %collective-permute-done.8.refs_1_), channel_id=1, source_target_pairs={{0,1},{1,2},{2,3},{3,4},{4,5},{5,6},{6,7},{7,0},{8,9},{9,10},{10,1... | collective-permute-start | bytes 1179656 | tf_op jit(solution)/shard_map/ppermute | solution.py:49
  27.6 11.3 %collective-permute-start.12 = (bf16[4,32,1536]{2,1,0:T(8,128)(2,1)S(1)}, bf16[4,32,1536]{2,1,0:T(8,128)(2,1)}, u32[]{:S(2)}, u32[]{:S(2)}) collective-permute-start(bf16[4,32,1536]{2,1,0:T(8,128)(2,1)S(1)} %collective-permute-done.11.refs_8_), channel_id=1, source_target_pairs={{0,7},{1,0},{2,1},{3,2},{4,3},{5,4},{6,5},{7,6},{8,15},{9,8},{10,9... | collective-permute-start | bytes 1179656 | tf_op jit(solution)/shard_map/ppermute | solution.py:49
  31.1 10.6 %collective-permute-start.7 = (bf16[64,3072]{1,0:T(8,128)(2,1)S(1)}, bf16[64,3072]{1,0:T(8,128)(2,1)S(1)}, u32[]{:S(2)}, u32[]{:S(2)}) collective-permute-start(bf16[64,3072]{1,0:T(8,128)(2,1)S(1)} %pad_maximum_fusion.3), channel_id=1, source_target_pairs={{0,24},{8,0},{16,8},{24,16},{1,25},{9,1},{17,9},{25,17},{2,26},{10... | collective-permute-start | bytes 1179656 | tf_op jit(solution)/shard_map/ppermute | solution.py:44
  34.7 10.3 %collective-permute-start.5 = (bf16[64,3072]{1,0:T(8,128)(2,1)S(1)}, bf16[64,3072]{1,0:T(8,128)(2,1)S(1)}, u32[]{:S(2)}, u32[]{:S(2)}) collective-permute-start(bf16[64,3072]{1,0:T(8,128)(2,1)S(1)} %pad_maximum_fusion.2), channel_id=1, source_target_pairs={{0,8},{8,16},{16,24},{24,0},{1,9},{9,17},{17,25},{25,1},{2,10},{10... | collective-permute-start | bytes 1179656 | tf_op jit(solution)/shard_map/ppermute | solution.py:44
  38.8 12.7 %collective-permute-start.10 = (bf16[4,32,1536]{2,1,0:T(8,128)(2,1)}, bf16[4,32,1536]{2,1,0:T(8,128)(2,1)S(1)}, u32[]{:S(2)}, u32[]{:S(2)}) collective-permute-start(bf16[4,32,1536]{2,1,0:T(8,128)(2,1)} %collective-permute-done.9.refs_2_), channel_id=1, source_target_pairs={{0,1},{1,2},{2,3},{3,4},{4,5},{5,6},{6,7},{7,0},{8,9},{9,10},{10,1... | collective-permute-start | bytes 1179656 | tf_op jit(solution)/shard_map/ppermute | solution.py:49
  38.8 12.7 %collective-permute-start.13 = (bf16[4,32,1536]{2,1,0:T(8,128)(2,1)}, bf16[4,32,1536]{2,1,0:T(8,128)(2,1)S(1)}, u32[]{:S(2)}, u32[]{:S(2)}) collective-permute-start(bf16[4,32,1536]{2,1,0:T(8,128)(2,1)} %collective-permute-done.12.refs_7_), channel_id=1, source_target_pairs={{0,7},{1,0},{2,1},{3,2},{4,3},{5,4},{6,5},{7,6},{8,15},{9,8},{10,9... | collective-permute-start | bytes 1179656 | tf_op jit(solution)/shard_map/ppermute | solution.py:49
  46.6 17.4 %all-to-all-start = ((bf16[8,64,384]{2,1,0:T(8,128)(2,1)}), bf16[8,64,384]{2,1,0:T(8,128)(2,1)S(1)}, u32[]{:S(2)}, u32[]{:S(2)}) async-start(bf16[8,64,384]{2,1,0:T(8,128)(2,1)} %bitcast.43), calls=%async_computation | async-start | bytes 786432 | tf_op jit(solution)/shard_map/all_to_all | solution.py:274
  51.6 8.9 %collective-permute-start.14 = (bf16[64,3072]{1,0:T(8,128)(2,1)S(1)}, bf16[64,3072]{1,0:T(8,128)(2,1)S(1)}, u32[]{:S(2)}, u32[]{:S(2)}) collective-permute-start(bf16[64,3072]{1,0:T(8,128)(2,1)S(1)} %get-tuple-element.28), channel_id=1, source_target_pairs={{0,8},{8,16},{16,24},{24,0},{1,9},{9,17},{17,25},{25,1},{2,10},{10... | collective-permute-start | bytes 1179656 | tf_op jit(solution)/shard_map/ppermute | solution.py:44
  51.7 9.0 %collective-permute-start.15 = (bf16[64,3072]{1,0:T(8,128)(2,1)S(1)}, bf16[64,3072]{1,0:T(8,128)(2,1)S(1)}, u32[]{:S(2)}, u32[]{:S(2)}) collective-permute-start(bf16[64,3072]{1,0:T(8,128)(2,1)S(1)} %get-tuple-element.28), channel_id=1, source_target_pairs={{0,24},{8,0},{16,8},{24,16},{1,25},{9,1},{17,9},{25,17},{2,26},{10... | collective-permute-start | bytes 1179656 | tf_op jit(solution)/shard_map/ppermute | solution.py:44
  55.0 11.5 %collective-permute-start.23 = (bf16[2,32,1536]{2,1,0:T(8,128)(2,1)}, bf16[2,32,1536]{2,1,0:T(8,128)(2,1)S(1)}, u32[]{:S(2)}, u32[]{:S(2)}) collective-permute-start(bf16[2,32,1536]{2,1,0:T(8,128)(2,1)} %slice.129), channel_id=1, source_target_pairs={{0,1},{1,2},{2,3},{3,4},{4,5},{5,6},{6,7},{7,0},{8,9},{9,10},{10,1... | collective-permute-start | bytes 589832 | tf_op jit(solution)/shard_map/ppermute | solution.py:49
  57.2 9.5 %collective-permute-start.24 = (bf16[2,32,1536]{2,1,0:T(8,128)(2,1)}, bf16[2,32,1536]{2,1,0:T(8,128)(2,1)S(1)}, u32[]{:S(2)}, u32[]{:S(2)}) collective-permute-start(bf16[2,32,1536]{2,1,0:T(8,128)(2,1)} %slice.130), channel_id=1, source_target_pairs={{0,7},{1,0},{2,1},{3,2},{4,3},{5,4},{6,5},{7,6},{8,15},{9,8},{10,9... | collective-permute-start | bytes 589832 | tf_op jit(solution)/shard_map/ppermute | solution.py:49
  60.5 15.4 %collective-permute-start.18 = (bf16[32,3072]{1,0:T(8,128)(2,1)S(1)}, bf16[32,3072]{1,0:T(8,128)(2,1)S(1)}, u32[]{:S(2)}, u32[]{:S(2)}) collective-permute-start(bf16[32,3072]{1,0:T(8,128)(2,1)S(1)} %slice.125), channel_id=1, source_target_pairs={{0,8},{8,16},{16,24},{24,0},{1,9},{9,17},{17,25},{25,1},{2,10},{10... | collective-permute-start | bytes 589832 | tf_op jit(solution)/shard_map/ppermute | solution.py:44
  61.4 14.5 %collective-permute-start.19 = (bf16[32,3072]{1,0:T(8,128)(2,1)}, bf16[32,3072]{1,0:T(8,128)(2,1)}, u32[]{:S(2)}, u32[]{:S(2)}) collective-permute-start(bf16[32,3072]{1,0:T(8,128)(2,1)} %slice.126), channel_id=1, source_target_pairs={{0,24},{8,0},{16,8},{24,16},{1,25},{9,1},{17,9},{25,17},{2,26},{10... | collective-permute-start | bytes 589832 | tf_op jit(solution)/shard_map/ppermute | solution.py:44
  64.0 18.3 %collective-permute-start.16 = (bf16[8,64,384]{2,1,0:T(8,128)(2,1)S(1)}, bf16[8,64,384]{2,1,0:T(8,128)(2,1)S(1)}, u32[]{:S(2)}, u32[]{:S(2)}) collective-permute-start(bf16[8,64,384]{2,1,0:T(8,128)(2,1)S(1)} %all-to-all-done.refs_7_), channel_id=1, source_target_pairs={{0,8},{8,16},{16,24},{24,0},{1,9},{9,17},{17,25},{25,1},{2,10},{10... | collective-permute-start | bytes 1179656 | tf_op jit(solution)/shard_map/ppermute | solution.py:44
  66.5 15.7 %collective-permute-start.17 = (bf16[8,64,384]{2,1,0:T(8,128)(2,1)S(1)}, bf16[8,64,384]{2,1,0:T(8,128)(2,1)S(1)}, u32[]{:S(2)}, u32[]{:S(2)}) collective-permute-start(bf16[8,64,384]{2,1,0:T(8,128)(2,1)S(1)} %all-to-all-done.refs_7_), channel_id=1, source_target_pairs={{0,24},{8,0},{16,8},{24,16},{1,25},{9,1},{17,9},{25,17},{2,26},{10... | collective-permute-start | bytes 1179656 | tf_op jit(solution)/shard_map/ppermute | solution.py:44
  70.6 19.4 %collective-permute-start.25 = (bf16[8,4,32,1536]{3,2,1,0:T(8,128)(2,1)}, bf16[8,4,32,1536]{3,2,1,0:T(8,128)(2,1)S(1)}, u32[]{:S(2)}, u32[]{:S(2)}) collective-permute-start(bf16[8,4,32,1536]{3,2,1,0:T(8,128)(2,1)} %stack_up.1.refs_1_.refs_3_.refs_5_.refs_2_), channel_id=1, source_target_pairs={{0,32},{32,0},{64,96},{96,64},{128,160},{160,128},{192,224},{224,1... | collective-permute-start | bytes 9437192 | tf_op jit(solution)/shard_map/ppermute | solution.py:39
  83.2 9.5 %collective-permute-start.21 = (bf16[4,64,384]{2,1,0:T(8,128)(2,1)S(1)}, bf16[4,64,384]{2,1,0:T(8,128)(2,1)S(1)}, u32[]{:S(2)}, u32[]{:S(2)}) collective-permute-start(bf16[4,64,384]{2,1,0:T(8,128)(2,1)S(1)} %slice.107), channel_id=1, source_target_pairs={{0,8},{8,16},{16,24},{24,0},{1,9},{9,17},{17,25},{25,1},{2,10},{10... | collective-permute-start | bytes 589832 | tf_op jit(solution)/shard_map/ppermute | solution.py:44
  83.3 9.4 %collective-permute-start.22 = (bf16[4,64,384]{2,1,0:T(8,128)(2,1)S(1)}, bf16[4,64,384]{2,1,0:T(8,128)(2,1)S(1)}, u32[]{:S(2)}, u32[]{:S(2)}) collective-permute-start(bf16[4,64,384]{2,1,0:T(8,128)(2,1)S(1)} %slice.108), channel_id=1, source_target_pairs={{0,24},{8,0},{16,8},{24,16},{1,25},{9,1},{17,9},{25,17},{2,26},{10... | collective-permute-start | bytes 589832 | tf_op jit(solution)/shard_map/ppermute | solution.py:44
  97.0 12.7 %all-to-all-start.1 = ((f32[32,1,128]{2,1,0:T(1,128)}), f32[32,1,128]{2,1,0:T(1,128)}, u32[]{:S(2)}, u32[]{:S(2)}) async-start(f32[32,1,128]{2,1,0:T(1,128)} %get-tuple-element.45), calls=%async_computation.1 | async-start | bytes 32768 | tf_op jit(solution)/shard_map/all_to_all | solution.py:274
  111.0 12.4 %all-to-all-start.2 = ((f32[8,1,128]{2,1,0:T(1,128)}), f32[8,1,128]{2,1,0:T(1,128)S(1)}, u32[]{:S(2)}, u32[]{:S(2)}) async-start(f32[8,1,128]{2,1,0:T(1,128)} %broadcast_in_dim.2), calls=%async_computation.2 | async-start | bytes 8192 | tf_op jit(solution)/shard_map/all_to_all | solution.py:274
  (22 other events, 142.2 us)
